TPU v7x, 128 devices: a whole 4x4x4 slice. The times are simulated.
128 devices in a mesh: dp: 8 (over y, z_lo), ctx: 16 (over z_hi, x, core).
Axes of the slice: x: 4, y: 4, z: 4 (z_hi: 2, z_lo: 2; z = z_hi * 2 + z_lo), core: 2. Of those that a mesh axis runs over, the one named last changes fastest.
Arguments:
- tokens: bfloat16 [24576, 1536], P(('dp', 'ctx')), may hold values from -6 to 6
- segments: int32 [24576], P('dp'), may hold values from 0 to 4, as said below
- routes: int32 [24576, 2], P(('dp', 'ctx')), may hold values from 0 to 15, all different within a row; in each aligned block of 192 rows (0 to 191, 192 to 383, ...) at most 36 rows name the same one
- gain_attn: bfloat16 [1536], P(('dp', 'ctx')), may hold values from 0.25 to 1.75
- w_query: bfloat16 [1536, 1536], P(('dp', 'ctx')), may hold values from -0.21875 to 0.21875
- key_weight: bfloat16 [1536, 512], P(('dp', 'ctx')), may hold values from -0.15625 to 0.15625
- value_weight: bfloat16 [1536, 512], P(('dp', 'ctx')), may hold values from -0.15625 to 0.15625
- w_out: bfloat16 [1536, 1536], P(('dp', 'ctx')), may hold values from -1.75 to 1.75
- w_router: bfloat16 [1536, 16], P(('dp', 'ctx')), may hold values from -0.109375 to 0.109375
- gain_ffn: bfloat16 [1536], P(('dp', 'ctx')), may hold values from 0.25 to 1.75
- w_gate: bfloat16 [16, 1536, 1024], P('ctx', 'dp'), may hold values from -0.15625 to 0.15625
- w_up: bfloat16 [16, 1536, 1024], P('ctx', 'dp'), may hold values from -0.15625 to 0.15625
- w_down: bfloat16 [16, 1024, 1536], P('ctx', 'dp'), may hold values from -0.375 to 0.375
- cotangent: bfloat16 [24576, 1536], P(('dp', 'ctx')), may hold values from -24 to 24
Outputs:
- mixed: bfloat16 [24576, 1536], P(('dp', 'ctx'))
- grad_input: bfloat16 [24576, 1536], P(('dp', 'ctx'))
- grad_gain_attn: float32 [1536], P(('dp', 'ctx'))
- grad_query: float32 [1536, 1536], P(('dp', 'ctx'))
- grad_key: float32 [1536, 512], P(('dp', 'ctx'))
- grad_value: float32 [1536, 512], P(('dp', 'ctx'))
- grad_out_proj: float32 [1536, 1536], P(('dp', 'ctx'))
- grad_router: float32 [1536, 16], P(('dp', 'ctx'))
- grad_gain_ffn: float32 [1536], P(('dp', 'ctx'))
- grad_gate: float32 [16, 1536, 1024], P('ctx', 'dp')
- grad_up: float32 [16, 1536, 1024], P('ctx', 'dp')
- grad_down: float32 [16, 1024, 1536], P('ctx', 'dp')
Inputs may be any that keep to these rules, and one draw needn't show every extreme that they name: `segments`: within each sequence of 3072 tokens (one per index of dp) the ids never fall and each id marks one document; every sequence packs five documents, the first two and last two of them of at least 204 tokens each, and the middle one of 1728 to 1920 tokens. `routes`: each row names 2 different experts; among the rows of one device no expert is named by more than 36 rows, a bound that some block reaches.
All inputs are finite; a program needn't handle non-finite values.
Results may differ from a plain program's by a relative error of at most 0.018.
Values may be sent and summed in bfloat16 or wider, within the bound.
A program may use at most 192 MiB of HBM per device.

v0:
```python
import math

import jax
import jax.numpy as jnp
from jax import lax
from jax.sharding import PartitionSpec as P

QUERY_HEAD_COUNT = 24
KEY_VALUE_HEADS = 8
HEAD_SIZE = 64
TOP = 2


EPSILON = 1e-06
NEGATIVE = -1e30


def inverse_rms(values):
    return lax.rsqrt(jnp.mean(values * values, axis=-1, keepdims=True) + EPSILON)


def norm_backward(grad_normed, values, inverse, gain):
    unit_rows = values * inverse
    grad_unit = grad_normed * gain
    grad_values = inverse * (
        grad_unit - unit_rows * jnp.mean(grad_unit * unit_rows, axis=-1, keepdims=True)
    )
    return (grad_values, jnp.sum(grad_normed * unit_rows, axis=0))


def contract_rows(left, right):
    return lax.dot_general(
        left, right, (((0,), (0,)), ((), ())), preferred_element_type=jnp.float32
    )


def contract_cols(left, right):
    return lax.dot_general(
        left, right, (((1,), (1,)), ((), ())), preferred_element_type=jnp.float32
    )


def allowed_pairs(query_pos, query_seg, block_pos, block_seg):
    return (block_pos[None, :] <= query_pos[:, None]) & (block_seg[None, :] == query_seg[:, None])


def block_scores(heads_of_queries, key_block, allowed, factor):
    scores = (
        jnp.einsum(
            "qhgd,khd->hgqk", heads_of_queries, key_block, preferred_element_type=jnp.float32
        )
        * factor
    )
    return jnp.where(allowed, scores, NEGATIVE)


def attend_forward(
    heads_of_queries, key_blocks, value_blocks, key_pos, key_seg, query_pos, query_seg, factor
):
    stat_shape = (
        heads_of_queries.shape[1],
        heads_of_queries.shape[2],
        heads_of_queries.shape[0],
        1,
    )

    def running_step(running, element):
        highest, total = running
        key_block, block_pos, block_seg = element
        scores = block_scores(
            heads_of_queries,
            key_block,
            allowed_pairs(query_pos, query_seg, block_pos, block_seg),
            factor,
        )
        new_high = jnp.maximum(highest, jnp.max(scores, axis=-1, keepdims=True))
        total = total * jnp.exp(highest - new_high) + jnp.sum(
            jnp.exp(scores - new_high), axis=-1, keepdims=True
        )
        return ((new_high, total), None)

    start_state = (jnp.full(stat_shape, NEGATIVE, jnp.float32), jnp.zeros(stat_shape, jnp.float32))
    (highest, total), _ = lax.scan(running_step, start_state, (key_blocks, key_pos, key_seg))
    log_total = highest + jnp.log(total)

    def output_step(summed, element):
        key_block, value_block, block_pos, block_seg = element
        scores = block_scores(
            heads_of_queries,
            key_block,
            allowed_pairs(query_pos, query_seg, block_pos, block_seg),
            factor,
        )
        weights = jnp.exp(scores - log_total).astype(jnp.bfloat16)
        return (
            summed
            + jnp.einsum(
                "hgqk,khd->qhgd", weights, value_block, preferred_element_type=jnp.float32
            ),
            None,
        )

    summed, _ = lax.scan(
        output_step,
        jnp.zeros(heads_of_queries.shape, jnp.float32),
        (key_blocks, value_blocks, key_pos, key_seg),
    )
    return (summed, log_total)


def attend_backward(
    heads_of_queries,
    head_gradient,
    key_blocks,
    value_blocks,
    key_pos,
    key_seg,
    query_pos,
    query_seg,
    log_total,
    factor,
):

    def probs_and_grads(key_block, value_block, block_pos, block_seg):
        scores = block_scores(
            heads_of_queries,
            key_block,
            allowed_pairs(query_pos, query_seg, block_pos, block_seg),
            factor,
        )
        probs = jnp.exp(scores - log_total)
        grad_probs = jnp.einsum(
            "qhgd,khd->hgqk", head_gradient, value_block, preferred_element_type=jnp.float32
        )
        return (probs, grad_probs)

    def delta_step(delta, element):
        probs, grad_probs = probs_and_grads(element[0], element[1], element[2], element[3])
        return (delta + jnp.sum(probs * grad_probs, axis=-1, keepdims=True), None)

    delta, _ = lax.scan(
        delta_step,
        jnp.zeros(log_total.shape, jnp.float32),
        (key_blocks, value_blocks, key_pos, key_seg),
    )

    def grad_step(grad_query_heads, element):
        key_block, value_block, block_pos, block_seg = element
        probs, grad_probs = probs_and_grads(key_block, value_block, block_pos, block_seg)
        grad_scores = (probs * (grad_probs - delta)).astype(jnp.bfloat16)
        grad_query_heads = grad_query_heads + jnp.einsum(
            "hgqk,khd->qhgd", grad_scores, key_block, preferred_element_type=jnp.float32
        )
        grad_key_block = (
            jnp.einsum(
                "hgqk,qhgd->khd", grad_scores, heads_of_queries, preferred_element_type=jnp.float32
            )
            * factor
        )
        grad_value_block = jnp.einsum(
            "hgqk,qhgd->khd",
            probs.astype(jnp.bfloat16),
            head_gradient,
            preferred_element_type=jnp.float32,
        )
        return (grad_query_heads, (grad_key_block, grad_value_block))

    grad_query_heads, (key_block_gradient, value_block_gradient) = lax.scan(
        grad_step,
        jnp.zeros(heads_of_queries.shape, jnp.float32),
        (key_blocks, value_blocks, key_pos, key_seg),
    )
    return (grad_query_heads * factor, key_block_gradient, value_block_gradient)


def shards(
    tokens,
    segments,
    routes,
    gain_attn,
    w_query,
    key_weight,
    value_weight,
    w_out,
    w_router,
    gain_ffn,
    w_gate,
    w_up,
    w_down,
    cotangent,
):
    device_local_rows, width = tokens.shape
    sequence_length = segments.shape[0]
    query_group_size = QUERY_HEAD_COUNT // KEY_VALUE_HEADS
    factor = HEAD_SIZE ** (-0.5)
    ctx_index = lax.axis_index("ctx")
    ctx_count = lax.axis_size("ctx")
    rows_per_block = math.gcd(sequence_length, 512)
    count_of_blocks = sequence_length // rows_per_block
    key_pos = jnp.arange(sequence_length, dtype=jnp.int32).reshape(count_of_blocks, rows_per_block)
    key_seg = segments.reshape(count_of_blocks, rows_per_block)
    query_pos = ctx_index * device_local_rows + jnp.arange(device_local_rows, dtype=jnp.int32)
    query_seg = lax.dynamic_slice_in_dim(segments, ctx_index * device_local_rows, device_local_rows)
    key_value_shape = (count_of_blocks, rows_per_block, KEY_VALUE_HEADS, HEAD_SIZE)
    gathered = (
        lax.all_gather(gain_attn, ("dp", "ctx"), axis=0, tiled=True),
        lax.all_gather(w_query, ("dp", "ctx"), axis=0, tiled=True),
        lax.all_gather(key_weight, ("dp", "ctx"), axis=0, tiled=True),
        lax.all_gather(value_weight, ("dp", "ctx"), axis=0, tiled=True),
        lax.all_gather(w_out, ("dp", "ctx"), axis=0, tiled=True),
        lax.all_gather(w_router, ("dp", "ctx"), axis=0, tiled=True),
        lax.all_gather(gain_ffn, ("dp", "ctx"), axis=0, tiled=True),
    )
    gain_one, query_proj, key_proj, value_proj, out_proj, router_proj, gain_two = gathered
    expert_weights = (
        lax.all_gather(w_gate, "dp", axis=1, tiled=True),
        lax.all_gather(w_up, "dp", axis=1, tiled=True),
        lax.all_gather(w_down, "dp", axis=1, tiled=True),
    )
    gate_proj, up_proj, down_proj = expert_weights
    residual = tokens.astype(jnp.float32)
    inverse_one = inverse_rms(residual)
    scale_one = gain_one.astype(jnp.float32)
    normed = (residual * inverse_one * scale_one).astype(jnp.bfloat16)
    rows_of_queries = jnp.dot(normed, query_proj, preferred_element_type=jnp.float32).astype(
        jnp.bfloat16
    )
    rows_of_keys = jnp.dot(normed, key_proj, preferred_element_type=jnp.float32).astype(
        jnp.bfloat16
    )
    rows_of_values = jnp.dot(normed, value_proj, preferred_element_type=jnp.float32).astype(
        jnp.bfloat16
    )
    all_keys, all_values = (
        lax.all_gather(rows_of_keys, "ctx", axis=0, tiled=True),
        lax.all_gather(rows_of_values, "ctx", axis=0, tiled=True),
    )
    heads_of_queries = rows_of_queries.reshape(
        device_local_rows, KEY_VALUE_HEADS, query_group_size, HEAD_SIZE
    )
    summed, log_total = attend_forward(
        heads_of_queries,
        all_keys.reshape(key_value_shape),
        all_values.reshape(key_value_shape),
        key_pos,
        key_seg,
        query_pos,
        query_seg,
        factor,
    )
    attended = summed.reshape(device_local_rows, QUERY_HEAD_COUNT * HEAD_SIZE).astype(jnp.bfloat16)
    hidden_one = residual + contract_cols(attended, out_proj)
    inverse_two = inverse_rms(hidden_one)
    scale_two = gain_two.astype(jnp.float32)
    normed_two = (hidden_one * inverse_two * scale_two).astype(jnp.bfloat16)
    logits = jnp.dot(normed_two, router_proj, preferred_element_type=jnp.float32)
    experts = router_proj.shape[1]
    per_device = experts // ctx_count
    capacity = max(2, 3 * device_local_rows // experts)
    picked = (routes[:, :, None] == jnp.arange(experts, dtype=jnp.int32)[None, None, :]).astype(
        jnp.float32
    )
    chosen = jnp.sum(picked * logits[:, None, :], axis=-1)
    gate_weights = jax.nn.softmax(chosen, axis=-1)
    flat_pick = picked.reshape(-1, experts)
    slot_ids = jnp.sum(flat_pick * (jnp.cumsum(flat_pick, axis=0) - 1.0), axis=-1).astype(jnp.int32)
    targets = routes.reshape(-1) * capacity + slot_ids
    placement = (
        targets[:, None] == jnp.arange(experts * capacity, dtype=jnp.int32)[None, :]
    ).astype(jnp.bfloat16)
    placement = placement.reshape(device_local_rows, TOP, experts * capacity)
    spread = jnp.sum(placement, axis=1)
    outgoing = (
        contract_rows(spread, normed_two)
        .astype(jnp.bfloat16)
        .reshape(ctx_count, per_device, capacity, width)
    )
    received = lax.all_to_all(outgoing, "ctx", split_axis=0, concat_axis=0, tiled=True)
    gate_pre = jnp.einsum("sxid,xdf->sxif", received, gate_proj, preferred_element_type=jnp.float32)
    up_pre = jnp.einsum("sxid,xdf->sxif", received, up_proj, preferred_element_type=jnp.float32)
    hidden = (jax.nn.silu(gate_pre) * up_pre).astype(jnp.bfloat16)
    produced = jnp.einsum(
        "sxif,xfd->sxid", hidden, down_proj, preferred_element_type=jnp.float32
    ).astype(jnp.bfloat16)
    produced, received, gate_pre, up_pre, hidden = (produced, received, gate_pre, up_pre, hidden)
    returned = lax.all_to_all(produced, "ctx", split_axis=0, concat_axis=0, tiled=True).reshape(
        experts * capacity, width
    )
    chosen_rows = jnp.einsum("tcr,rd->tcd", placement, returned, preferred_element_type=jnp.float32)
    mixed = (hidden_one + jnp.sum(gate_weights[:, :, None] * chosen_rows, axis=1)).astype(
        jnp.bfloat16
    )
    gain_back, query_back, key_back, value_back, out_back, router_back, gain_ffn_back = (
        lax.all_gather(gain_attn, ("dp", "ctx"), axis=0, tiled=True),
        lax.all_gather(w_query, ("dp", "ctx"), axis=0, tiled=True),
        lax.all_gather(key_weight, ("dp", "ctx"), axis=0, tiled=True),
        lax.all_gather(value_weight, ("dp", "ctx"), axis=0, tiled=True),
        lax.all_gather(w_out, ("dp", "ctx"), axis=0, tiled=True),
        lax.all_gather(w_router, ("dp", "ctx"), axis=0, tiled=True),
        lax.all_gather(gain_ffn, ("dp", "ctx"), axis=0, tiled=True),
    )
    gate_back, up_back, down_back = (
        lax.all_gather(w_gate, "dp", axis=1, tiled=True),
        lax.all_gather(w_up, "dp", axis=1, tiled=True),
        lax.all_gather(w_down, "dp", axis=1, tiled=True),
    )
    keys_back, values_back = (
        lax.all_gather(rows_of_keys, "ctx", axis=0, tiled=True),
        lax.all_gather(rows_of_values, "ctx", axis=0, tiled=True),
    )
    scale_one = gain_back.astype(jnp.float32)
    scale_two = gain_ffn_back.astype(jnp.float32)
    grad_y = cotangent.astype(jnp.float32)
    grad_gates = jnp.sum(chosen_rows * grad_y[:, None, :], axis=-1)
    grad_routed = (gate_weights[:, :, None] * grad_y[:, None, :]).astype(jnp.bfloat16)
    grad_outgoing = jnp.einsum(
        "tcr,tcd->rd", placement, grad_routed, preferred_element_type=jnp.float32
    )
    grad_outgoing = grad_outgoing.astype(jnp.bfloat16).reshape(
        ctx_count, per_device, capacity, width
    )
    grad_received = lax.all_to_all(grad_outgoing, "ctx", split_axis=0, concat_axis=0, tiled=True)
    grad_hidden = jnp.einsum(
        "sxid,xfd->sxif", grad_received, down_back, preferred_element_type=jnp.float32
    )
    sigmoid = jax.nn.sigmoid(gate_pre)
    grad_gate_pre = (grad_hidden * up_pre * sigmoid * (1.0 + gate_pre * (1.0 - sigmoid))).astype(
        jnp.bfloat16
    )
    grad_up_pre = (grad_hidden * gate_pre * sigmoid).astype(jnp.bfloat16)
    grad_expert_in = jnp.einsum(
        "sxif,xdf->sxid", grad_gate_pre, gate_back, preferred_element_type=jnp.float32
    )
    grad_expert_in = grad_expert_in + jnp.einsum(
        "sxif,xdf->sxid", grad_up_pre, up_back, preferred_element_type=jnp.float32
    )
    grad_expert_in = grad_expert_in.astype(jnp.bfloat16)
    grad_gate_full = jnp.einsum(
        "sxid,sxif->xdf", received, grad_gate_pre, preferred_element_type=jnp.float32
    )
    grad_up_full = jnp.einsum(
        "sxid,sxif->xdf", received, grad_up_pre, preferred_element_type=jnp.float32
    )
    grad_down_full = jnp.einsum(
        "sxif,sxid->xfd", hidden, grad_received, preferred_element_type=jnp.float32
    )
    grad_gate, grad_up, grad_down = (
        lax.psum_scatter(
            grad_gate_full.astype(jnp.bfloat16), "dp", scatter_dimension=1, tiled=True
        ).astype(jnp.float32),
        lax.psum_scatter(
            grad_up_full.astype(jnp.bfloat16), "dp", scatter_dimension=1, tiled=True
        ).astype(jnp.float32),
        lax.psum_scatter(
            grad_down_full.astype(jnp.bfloat16), "dp", scatter_dimension=1, tiled=True
        ).astype(jnp.float32),
    )
    grad_back = lax.all_to_all(
        grad_expert_in, "ctx", split_axis=0, concat_axis=0, tiled=True
    ).reshape(experts * capacity, width)
    grad_normed_two = jnp.einsum(
        "tcr,rd->td", placement, grad_back, preferred_element_type=jnp.float32
    )
    grad_chosen = gate_weights * (
        grad_gates - jnp.sum(gate_weights * grad_gates, axis=-1, keepdims=True)
    )
    grad_logits = jnp.sum(picked * grad_chosen[:, :, None], axis=1).astype(jnp.bfloat16)
    grad_normed_two = grad_normed_two + contract_cols(grad_logits, router_back)
    grad_router_full = contract_rows(normed_two, grad_logits)
    grad_hidden_one, grad_gain_two = norm_backward(
        grad_normed_two, hidden_one, inverse_two, scale_two
    )
    grad_hidden_one = grad_hidden_one + grad_y
    grad_branch = grad_hidden_one.astype(jnp.bfloat16)
    grad_out_full = contract_rows(grad_branch, attended)
    attended_gradient = jnp.dot(grad_branch, out_back, preferred_element_type=jnp.float32).astype(
        jnp.bfloat16
    )
    head_gradient = attended_gradient.reshape(
        device_local_rows, KEY_VALUE_HEADS, query_group_size, HEAD_SIZE
    )
    grad_query_heads, key_block_gradient, value_block_gradient = attend_backward(
        heads_of_queries,
        head_gradient,
        keys_back.reshape(key_value_shape),
        values_back.reshape(key_value_shape),
        key_pos,
        key_seg,
        query_pos,
        query_seg,
        log_total,
        factor,
    )
    grad_keys, grad_values = (
        lax.psum_scatter(
            key_block_gradient.reshape(sequence_length, KEY_VALUE_HEADS * HEAD_SIZE).astype(
                jnp.bfloat16
            ),
            "ctx",
            scatter_dimension=0,
            tiled=True,
        ).astype(jnp.float32),
        lax.psum_scatter(
            value_block_gradient.reshape(sequence_length, KEY_VALUE_HEADS * HEAD_SIZE).astype(
                jnp.bfloat16
            ),
            "ctx",
            scatter_dimension=0,
            tiled=True,
        ).astype(jnp.float32),
    )
    grad_queries = grad_query_heads.reshape(device_local_rows, QUERY_HEAD_COUNT * HEAD_SIZE).astype(
        jnp.bfloat16
    )
    grad_keys = grad_keys.astype(jnp.bfloat16)
    grad_values = grad_values.astype(jnp.bfloat16)
    grad_normed = (
        contract_cols(grad_queries, query_back)
        + contract_cols(grad_keys, key_back)
        + contract_cols(grad_values, value_back)
    )
    grad_query_full = contract_rows(normed, grad_queries)
    grad_key_full = contract_rows(normed, grad_keys)
    grad_value_full = contract_rows(normed, grad_values)
    grad_residual, grad_gain_one = norm_backward(grad_normed, residual, inverse_one, scale_one)
    grad_input = (grad_residual + grad_hidden_one).astype(jnp.bfloat16)
    shares = (
        lax.psum_scatter(grad_gain_one, ("dp", "ctx"), scatter_dimension=0, tiled=True),
        lax.psum_scatter(grad_query_full, ("dp", "ctx"), scatter_dimension=0, tiled=True),
        lax.psum_scatter(grad_key_full, ("dp", "ctx"), scatter_dimension=0, tiled=True),
        lax.psum_scatter(grad_value_full, ("dp", "ctx"), scatter_dimension=0, tiled=True),
        lax.psum_scatter(grad_out_full, ("dp", "ctx"), scatter_dimension=0, tiled=True),
        lax.psum_scatter(grad_router_full, ("dp", "ctx"), scatter_dimension=0, tiled=True),
        lax.psum_scatter(grad_gain_two, ("dp", "ctx"), scatter_dimension=0, tiled=True),
    )
    return (
        mixed,
        grad_input,
        shares[0],
        shares[1],
        shares[2],
        shares[3],
        shares[4],
        shares[5],
        shares[6],
        grad_gate,
        grad_up,
        grad_down,
    )


def solution(mesh):
    in_specs = (
        P(("dp", "ctx"), None),
        P("dp"),
        P(("dp", "ctx"), None),
        P(("dp", "ctx")),
        P(("dp", "ctx"), None),
        P(("dp", "ctx"), None),
        P(("dp", "ctx"), None),
        P(("dp", "ctx"), None),
        P(("dp", "ctx"), None),
        P(("dp", "ctx")),
        P("ctx", "dp", None),
        P("ctx", "dp", None),
        P("ctx", "dp", None),
        P(("dp", "ctx"), None),
    )
    out_specs = (
        P(("dp", "ctx"), None),
        P(("dp", "ctx"), None),
        P(("dp", "ctx")),
        P(("dp", "ctx"), None),
        P(("dp", "ctx"), None),
        P(("dp", "ctx"), None),
        P(("dp", "ctx"), None),
        P(("dp", "ctx"), None),
        P(("dp", "ctx")),
        P("ctx", "dp", None),
        P("ctx", "dp", None),
        P("ctx", "dp", None),
    )
    return jax.shard_map(shards, mesh=mesh, in_specs=in_specs, out_specs=out_specs, check_vma=False)
```

profile of v0, /device:TPU:1, one launch (start us, length us, event | category | flops | bytes accessed | tf_op | source)
XLA Modules:
  0.0 2773.0 jit_solution(3130990620297697247)
XLA Ops:
  10.4 68.9 %all-reduce.15 = (bf16[1536]{0:T(1024)(128)(2,1)S(1)}, bf16[1536]{0:T(1024)(128)(2,1)S(1)}) all-reduce(bf16[1536]{0:T(1024)(128)(2,1)S(1)} %dynamic-update-slice, bf16[1536]{0:T(1024)(128)(2,1)S(1)} %dynamic-update-slice.1), channel_id=1, replica_groups=mesh['dp'=8,'ctx'=16] {'dp','ctx'}, use_global_device_ids=true, to_apply=%add | all-reduce | flops 3072 | bytes 12288
  80.6 126.4 %all-gather.25.cloned.1.call-done = bf16[128,12,512]{2,1,0:T(8,128)(2,1)} async-done(((bf16[1,12,512]{2,1,0:T(8,128)(2,1)}), bf16[128,12,512]{2,1,0:T(8,128)(2,1)}) %all-gather.25.cloned.1.call-update) | async-done | bytes 1572880 | tf_op jit(solution)/shard_map/all_gather | solution.py:209
  210.8 190.8 %all-gather.27.cloned.1.call-done = bf16[128,12,512]{2,1,0:T(8,128)(2,1)} async-done(((bf16[1,12,512]{2,1,0:T(8,128)(2,1)}), bf16[128,12,512]{2,1,0:T(8,128)(2,1)}) %all-gather.27.cloned.1.call-update) | async-done | bytes 1572880 | tf_op jit(solution)/shard_map/all_gather | solution.py:208
  414.1 42.0 %all-gather.15.cloned.1.call-done = bf16[3072,512]{1,0:T(8,128)(2,1)} async-done(((bf16[192,512]{1,0:T(8,128)(2,1)}), bf16[3072,512]{1,0:T(8,128)(2,1)}) %all-gather.15.cloned.1.call-update) | async-done | bytes 3145744 | tf_op jit(solution)/shard_map/all_gather | solution.py:236
  456.2 8.9 reshape.367
  465.0 7.7 copy.129
  472.7 37.3 %all-gather.17.cloned.1.call-done = bf16[3072,512]{1,0:T(8,128)(2,1)} async-done(((bf16[192,512]{1,0:T(8,128)(2,1)}), bf16[3072,512]{1,0:T(8,128)(2,1)}) %all-gather.17.cloned.1.call-update) | async-done | bytes 3145744 | tf_op jit(solution)/shard_map/all_gather | solution.py:235
  510.0 8.9 reshape.368
  518.9 7.6 copy.130
  526.5 184.2 %all-gather.29.cloned.1.call-done = bf16[128,12,1536]{2,1,0:T(8,128)(2,1)} async-done(((bf16[1,12,1536]{2,1,0:T(8,128)(2,1)}), bf16[128,12,1536]{2,1,0:T(8,128)(2,1)}) %all-gather.29.cloned.1.call-update) | async-done | bytes 4718608 | tf_op jit(solution)/shard_map/all_gather | solution.py:207
  710.7 8.2 reshape.339
  724.6 35.0 %while.50 = (s32[]{:T(128)}, f32[8,3,192,1]{2,1,0,3:T(4,128)S(1)}, f32[8,3,192,1]{2,1,0,3:T(4,128)S(1)}, s32[6,512]{1,0:T(8,128)S(1)}, s32[6,512]{1,0:T(8,128)S(...) while((s32[]{:T(128)}, f32[8,3,192,1]{2,1,0,3:T(4,128)S(1)}, ...), condition=%wide.region_4.5_spmd.clone, body=%wide.region_1.4_spmd.clone.sunk | while | flops 318823104 | bytes 20537740 | solution.py:83
  759.7 35.9 %while.51 = (s32[]{:T(128)}, f32[192,8,3,64]{0,3,2,1:T(8,128)S(1)}, bf16[6,512,8,64]{1,3,2,0:T(8,128)(2,1)}, s32[6,512]{1,0:T(8,128)S(1)}, s32[6,512]{1,0:T(8,12...) while((s32[]{:T(128)}, f32[192,8,3,64]{0,3,2,1:T(8,128)S(1)}, ...), condition=%wide.region_6.7_spmd.clone, body=%wide.region_5.6_spmd.clone.sunk | while | flops 614301888 | bytes 4229006 | solution.py:103
  798.3 113.7 %all-gather.31.cloned.1.call-done = bf16[128,12,1536]{2,1,0:T(8,128)(2,1)} async-done(((bf16[1,12,1536]{2,1,0:T(8,128)(2,1)}), bf16[128,12,1536]{2,1,0:T(8,128)(2,1)}) %all-gather.31.cloned.1.call-update) | async-done | bytes 4718608 | tf_op jit(solution)/shard_map/all_gather | solution.py:210
  912.0 8.2 reshape.341
  936.1 205.2 %all-gather.4 = bf16[128,12,16]{2,1,0:T(8,128)(2,1)} all-gather(bf16[1,12,16]{2,1,0:T(8,128)(2,1)S(1)} %bitcast.486), channel_id=1, replica_groups=mesh['dp'=8,'ctx'=16] {'dp','ctx'}, dimensions={0}, use_global_device_ids=true | all-gather | bytes 49536 | tf_op jit(solution)/shard_map/all_gather | solution.py:211
  1172.1 13.9 all-to-all-done.2
  1186.0 8.4 fusion.100
  1212.9 18.9 all-to-all-done.1
  1245.6 18.5 all-to-all-done.3
  1278.0 48.9 %while.52 = (s32[]{:T(128)}, f32[8,3,192,1]{2,0,3,1:T(8,128)S(1)}, s32[6,512]{1,0:T(8,128)}, s32[6,512]{1,0:T(8,128)}, s32[192]{0:T(256)S(1)}, /*index=5*/bf16[6...) while((s32[]{:T(128)}, f32[8,3,192,1]{2,0,3,1:T(8,128)S(1)}, ...), condition=%wide.region_22.23_spmd.clone, body=%wide.region_20.22_spmd.clone.sunk | while | flops 616075968 | bytes 21406108 | solution.py:141
  1327.0 95.0 %while.53 = (s32[]{:T(128)}, f32[192,8,3,64]{0,3,2,1:T(8,128)S(1)}, bf16[6,512,8,64]{1,3,2,0:T(8,128)(2,1)}, bf16[6,512,8,64]{1,3,2,0:T(8,128)(2,1)}, bf16[6,512...) while((s32[]{:T(128)}, f32[192,8,3,64]{0,3,2,1:T(8,128)S(1)}, ...), condition=%wide.region_24.25_spmd.clone, body=%wide.region_23.24_spmd.clone.sunk | while | flops 1534689536 | bytes 51220928 | solution.py:168
  1421.9 8.2 copy.167
  1430.1 9.3 reshape.365
  1439.5 7.8 copy.166
  1447.4 9.5 reshape.363
  1489.3 20.9 reduce-scatter.28.cloned.1.call-done
  1513.5 74.7 %reduce-scatter.26.cloned.1.call-done = bf16[192,512]{1,0:T(8,128)(2,1)} async-done(((bf16[3072,512]{1,0:T(8,128)(2,1)}), bf16[192,512]{1,0:T(8,128)(2,1)}) %reduce-scatter.26.cloned.1.call-update) | async-done | bytes 196624
  1591.4 416.9 %fusion.159 = (f32[16,1536]{1,0:T(8,128)S(1)}, f32[16,512]{1,0:T(8,128)S(1)}, f32[16,512]{1,0:T(8,128)S(1)}, f32[16,1536]{1,0:T(8,128)}, f32[16,16]{1,0:T(8,128)S(1)}) fusion(f32[1536,1536]{1,0:T(8,128)} %fusion.154, f32[1536,512]{1,0:T(8,128)} %fusion.152, f32[1536,512]{1,0:T(8,128)} %fusion.150, f32[1536,1536]{1,0:T(8,128)} %fusion.138, ...), kind=kCustom, calls=%all-reduce-scatter.5 | all-reduce-scatter fusion | flops 8421377 | bytes 25527296
  2015.6 8.9 collective-permute-start.157
  2031.4 7.2 collective-permute-start.61
  2085.7 6.8 collective-permute-start.144
  2096.8 7.8 collective-permute-start.142
  2105.4 6.8 collective-permute-start.141
  2118.5 11.0 collective-permute-start.138
  2137.2 10.0 collective-permute-start.136
  2158.7 8.9 collective-permute-start.133
  2172.6 7.8 collective-permute-start.131
  2181.3 7.9 collective-permute-start.130
  2199.6 20.7 collective-permute-start.60
  2389.0 7.2 collective-permute-start.26
  2435.9 8.5 collective-permute-start.10
  2512.3 67.5 %all-reduce.14 = (f32[1536]{0:T(1024)S(1)}, f32[1536]{0:T(1024)S(1)}) all-reduce(f32[1536]{0:T(1024)S(1)} %get-tuple-element.630, f32[1536]{0:T(1024)S(1)} %copy-done.132), channel_id=4, replica_groups=mesh['dp'=8,'ctx'=16] {'dp','ctx'}, use_global_device_ids=true, to_apply=%region_29.30.clone | all-reduce | flops 3072 | bytes 24576
  2604.8 26.7 concatenate.1
  2631.6 19.5 concatenate.2
  2655.5 7.1 collective-permute-start.109
  2687.4 30.9 %concatenate = f32[524,1536]{1,0:T(8,128)S(1)} concatenate(f32[12,1536]{1,0:T(8,128)} %copy-done.31, f32[16,1536]{1,0:T(8,128)S(1)} %copy-done.29, f32[16,1536]{1,0:T(8,128)} %copy-done.30, f32[16,1536]{1,0:T(8,128)} %copy-done.32, f32[16,1536]{1,0:T(8,128)} %copy-done.33, f32[16,1536]{1,0:T(8,128)} %copy-done.34, f32[16,1536]{1,0:T(8,128)} %copy-done.35, f32[16,1536]{1,0:T(8,128)} %copy-done.36, ...), dimensions={0} | concatenate | bytes 6438912
  2735.3 30.0 %concatenate.3 = f32[524,1536]{1,0:T(8,128)S(1)} concatenate(f32[12,1536]{1,0:T(8,128)S(1)} %copy-done.27, f32[16,1536]{1,0:T(8,128)} %copy-done.43, f32[16,1536]{1,0:T(8,128)} %copy-done.46, f32[16,1536]{1,0:T(8,128)} %copy-done.48, f32[16,1536]{1,0:T(8,128)} %copy-done.50, f32[16,1536]{1,0:T(8,128)} %copy-done.52, f32[16,1536]{1,0:T(8,128)} %copy-done.54, ...), dimensions={0} | concatenate | bytes 6438912
  (1029 shorter events, 826.1 us)
Async XLA Ops:
  7.2 199.8 %all-gather.25.cloned.1.call-start = ((), (), s32[]{:S(2)}) async-start(), calls=%async_computation.17 | async-start | bytes 2113536 | tf_op jit(solution)/shard_map/all_gather | solution.py:209
  7.9 393.6 %all-gather.27.cloned.1.call-start = ((), (), s32[]{:S(2)}) async-start(), calls=%async_computation.18 | async-start | bytes 2113536 | tf_op jit(solution)/shard_map/all_gather | solution.py:208
  8.7 447.5 %all-gather.15.cloned.1.call-start = ((), (), s32[]{:S(2)}) async-start(), calls=%async_computation.9 | async-start | bytes 3342336 | tf_op jit(solution)/shard_map/all_gather | solution.py:236
  210.8 299.2 %all-gather.17.cloned.1.call-start = ((), (), s32[]{:S(2)}) async-start(), calls=%async_computation.10 | async-start | bytes 3342336 | tf_op jit(solution)/shard_map/all_gather | solution.py:235
  407.9 302.8 %all-gather.29.cloned.1.call-start = ((), (), s32[]{:S(2)}) async-start(), calls=%async_computation.19 | async-start | bytes 6340608 | tf_op jit(solution)/shard_map/all_gather | solution.py:207
  408.5 503.5 %all-gather.31.cloned.1.call-start = ((), (), s32[]{:S(2)}) async-start(), calls=%async_computation.20 | async-start | bytes 6340608 | tf_op jit(solution)/shard_map/all_gather | solution.py:210
  409.0 747.6 %all-gather.21.cloned.1.call-start = ((), (), s32[]{:S(2)}) async-start(), calls=%async_computation.12 | async-start | bytes 3538944 | tf_op jit(solution)/shard_map/all_gather | solution.py:217
  409.8 753.2 %all-gather.19.cloned.1.call-start = ((), (), s32[]{:S(2)}) async-start(), calls=%async_computation.11 | async-start | bytes 3538944 | tf_op jit(solution)/shard_map/all_gather | solution.py:216
  410.5 761.6 %all-gather.23.cloned.1.call-start = ((), (), s32[]{:S(2)}) async-start(), calls=%async_computation.13 | async-start | bytes 3538944 | tf_op jit(solution)/shard_map/all_gather | solution.py:218
  930.1 221.9 %all-to-all-start = ((bf16[16,1,36,1536]{3,2,1,0:T(8,128)(2,1)}), bf16[16,1,36,1536]{3,2,1,0:T(8,128)(2,1)}, u32[]{:S(2)}, u32[]{:S(2)}) async-start(bf16[16,1,36,1536]{3,2,1,0:T(8,128)(2,1)} %bitcast.463), calls=%async_computation | async-start | bytes 3932160 | tf_op jit(solution)/shard_map/all_to_all | solution.py:278
  1152.0 34.0 %all-to-all-start.2 = ((bf16[16,1,36,1536]{3,2,1,0:T(8,128)(2,1)}), bf16[16,1,36,1536]{3,2,1,0:T(8,128)(2,1)}, u32[]{:S(2)}, u32[]{:S(2)}) async-start(bf16[16,1,36,1536]{3,2,1,0:T(8,128)(2,1)} %bitcast.462), calls=%async_computation.2 | async-start | bytes 3932160 | tf_op jit(solution)/shard_map/all_to_all | solution.py:322
  1199.0 32.8 %all-to-all-start.1 = ((bf16[16,1,36,1536]{3,2,1,0:T(8,128)(2,1)}), bf16[16,1,36,1536]{3,2,1,0:T(8,128)(2,1)}, u32[]{:S(2)}, u32[]{:S(2)}) async-start(bf16[16,1,36,1536]{3,2,1,0:T(8,128)(2,1)} %fusion.90), calls=%async_computation.1 | async-start | bytes 3932160 | tf_op jit(solution)/shard_map/all_to_all | solution.py:286
  1231.7 32.4 %all-to-all-start.3 = ((bf16[16,1,36,1536]{3,2,1,0:T(8,128)(2,1)}), bf16[16,1,36,1536]{3,2,1,0:T(8,128)(2,1)}, u32[]{:S(2)}, u32[]{:S(2)}) async-start(bf16[16,1,36,1536]{3,2,1,0:T(8,128)(2,1)} %fusion.93), calls=%async_computation.3 | async-start | bytes 3932160 | tf_op jit(solution)/shard_map/all_to_all | solution.py:358
  1236.8 273.4 %reduce-scatter.28.cloned.1.call-start = ((), (), s32[]{:S(2)}) async-start(), calls=%async_computation.22 | async-start | bytes 3342336
  1439.5 148.7 %reduce-scatter.26.cloned.1.call-start = ((), (), s32[]{:S(2)}) async-start(), calls=%async_computation.21 | async-start | bytes 3342336
  1456.9 994.5 %reduce-scatter.24.cloned.1.call-start = ((), (), s32[]{:S(2)}) async-start(), calls=%async_computation.16 | async-start | bytes 3538944 | tf_op jit(solution)/shard_map/reduce_scatter | solution.py:354
  1463.3 990.1 %reduce-scatter.22.cloned.1.call-start = ((), (), s32[]{:S(2)}) async-start(), calls=%async_computation.15 | async-start | bytes 3538944 | tf_op jit(solution)/shard_map/reduce_scatter | solution.py:351
  1469.6 985.8 %reduce-scatter.20.cloned.1.call-start = ((), (), s32[]{:S(2)}) async-start(), calls=%async_computation.14 | async-start | bytes 3538944 | tf_op jit(solution)/shard_map/reduce_scatter | solution.py:348
  2008.3 30.3 %collective-permute-start.158 = (f32[16,16]{1,0:T(8,128)S(1)}, f32[16,16]{1,0:T(8,128)S(1)}, u32[]{:S(2)}, u32[]{:S(2)}) collective-permute-start(f32[16,16]{1,0:T(8,128)S(1)} %get-tuple-element.733), channel_id=1, source_target_pairs={{0,31},{1,32},{2,33},{3,34},{4,35},{5,36},{6,37},{7,38},{8,39},{9,... | collective-permute-start | bytes 3080
  2015.6 25.6 collective-permute-start.157
  2024.4 195.9 %collective-permute-start.95 = (f32[12,512]{1,0:T(8,128)S(1)}, f32[12,512]{1,0:T(8,128)S(1)}, u32[]{:S(2)}, u32[]{:S(2)}) collective-permute-start(f32[12,512]{1,0:T(8,128)S(1)} %slice.11), channel_id=1, source_target_pairs={{0,32},{1,33},{2,34},{3,35},{4,36},{5,37},{6,38},{7,39},{8,40},{9,... | collective-permute-start | bytes 73736
  2027.7 200.3 %collective-permute-start.62 = (f32[16,512]{1,0:T(8,128)S(1)}, f32[16,512]{1,0:T(8,128)S(1)}, u32[]{:S(2)}, u32[]{:S(2)}) collective-permute-start(f32[16,512]{1,0:T(8,128)S(1)} %get-tuple-element.730), channel_id=1, source_target_pairs={{0,31},{1,32},{2,33},{3,34},{4,35},{5,36},{6,37},{7,38},{8,39},{9,... | collective-permute-start | bytes 98312
  2031.4 198.0 %collective-permute-start.61 = (f32[16,512]{1,0:T(8,128)S(1)}, f32[16,512]{1,0:T(8,128)S(1)}, u32[]{:S(2)}, u32[]{:S(2)}) collective-permute-start(f32[16,512]{1,0:T(8,128)S(1)} %get-tuple-element.730), channel_id=1, source_target_pairs={{0,30},{1,31},{2,32},{3,33},{4,34},{5,35},{6,36},{7,37},{8,38},{9,... | collective-permute-start | bytes 98312
  2094.0 127.6 %collective-permute-start.63 = (f32[12,512]{1,0:T(8,128)S(1)}, f32[12,512]{1,0:T(8,128)S(1)}, u32[]{:S(2)}, u32[]{:S(2)}) collective-permute-start(f32[12,512]{1,0:T(8,128)S(1)} %slice.10), channel_id=1, source_target_pairs={{0,32},{1,33},{2,34},{3,35},{4,36},{5,37},{6,38},{7,39},{8,40},{9,... | collective-permute-start | bytes 73736
  2199.6 31.1 %collective-permute-start.60 = (f32[16,512]{1,0:T(8,128)S(1)}, f32[16,512]{1,0:T(8,128)S(1)}, u32[]{:S(2)}, u32[]{:S(2)}) collective-permute-start(f32[16,512]{1,0:T(8,128)S(1)} %get-tuple-element.730), channel_id=1, source_target_pairs={{0,29},{1,30},{2,31},{3,32},{4,33},{5,34},{6,35},{7,36},{8,37},{9,... | collective-permute-start | bytes 98312
  2367.6 28.6 %collective-permute-start.30 = (f32[16,1536]{1,0:T(8,128)S(1)}, f32[16,1536]{1,0:T(8,128)S(1)}, u32[]{:S(2)}, u32[]{:S(2)}) collective-permute-start(f32[16,1536]{1,0:T(8,128)S(1)} %get-tuple-element.729), channel_id=1, source_target_pairs={{0,31},{1,32},{2,33},{3,34},{4,35},{5,36},{6,37},{7,38},{8,39},{9,... | collective-permute-start | bytes 294920
  2369.7 27.9 %collective-permute-start.29 = (f32[16,1536]{1,0:T(8,128)S(1)}, f32[16,1536]{1,0:T(8,128)S(1)}, u32[]{:S(2)}, u32[]{:S(2)}) collective-permute-start(f32[16,1536]{1,0:T(8,128)S(1)} %get-tuple-element.729), channel_id=1, source_target_pairs={{0,30},{1,31},{2,32},{3,33},{4,34},{5,35},{6,36},{7,37},{8,38},{9,... | collective-permute-start | bytes 294920
  2423.3 21.1 collective-permute-start.14
  2426.1 31.4 %collective-permute-start.13 = (f32[16,1536]{1,0:T(8,128)S(1)}, f32[16,1536]{1,0:T(8,128)}, u32[]{:S(2)}, u32[]{:S(2)}) collective-permute-start(f32[16,1536]{1,0:T(8,128)S(1)} %get-tuple-element.729), channel_id=1, source_target_pairs={{0,14},{1,15},{2,16},{3,17},{4,18},{5,19},{6,20},{7,21},{8,22},{9,... | collective-permute-start | bytes 294920
  2431.3 27.4 collective-permute-start.12
  2434.0 26.4 collective-permute-start.11
  2435.9 27.0 collective-permute-start.10
  2444.4 21.2 collective-permute-start.9
  2499.2 87.6 %collective-permute-start.120 = (f32[16,1536]{1,0:T(8,128)}, f32[16,1536]{1,0:T(8,128)S(1)}, u32[]{:S(2)}, u32[]{:S(2)}) collective-permute-start(f32[16,1536]{1,0:T(8,128)} %get-tuple-element.732), channel_id=1, source_target_pairs={{0,25},{1,26},{2,27},{3,28},{4,29},{5,30},{6,31},{7,32},{8,33},{9,... | collective-permute-start | bytes 294920
  2500.8 89.6 %collective-permute-start.119 = (f32[16,1536]{1,0:T(8,128)}, f32[16,1536]{1,0:T(8,128)S(1)}, u32[]{:S(2)}, u32[]{:S(2)}) collective-permute-start(f32[16,1536]{1,0:T(8,128)} %get-tuple-element.732), channel_id=1, source_target_pairs={{0,24},{1,25},{2,26},{3,27},{4,28},{5,29},{6,30},{7,31},{8,32},{9,... | collective-permute-start | bytes 294920
  2502.7 92.5 %collective-permute-start.118 = (f32[16,1536]{1,0:T(8,128)}, f32[16,1536]{1,0:T(8,128)S(1)}, u32[]{:S(2)}, u32[]{:S(2)}) collective-permute-start(f32[16,1536]{1,0:T(8,128)} %get-tuple-element.732), channel_id=1, source_target_pairs={{0,23},{1,24},{2,25},{3,26},{4,27},{5,28},{6,29},{7,30},{8,31},{9,... | collective-permute-start | bytes 294920
  2505.0 93.9 %collective-permute-start.117 = (f32[16,1536]{1,0:T(8,128)}, f32[16,1536]{1,0:T(8,128)S(1)}, u32[]{:S(2)}, u32[]{:S(2)}) collective-permute-start(f32[16,1536]{1,0:T(8,128)} %get-tuple-element.732), channel_id=1, source_target_pairs={{0,22},{1,23},{2,24},{3,25},{4,26},{5,27},{6,28},{7,29},{8,30},{9,... | collective-permute-start | bytes 294920
  2508.4 92.5 %collective-permute-start.116 = (f32[16,1536]{1,0:T(8,128)}, f32[16,1536]{1,0:T(8,128)S(1)}, u32[]{:S(2)}, u32[]{:S(2)}) collective-permute-start(f32[16,1536]{1,0:T(8,128)} %get-tuple-element.732), channel_id=1, source_target_pairs={{0,21},{1,22},{2,23},{3,24},{4,25},{5,26},{6,27},{7,28},{8,29},{9,... | collective-permute-start | bytes 294920
  2586.8 64.2 %collective-permute-start.115 = (f32[16,1536]{1,0:T(8,128)}, f32[16,1536]{1,0:T(8,128)S(1)}, u32[]{:S(2)}, u32[]{:S(2)}) collective-permute-start(f32[16,1536]{1,0:T(8,128)} %get-tuple-element.732), channel_id=1, source_target_pairs={{0,20},{1,21},{2,22},{3,23},{4,24},{5,25},{6,26},{7,27},{8,28},{9,... | collective-permute-start | bytes 294920
  2590.4 65.1 %collective-permute-start.114 = (f32[16,1536]{1,0:T(8,128)}, f32[16,1536]{1,0:T(8,128)S(1)}, u32[]{:S(2)}, u32[]{:S(2)}) collective-permute-start(f32[16,1536]{1,0:T(8,128)} %get-tuple-element.732), channel_id=1, source_target_pairs={{0,19},{1,20},{2,21},{3,22},{4,23},{5,24},{6,25},{7,26},{8,27},{9,... | collective-permute-start | bytes 294920
  2595.2 67.4 %collective-permute-start.113 = (f32[16,1536]{1,0:T(8,128)}, f32[16,1536]{1,0:T(8,128)S(1)}, u32[]{:S(2)}, u32[]{:S(2)}) collective-permute-start(f32[16,1536]{1,0:T(8,128)} %get-tuple-element.732), channel_id=1, source_target_pairs={{0,18},{1,19},{2,20},{3,21},{4,22},{5,23},{6,24},{7,25},{8,26},{9,... | collective-permute-start | bytes 294920
  2598.9 65.1 %collective-permute-start.112 = (f32[16,1536]{1,0:T(8,128)}, f32[16,1536]{1,0:T(8,128)S(1)}, u32[]{:S(2)}, u32[]{:S(2)}) collective-permute-start(f32[16,1536]{1,0:T(8,128)} %get-tuple-element.732), channel_id=1, source_target_pairs={{0,17},{1,18},{2,19},{3,20},{4,21},{5,22},{6,23},{7,24},{8,25},{9,... | collective-permute-start | bytes 294920
  2600.9 67.3 %collective-permute-start.111 = (f32[16,1536]{1,0:T(8,128)}, f32[16,1536]{1,0:T(8,128)S(1)}, u32[]{:S(2)}, u32[]{:S(2)}) collective-permute-start(f32[16,1536]{1,0:T(8,128)} %get-tuple-element.732), channel_id=1, source_target_pairs={{0,16},{1,17},{2,18},{3,19},{4,20},{5,21},{6,22},{7,23},{8,24},{9,... | collective-permute-start | bytes 294920
  2672.1 46.3 %collective-permute-start.105 = (f32[16,1536]{1,0:T(8,128)}, f32[16,1536]{1,0:T(8,128)}, u32[]{:S(2)}, u32[]{:S(2)}) collective-permute-start(f32[16,1536]{1,0:T(8,128)} %get-tuple-element.732), channel_id=1, source_target_pairs={{0,10},{1,11},{2,12},{3,13},{4,14},{5,15},{6,16},{7,17},{8,18},{9,... | collective-permute-start | bytes 294920
  2676.5 44.5 %collective-permute-start.104 = (f32[16,1536]{1,0:T(8,128)}, f32[16,1536]{1,0:T(8,128)}, u32[]{:S(2)}, u32[]{:S(2)}) collective-permute-start(f32[16,1536]{1,0:T(8,128)} %get-tuple-element.732), channel_id=1, source_target_pairs={{0,9},{1,10},{2,11},{3,12},{4,13},{5,14},{6,15},{7,16},{8,17},{9,1... | collective-permute-start | bytes 294920
  2678.4 46.0 %collective-permute-start.103 = (f32[16,1536]{1,0:T(8,128)}, f32[16,1536]{1,0:T(8,128)}, u32[]{:S(2)}, u32[]{:S(2)}) collective-permute-start(f32[16,1536]{1,0:T(8,128)} %get-tuple-element.732), channel_id=1, source_target_pairs={{0,8},{1,9},{2,10},{3,11},{4,12},{5,13},{6,14},{7,15},{8,16},{9,17... | collective-permute-start | bytes 294920
  2680.6 48.4 %collective-permute-start.102 = (f32[16,1536]{1,0:T(8,128)}, f32[16,1536]{1,0:T(8,128)}, u32[]{:S(2)}, u32[]{:S(2)}) collective-permute-start(f32[16,1536]{1,0:T(8,128)} %get-tuple-element.732), channel_id=1, source_target_pairs={{0,7},{1,8},{2,9},{3,10},{4,11},{5,12},{6,13},{7,14},{8,15},{9,16}... | collective-permute-start | bytes 294920
  2684.1 46.2 %collective-permute-start.101 = (f32[16,1536]{1,0:T(8,128)}, f32[16,1536]{1,0:T(8,128)}, u32[]{:S(2)}, u32[]{:S(2)}) collective-permute-start(f32[16,1536]{1,0:T(8,128)} %get-tuple-element.732), channel_id=1, source_target_pairs={{0,6},{1,7},{2,8},{3,9},{4,10},{5,11},{6,12},{7,13},{8,14},{9,15},... | collective-permute-start | bytes 294920
  (343 other events, 17468.4 us)
Sparse Core Ops, SparseCore 0:
  9.7 197.2 all-gather.24
  208.7 192.7 all-gather.26
  404.6 51.5 all-gather.14
  459.0 50.9 all-gather.16
  511.6 199.1 all-gather.28
  712.3 199.6 all-gather.30
  913.6 90.7 all-gather.20
  1006.1 71.9 all-gather.18
  1079.8 92.2 all-gather.22
  1439.6 70.5 reduce-scatter.27
  1514.2 73.8 reduce-scatter.25
  1590.4 119.3 reduce-scatter.23
  1712.2 133.1 reduce-scatter.21
  1847.7 126.8 reduce-scatter.19
where the time goes:
time: 2800 us; the launch traced here: 2770 us
  waiting for transfers between devices  863 us (31%)
  blocking collectives  758 us (27%)
  starting transfers between devices  558 us (20%)
  matrix products  291 us (10%)
  local copies, waits for them, and re-layouts  247 us (9%)
  other arithmetic  35.8 us (1%)
    unnamed x3, blocking collectives  553 us
    unnamed x162, starting transfers between devices  536 us
    all_gather x1, blocking collectives, shards(): lax.all_gather(w_router, ('dp', 'ctx'), axis=0, tiled=True)  205 us
    unnamed x460, local copies, waits for them, and re-layouts  203 us
    all_gather x1, waiting for transfers between devices, shards(): lax.all_gather(key_weight, ('dp', 'ctx'), axis=0, tiled=True)  191 us
    all_gather x1, waiting for transfers between devices, shards(): lax.all_gather(w_query, ('dp', 'ctx'), axis=0, tiled=True)  184 us
    all_gather x1, waiting for transfers between devices, shards(): lax.all_gather(value_weight, ('dp', 'ctx'), axis=0, tiled=True)  126 us
    unnamed x176, waiting for transfers between devices  114 us
  transfers between devices with their start and end apart: 178, of which 29 were waited for; matrix products, arithmetic and copies ran while one was open for 28% of the time, Pallas kernels for 0%

commit v1 on v0

--- a/solution.py
+++ b/solution.py
@@ -3,6 +3,8 @@
 import jax
 import jax.numpy as jnp
 from jax import lax
+from jax.experimental import pallas as pl
+from jax.experimental.pallas import tpu as pltpu
 from jax.sharding import PartitionSpec as P
 
 QUERY_HEAD_COUNT = 24
@@ -171,6 +173,359 @@
         (key_blocks, value_blocks, key_pos, key_seg),
     )
     return (grad_query_heads * factor, key_block_gradient, value_block_gradient)
+
+
+MESH = pl.DeviceIdType.MESH
+
+PACK = 4608
+HALF = PACK // 2
+QUARTER = PACK // 4
+RING_ORDERS = (("x", "y", "z"), ("y", "z", "x"), ("z", "x", "y"))
+
+
+def place():
+    dp = lax.axis_index("dp")
+    ctx = lax.axis_index("ctx")
+    return {"y": dp // 2, "z": (ctx // 8) * 2 + dp % 2, "x": (ctx // 2) % 4, "core": ctx % 2}
+
+
+def device_of(spot):
+    z = spot["z"]
+    return (spot["y"] * 2 + z % 2, (z // 2) * 8 + spot["x"] * 2 + spot["core"])
+
+
+def moved(spot, axis, step):
+    other = dict(spot)
+    if axis == "core":
+        other["core"] = 1 - spot["core"]
+    else:
+        other[axis] = (spot[axis] + step) % 4
+    return other
+
+
+def member(spot, step):
+    index = (spot["x"] % 2) * 2 + spot["core"]
+    target = (index // 2 + step // 2) % 2 * 2 + (index % 2 + step % 2) % 2
+    other = dict(spot)
+    other["x"] = (spot["x"] // 2) * 2 + target // 2
+    other["core"] = target % 2
+    return other, target
+
+
+def meet(spot):
+    barrier = pltpu.get_barrier_semaphore()
+    others = [member(spot, step)[0] for step in (1, 2, 3)]
+    others += [moved(spot, axis, step) for axis in "xyz" for step in (1, 2, 3)]
+    for other in others:
+        pl.semaphore_signal(barrier, inc=1, device_id=device_of(other), device_id_type=MESH)
+    pl.semaphore_wait(barrier, len(others))
+
+
+def region(spot, known, part, base):
+    def pick(axis, value, size):
+        return pl.ds(0, size) if axis in known else pl.ds(value, 1)
+
+    z = spot["z"]
+    if "x" in known:
+        columns = pl.ds(base, HALF)
+    else:
+        columns = pl.ds(pl.multiple_of(base + (spot["x"] % 2) * QUARTER, 128), QUARTER)
+    return (
+        pick("y", spot["y"], 4),
+        pick("z", z % 2, 2),
+        pick("z", z // 2, 2),
+        pick("x", spot["x"] // 2, 2),
+        pl.ds(part * 16, 16),
+        columns,
+    )
+
+
+def gather_kernel(shard, merge, out, pieces, joined, send0, recv0, send, recv, send_core, recv_core, local):
+    spot = place()
+    meet(spot)
+    index = (spot["x"] % 2) * 2 + spot["core"]
+    quarter = spot["core"] * 2 + spot["x"] % 2
+    copies = []
+    for step in (1, 2, 3):
+        other, target = member(spot, step)
+        goal = other["core"] * 2 + other["x"] % 2
+        copy = pltpu.make_async_remote_copy(
+            src_ref=shard.at[:, pl.ds(pl.multiple_of(goal * QUARTER, 128), QUARTER)],
+            dst_ref=pieces.at[index],
+            send_sem=send0.at[step - 1],
+            recv_sem=recv0.at[step - 1],
+            device_id=device_of(other),
+            device_id_type=MESH,
+        )
+        copy.start()
+        copies.append(copy)
+    pieces[index] = shard[:, pl.ds(pl.multiple_of(quarter * QUARTER, 128), QUARTER)]
+    for copy in copies:
+        copy.wait()
+    joined[...] = jnp.dot(
+        merge[...], pieces[...].reshape(64, QUARTER), preferred_element_type=jnp.float32
+    ).astype(jnp.bfloat16)
+    base = pl.multiple_of(spot["core"] * HALF, 128)
+    mine = region(spot, "", 0, base)
+    own = pltpu.make_async_copy(
+        joined,
+        out.at[spot["y"], spot["z"] % 2, spot["z"] // 2, spot["x"] // 2, :, mine[5]],
+        local,
+    )
+    own.start()
+    own.wait()
+    mate = moved(spot, "core", 1)
+    core_copies = []
+
+    def to_mate(number, where):
+        copy = pltpu.make_async_remote_copy(
+            src_ref=out.at[where],
+            dst_ref=out.at[where],
+            send_sem=send_core.at[number],
+            recv_sem=recv_core.at[number],
+            device_id=device_of(mate),
+            device_id_type=MESH,
+        )
+        copy.start()
+        core_copies.append(copy)
+
+    flights = {}
+    for stage in range(3):
+        for part, order in enumerate(RING_ORDERS):
+            axis, known = order[stage], order[:stage]
+            if stage > 0:
+                for copy in flights[part]:
+                    copy.wait_recv()
+            where = region(spot, known, part, base)
+            started = []
+            for step in (1, 3, 2):
+                number = (stage * 3 + part) * 3 + step - 1
+                copy = pltpu.make_async_remote_copy(
+                    src_ref=out.at[where],
+                    dst_ref=out.at[where],
+                    send_sem=send.at[number],
+                    recv_sem=recv.at[number],
+                    device_id=device_of(moved(spot, axis, step)),
+                    device_id_type=MESH,
+                )
+                copy.start()
+                started.append(copy)
+            if stage == 2:
+                to_mate(part * 4, where)
+            flights[part] = started
+            copies += started
+    for step in (1, 3, 2):
+        for part, order in enumerate(RING_ORDERS):
+            axis = order[2]
+            flights[part][(1, 3, 2).index(step)].wait_recv()
+            source = moved(spot, axis, -step)
+            to_mate(part * 4 + step, region(source, order[:2], part, base))
+    for copy in copies[3:]:
+        copy.wait_send()
+    for copy in core_copies:
+        copy.wait()
+
+
+def gather_weights(shard):
+    shard = jnp.pad(shard, ((0, 4), (0, 0)))
+    target = jnp.arange(48, dtype=jnp.int32)[:, None]
+    source = jnp.arange(64, dtype=jnp.int32)[None, :]
+    merge = ((target // 12 == source // 16) & (target % 12 == source % 16)).astype(jnp.bfloat16)
+    out = pl.pallas_call(
+        gather_kernel,
+        out_shape=jax.ShapeDtypeStruct((4, 2, 2, 2, 48, PACK), jnp.bfloat16),
+        in_specs=[pl.BlockSpec(memory_space=pltpu.VMEM)] * 2,
+        out_specs=pl.BlockSpec(memory_space=pl.ANY),
+        scratch_shapes=[
+            pltpu.VMEM((4, 16, QUARTER), jnp.bfloat16),
+            pltpu.VMEM((48, QUARTER), jnp.bfloat16),
+            pltpu.SemaphoreType.DMA((3,)),
+            pltpu.SemaphoreType.DMA((3,)),
+            pltpu.SemaphoreType.DMA((27,)),
+            pltpu.SemaphoreType.DMA((27,)),
+            pltpu.SemaphoreType.DMA((12,)),
+            pltpu.SemaphoreType.DMA((12,)),
+            pltpu.SemaphoreType.DMA,
+        ],
+        compiler_params=pltpu.CompilerParams(collective_id=1, has_side_effects=True),
+        cost_estimate=pl.CostEstimate(flops=0, bytes_accessed=28 * 2**20, transcendentals=0),
+        name="gather_weights",
+    )(shard, merge)
+    return out.reshape(1536, PACK)
+
+
+def scatter_kernel(grads, split, out, total, from_mate, done, packed, send_core, recv_core, send, recv, send0, recv0, *flat_landing):
+    spot = place()
+    meet(spot)
+    mate = moved(spot, "core", 1)
+    base = pl.multiple_of(spot["core"] * HALF, 128)
+    mate_base = pl.multiple_of(mate["core"] * HALF, 128)
+    core_copies = []
+    for part in range(3):
+        rows = pl.ds(part * 16, 16)
+        copy = pltpu.make_async_remote_copy(
+            src_ref=grads.at[:, :, :, :, rows, pl.ds(mate_base, HALF)],
+            dst_ref=from_mate.at[:, :, :, :, rows, :],
+            send_sem=send_core.at[part],
+            recv_sem=recv_core.at[part],
+            device_id=device_of(mate),
+            device_id_type=MESH,
+        )
+        copy.start()
+        core_copies.append(copy)
+    landing = (flat_landing[:3], flat_landing[3:6], flat_landing[6:])
+    all_copies = list(core_copies)
+
+    for part, order in enumerate(RING_ORDERS):
+        rows = pl.ds(part * 16, 16)
+        core_copies[part].wait_recv()
+
+        @pl.loop(0, 32)
+        def _(block):
+            at = (block // 8, (block // 4) % 2, (block // 2) % 2, block % 2, rows)
+            total[at] = (
+                grads[at + (pl.ds(base, HALF),)].astype(jnp.float32)
+                + from_mate[at].astype(jnp.float32)
+            ).astype(jnp.bfloat16)
+
+        flights = start_ring(spot, part, 0, total, landing, send, recv, all_copies)
+        if part == 0:
+            pending = []
+        pending.append(flights)
+    for stage in range(3):
+        for part, order in enumerate(RING_ORDERS):
+            known = order[: 2 - stage]
+            for copy in pending[part]:
+                copy.wait_recv()
+            where = region(spot, known, part, 0)
+            add_ring(spot, known, part, total, landing[stage][part], where)
+            if stage < 2:
+                pending[part] = start_ring(spot, part, stage + 1, total, landing, send, recv, all_copies)
+    index = (spot["x"] % 2) * 2 + spot["core"]
+    quarter = spot["core"] * 2 + spot["x"] % 2
+    mine = region(spot, "", 0, 0)
+    done[...] = total[spot["y"], spot["z"] % 2, spot["z"] // 2, spot["x"] // 2, :, mine[5]]
+    packed[...] = (
+        jnp.dot(split[...], done[...], preferred_element_type=jnp.float32)
+        .astype(jnp.bfloat16)
+        .reshape(4, 16, QUARTER)
+    )
+    columns = pl.ds(pl.multiple_of(quarter * QUARTER, 128), QUARTER)
+    copies = []
+    for step in (1, 2, 3):
+        other, target = member(spot, step)
+        copy = pltpu.make_async_remote_copy(
+            src_ref=packed.at[target],
+            dst_ref=out.at[:, columns],
+            send_sem=send0.at[step - 1],
+            recv_sem=recv0.at[step - 1],
+            device_id=device_of(other),
+            device_id_type=MESH,
+        )
+        copy.start()
+        copies.append(copy)
+    out[:, columns] = packed[index]
+    for copy in copies:
+        copy.wait()
+    for copy in all_copies:
+        copy.wait_send()
+
+
+def start_ring(spot, part, stage, total, landing, send, recv, all_copies):
+    order = RING_ORDERS[part]
+    axis, known = order[2 - stage], order[: 2 - stage]
+    started = []
+    for step in (1, 3, 2):
+        other = moved(spot, axis, step)
+        number = (stage * 3 + part) * 3 + step - 1
+        copy = pltpu.make_async_remote_copy(
+            src_ref=total.at[region(other, known, part, 0)],
+            dst_ref=landing[stage][part].at[step - 1],
+            send_sem=send.at[number],
+            recv_sem=recv.at[number],
+            device_id=device_of(other),
+            device_id_type=MESH,
+        )
+        copy.start()
+        started.append(copy)
+    all_copies += started
+    return started
+
+
+def landing_shape(known):
+    return (
+        4 if "y" in known else 1,
+        2 if "z" in known else 1,
+        2 if "z" in known else 1,
+        2 if "x" in known else 1,
+        16,
+        HALF if "x" in known else QUARTER,
+    )
+
+
+def add_ring(spot, known, part, total, landing, where):
+    shape = landing_shape(known)
+    count = shape[0] * shape[1] * shape[2] * shape[3]
+
+    def body(block):
+        a, b, c, d = (
+            block // (shape[1] * shape[2] * shape[3]),
+            (block // (shape[2] * shape[3])) % shape[1],
+            (block // shape[3]) % shape[2],
+            block % shape[3],
+        )
+        at = (
+            a + (0 if "y" in known else spot["y"]),
+            b + (0 if "z" in known else spot["z"] % 2),
+            c + (0 if "z" in known else spot["z"] // 2),
+            d + (0 if "x" in known else spot["x"] // 2),
+            pl.ds(part * 16, 16),
+            where[5],
+        )
+        summed = total[at].astype(jnp.float32)
+        for step in range(3):
+            summed += landing[step, a, b, c, d].astype(jnp.float32)
+        total[at] = summed.astype(jnp.bfloat16)
+
+    if count == 1:
+        body(0)
+    else:
+        pl.loop(0, count)(body)
+
+
+def scatter_sum(grads):
+    source = jnp.arange(48, dtype=jnp.int32)[None, :]
+    target = jnp.arange(64, dtype=jnp.int32)[:, None]
+    split = ((source // 12 == target // 16) & (source % 12 == target % 16)).astype(jnp.bfloat16)
+    landings = [
+        pltpu.VMEM((3,) + landing_shape(order[: 2 - stage]), jnp.bfloat16)
+        for stage in range(3)
+        for order in RING_ORDERS
+    ]
+    out = pl.pallas_call(
+        scatter_kernel,
+        out_shape=jax.ShapeDtypeStruct((16, PACK), jnp.bfloat16),
+        in_specs=[pl.BlockSpec(memory_space=pltpu.VMEM)] * 2,
+        out_specs=pl.BlockSpec(memory_space=pltpu.VMEM),
+        scratch_shapes=[
+            pltpu.VMEM((4, 2, 2, 2, 48, HALF), jnp.bfloat16),
+            pltpu.VMEM((4, 2, 2, 2, 48, HALF), jnp.bfloat16),
+            pltpu.VMEM((48, QUARTER), jnp.bfloat16),
+            pltpu.VMEM((4, 16, QUARTER), jnp.bfloat16),
+            pltpu.SemaphoreType.DMA((3,)),
+            pltpu.SemaphoreType.DMA((3,)),
+            pltpu.SemaphoreType.DMA((27,)),
+            pltpu.SemaphoreType.DMA((27,)),
+            pltpu.SemaphoreType.DMA((3,)),
+            pltpu.SemaphoreType.DMA((3,)),
+        ] + landings,
+        compiler_params=pltpu.CompilerParams(
+            collective_id=2, has_side_effects=True, vmem_limit_bytes=56 * 2**20
+        ),
+        cost_estimate=pl.CostEstimate(flops=0, bytes_accessed=28 * 2**20, transcendentals=0),
+        name="scatter_sum",
+    )(grads.reshape(4, 2, 2, 2, 48, PACK), split)
+    return out[:12]
 
 
 def shards(
@@ -202,16 +557,18 @@
     query_pos = ctx_index * device_local_rows + jnp.arange(device_local_rows, dtype=jnp.int32)
     query_seg = lax.dynamic_slice_in_dim(segments, ctx_index * device_local_rows, device_local_rows)
     key_value_shape = (count_of_blocks, rows_per_block, KEY_VALUE_HEADS, HEAD_SIZE)
-    gathered = (
-        lax.all_gather(gain_attn, ("dp", "ctx"), axis=0, tiled=True),
-        lax.all_gather(w_query, ("dp", "ctx"), axis=0, tiled=True),
-        lax.all_gather(key_weight, ("dp", "ctx"), axis=0, tiled=True),
-        lax.all_gather(value_weight, ("dp", "ctx"), axis=0, tiled=True),
-        lax.all_gather(w_out, ("dp", "ctx"), axis=0, tiled=True),
-        lax.all_gather(w_router, ("dp", "ctx"), axis=0, tiled=True),
-        lax.all_gather(gain_ffn, ("dp", "ctx"), axis=0, tiled=True),
-    )
-    gain_one, query_proj, key_proj, value_proj, out_proj, router_proj, gain_two = gathered
+    shard = jnp.concatenate(
+        [w_query, key_weight, value_weight, w_out, w_router, gain_attn[:, None], gain_ffn[:, None]],
+        axis=1,
+    )
+    packed = gather_weights(jnp.pad(shard, ((0, 0), (0, PACK - shard.shape[1]))))
+    query_proj = packed[:, :1536]
+    key_proj = packed[:, 1536:2048]
+    value_proj = packed[:, 2048:2560]
+    out_proj = packed[:, 2560:4096]
+    router_proj = packed[:, 4096:4112]
+    gain_one = packed[:, 4112]
+    gain_two = packed[:, 4113]
     expert_weights = (
         lax.all_gather(w_gate, "dp", axis=1, tiled=True),
         lax.all_gather(w_up, "dp", axis=1, tiled=True),
@@ -291,13 +648,7 @@
         jnp.bfloat16
     )
     gain_back, query_back, key_back, value_back, out_back, router_back, gain_ffn_back = (
-        lax.all_gather(gain_attn, ("dp", "ctx"), axis=0, tiled=True),
-        lax.all_gather(w_query, ("dp", "ctx"), axis=0, tiled=True),
-        lax.all_gather(key_weight, ("dp", "ctx"), axis=0, tiled=True),
-        lax.all_gather(value_weight, ("dp", "ctx"), axis=0, tiled=True),
-        lax.all_gather(w_out, ("dp", "ctx"), axis=0, tiled=True),
-        lax.all_gather(w_router, ("dp", "ctx"), axis=0, tiled=True),
-        lax.all_gather(gain_ffn, ("dp", "ctx"), axis=0, tiled=True),
+        gain_one, query_proj, key_proj, value_proj, out_proj, router_proj, gain_two
     )
     gate_back, up_back, down_back = (
         lax.all_gather(w_gate, "dp", axis=1, tiled=True),
@@ -424,14 +775,29 @@
     grad_value_full = contract_rows(normed, grad_values)
     grad_residual, grad_gain_one = norm_backward(grad_normed, residual, inverse_one, scale_one)
     grad_input = (grad_residual + grad_hidden_one).astype(jnp.bfloat16)
+    low = jnp.bfloat16
+    grads = jnp.concatenate(
+        [
+            grad_query_full.astype(low),
+            grad_key_full.astype(low),
+            grad_value_full.astype(low),
+            grad_out_full.astype(low),
+            grad_router_full.astype(low),
+            grad_gain_one.astype(low)[:, None],
+            grad_gain_two.astype(low)[:, None],
+            jnp.zeros((width, PACK - 4114), low),
+        ],
+        axis=1,
+    )
+    share = scatter_sum(grads).astype(jnp.float32)
     shares = (
-        lax.psum_scatter(grad_gain_one, ("dp", "ctx"), scatter_dimension=0, tiled=True),
-        lax.psum_scatter(grad_query_full, ("dp", "ctx"), scatter_dimension=0, tiled=True),
-        lax.psum_scatter(grad_key_full, ("dp", "ctx"), scatter_dimension=0, tiled=True),
-        lax.psum_scatter(grad_value_full, ("dp", "ctx"), scatter_dimension=0, tiled=True),
-        lax.psum_scatter(grad_out_full, ("dp", "ctx"), scatter_dimension=0, tiled=True),
-        lax.psum_scatter(grad_router_full, ("dp", "ctx"), scatter_dimension=0, tiled=True),
-        lax.psum_scatter(grad_gain_two, ("dp", "ctx"), scatter_dimension=0, tiled=True),
+        share[:, 4112],
+        share[:, :1536],
+        share[:, 1536:2048],
+        share[:, 2048:2560],
+        share[:, 2560:4096],
+        share[:, 4096:4112],
+        share[:, 4113],
     )
     return (
         mixed,

time: 2800 us -> 1000 us (0.36)
  blocking collectives: 758 us -> 0 us
  starting transfers between devices: 558 us -> 22.3 us
  waiting for transfers between devices: 863 us -> 360 us
  Pallas kernels: 0 us -> 131 us
  local copies, waits for them, and re-layouts: 247 us -> 134 us
    all_gather x4 -> x0, waiting for transfers between devices: 615 us -> none  [the longest x1 191 us: shards(): lax.all_gather(key_weight, ('dp', 'ctx'), axis=0, tiled=True)]
    unnamed x3 -> x0, blocking collectives: 553 us -> none
    unnamed x162 -> x2, starting transfers between devices: 536 us -> 0.08 us
    all_gather x1 -> x0, blocking collectives: 205 us -> none  [shards(): lax.all_gather(w_router, ('dp', 'ctx'), axis=0, tiled=True)]
    unnamed x460 -> x116, local copies, waits for them, and re-layouts: 203 us -> 55.8 us
    pallas_call x0 -> x2, Pallas kernels: none -> 131 us  [the longest x1 68.1 us: scatter_sum(): pl.pallas_call(scatter_kernel, out_shape=jax.ShapeDtypeStruct((16, PACK),...]
    all_gather x1, waiting for transfers between devices: 2.96 us -> 66.5 us  [shards(): lax.all_gather(w_down, 'dp', axis=1, tiled=True)]
    all_gather x1, waiting for transfers between devices: 0.01 us -> 32.1 us  [shards(): lax.all_gather(w_gate, 'dp', axis=1, tiled=True)]
  transfers between devices with their start and end apart: 178 -> 14, of which waited for: 29 -> 9; matrix products, arithmetic and copies ran while one was open for 28% -> 40% of each run, Pallas kernels for 0% -> 0%
where the time goes in v1:
time: 1000 us; the launch traced here: 995 us
  waiting for transfers between devices  360 us (36%)
  matrix products  292 us (29%)
  local copies, waits for them, and re-layouts  134 us (13%)
  Pallas kernels  131 us (13%)
  other arithmetic  37.6 us (4%)
  starting transfers between devices  22.3 us (2%)
  between operations  15.4 us (2%)
    unnamed x12, waiting for transfers between devices  112 us
    pallas_call x1, Pallas kernels, scatter_sum(): pl.pallas_call(scatter_kernel, out_shape=jax.ShapeDtypeStruct((16, PACK),...  68.1 us
    all_gather x1, waiting for transfers between devices, shards(): lax.all_gather(w_down, 'dp', axis=1, tiled=True)  66.5 us
    pallas_call x1, Pallas kernels, gather_weights(): pl.pallas_call(gather_kernel, out_shape=jax.ShapeDtypeStruct((4, 2, 2, 2,...  63.2 us
    dot_general x18, matrix products, block_scores(): jnp.einsum('qhgd,khd->hgqk', heads_of_queries, key_block, preferred_eleme...  60.7 us
    unnamed x116, local copies, waits for them, and re-layouts  55.8 us
    dot_general x12, matrix products, probs_and_grads(): jnp.einsum('qhgd,khd->hgqk', head_gradient, value_block, preferred_elemen...  42 us
    all_gather x1, waiting for transfers between devices, shards(): lax.all_gather(rows_of_keys, 'ctx', axis=0, tiled=True)  37.4 us
  transfers between devices with their start and end apart: 14, of which 9 were waited for; matrix products, arithmetic and copies ran while one was open for 40% of the time, Pallas kernels for 0%

profile of v1, /device:TPU:1, one launch (start us, length us, event | category | flops | bytes accessed | tf_op | source)
XLA Modules:
  0.0 994.9 jit_solution(1591147418356522315)
XLA Ops:
  12.4 63.2 %gather_weights.1 = bf16[4,2,2,2,48,4608]{5,4,3,2,1,0:T(8,128)(2,1)} custom-call(bf16[16,4608]{1,0:T(8,128)(2,1)} %pad.10.shard, bf16[48,64]{1,0:T(8,128)(2,1)} %and_convert_fusion.1.merge), custom_call_target="tpu_custom_call" | custom-call | bytes 29360128 | tf_op jit(solution)/shard_map/gather_weights/pallas_call | solution.py:334
  93.6 34.7 %all-gather.6.cloned.1.call-done = bf16[3072,512]{1,0:T(8,128)(2,1)} async-done(((bf16[192,512]{1,0:T(8,128)(2,1)}), bf16[3072,512]{1,0:T(8,128)(2,1)}) %all-gather.6.cloned.1.call-update) | async-done | bytes 3145744 | tf_op jit(solution)/shard_map/all_gather | solution.py:593
  128.3 8.9 reshape.577
  137.2 7.6 copy.153
  144.8 37.4 %all-gather.8.cloned.1.call-done = bf16[3072,512]{1,0:T(8,128)(2,1)} async-done(((bf16[192,512]{1,0:T(8,128)(2,1)}), bf16[3072,512]{1,0:T(8,128)(2,1)}) %all-gather.8.cloned.1.call-update) | async-done | bytes 3145744 | tf_op jit(solution)/shard_map/all_gather | solution.py:592
  182.3 8.9 reshape.578
  191.1 7.6 copy.154
  198.7 35.0 %while.50 = (s32[]{:T(128)}, f32[8,3,192,1]{2,1,0,3:T(4,128)S(1)}, f32[8,3,192,1]{2,1,0,3:T(4,128)S(1)}, s32[6,512]{1,0:T(8,128)S(1)}, s32[6,512]{1,0:T(8,128)S(...) while((s32[]{:T(128)}, f32[8,3,192,1]{2,1,0,3:T(4,128)S(1)}, ...), condition=%wide.region_4.5_spmd.clone, body=%wide.region_1.4_spmd.clone.sunk | while | flops 318823104 | bytes 20537740 | solution.py:85
  233.7 35.8 %while.51 = (s32[]{:T(128)}, f32[192,8,3,64]{0,3,2,1:T(8,128)S(1)}, bf16[6,512,8,64]{1,3,2,0:T(8,128)(2,1)}, s32[6,512]{1,0:T(8,128)S(1)}, s32[6,512]{1,0:T(8,12...) while((s32[]{:T(128)}, f32[192,8,3,64]{0,3,2,1:T(8,128)S(1)}, ...), condition=%wide.region_6.7_spmd.clone, body=%wide.region_5.6_spmd.clone.sunk | while | flops 614301888 | bytes 4229006 | solution.py:105
  233.9 5.7 bitcast_add_fusion.9
  239.8 5.7 bitcast_add_fusion.9
  245.7 5.7 bitcast_add_fusion.9
  251.6 5.7 bitcast_add_fusion.9
  257.5 5.7 bitcast_add_fusion.9
  263.4 5.7 bitcast_add_fusion.9
  296.8 27.2 %all-to-all-done = bf16[16,1,36,1536]{3,2,1,0:T(8,128)(2,1)} async-done(((bf16[16,1,36,1536]{3,2,1,0:T(8,128)(2,1)}), bf16[16,1,36,1536]{3,2,1,0:T(8,128)(2,1)}, u32[]{:S(2)}, u32[]{:S(2)}) %all-to-all-start) | async-done | bytes 1769504 | tf_op jit(solution)/shard_map/all_to_all | solution.py:635
  324.0 4.7 all-to-all-start.2
  328.8 6.2 fusion.87
  335.0 32.1 %all-gather.10.cloned.1.call-done = bf16[1,1536,1024]{2,1,0:T(8,128)(2,1)} async-done(((bf16[1,192,1024]{2,1,0:T(8,128)(2,1)}), bf16[1,1536,1024]{2,1,0:T(8,128)(2,1)}) %all-gather.10.cloned.1.call-update) | async-done | bytes 3145744 | tf_op jit(solution)/shard_map/all_gather | solution.py:573
  367.1 6.2 fusion.91
  373.2 66.5 %all-gather.14.cloned.1.call-done = bf16[1,1024,1536]{2,1,0:T(8,128)(2,1)} async-done(((bf16[1,128,1536]{2,1,0:T(8,128)(2,1)}), bf16[1,1024,1536]{2,1,0:T(8,128)(2,1)}) %all-gather.14.cloned.1.call-update) | async-done | bytes 3145744 | tf_op jit(solution)/shard_map/all_gather | solution.py:575
  439.7 8.3 fusion.103
  449.1 5.6 fusion.82
  454.8 5.8 fusion.81
  461.9 5.4 fusion.93
  467.3 7.8 all-to-all-start.1
  475.1 4.7 fusion.89
  483.4 27.2 %all-to-all-done.1 = bf16[16,1,36,1536]{3,2,1,0:T(8,128)(2,1)} async-done(((bf16[16,1,36,1536]{3,2,1,0:T(8,128)(2,1)}), bf16[16,1,36,1536]{3,2,1,0:T(8,128)(2,1)}, u32[]{:S(2)}, u32[]{:S(2)}) %all-to-all-start.1) | async-done | bytes 1769504 | tf_op jit(solution)/shard_map/all_to_all | solution.py:643
  510.6 4.8 all-to-all-start.3
  515.4 6.2 fusion.80
  530.3 23.5 %all-to-all-done.3 = bf16[16,1,36,1536]{3,2,1,0:T(8,128)(2,1)} async-done(((bf16[16,1,36,1536]{3,2,1,0:T(8,128)(2,1)}), bf16[16,1,36,1536]{3,2,1,0:T(8,128)(2,1)}, u32[]{:S(2)}, u32[]{:S(2)}) %all-to-all-start.3) | async-done | bytes 1769504 | tf_op jit(solution)/shard_map/all_to_all | solution.py:709
  569.4 49.0 %while.52 = (s32[]{:T(128)}, f32[8,3,192,1]{2,0,3,1:T(8,128)S(1)}, s32[6,512]{1,0:T(8,128)}, s32[6,512]{1,0:T(8,128)}, s32[192]{0:T(256)S(1)}, /*index=5*/bf16[6...) while((s32[]{:T(128)}, f32[8,3,192,1]{2,0,3,1:T(8,128)S(1)}, ...), condition=%wide.region_22.23_spmd.clone, body=%wide.region_20.22_spmd.clone.sunk | while | flops 616075968 | bytes 21406108 | solution.py:143
  572.8 4.7 fusion.249
  581.0 4.7 fusion.249
  589.2 4.7 fusion.249
  597.3 4.7 fusion.249
  605.5 4.7 fusion.249
  613.7 4.7 fusion.249
  618.4 95.1 %while.53 = (s32[]{:T(128)}, f32[192,8,3,64]{0,3,2,1:T(8,128)S(1)}, bf16[6,512,8,64]{1,3,2,0:T(8,128)(2,1)}, bf16[6,512,8,64]{1,3,2,0:T(8,128)(2,1)}, bf16[6,512...) while((s32[]{:T(128)}, f32[192,8,3,64]{0,3,2,1:T(8,128)S(1)}, ...), condition=%wide.region_24.25_spmd.clone, body=%wide.region_23.24_spmd.clone.sunk | while | flops 1534689536 | bytes 51220928 | solution.py:170
  713.5 8.0 copy.192
  721.5 9.3 reshape.573
  730.9 7.8 copy.193
  738.7 9.5 reshape.575
  759.8 5.1 fusion.76
  770.8 34.5 %reduce-scatter.16.cloned.1.call-done = bf16[192,512]{1,0:T(8,128)(2,1)} async-done(((bf16[3072,512]{1,0:T(8,128)(2,1)}), bf16[192,512]{1,0:T(8,128)(2,1)}) %reduce-scatter.16.cloned.1.call-update) | async-done | bytes 196624
  807.8 75.5 %reduce-scatter.18.cloned.1.call-done = bf16[192,512]{1,0:T(8,128)(2,1)} async-done(((bf16[3072,512]{1,0:T(8,128)(2,1)}), bf16[192,512]{1,0:T(8,128)(2,1)}) %reduce-scatter.18.cloned.1.call-update) | async-done | bytes 196624
  892.1 22.7 %concatenate.23.grads = bf16[4,2,2,2,48,4608]{5,4,3,2,1,0:T(8,128)(2,1)} concatenate(bf16[4,2,2,2,48,1536]{5,4,3,2,1,0:T(8,128)(2,1)} %bitcast.451, bf16[4,2,2,2,48,512]{5,4,3,2,1,0:T(8,128)(2,1)} %bitcast.474, bf16[4,2,2,2,48,512]{5,4,3,2,1,0:T(8,128)(2,1)} %bitcast.473, bf16[4,2,2,2,48,1536]{5,4,3,2,1,0:T(8,128)(2,1)} %bitcast.452, bf16[4,2,2,2,48,16]{5,4,3,2,1,0:T(8,128)(2,1)} %bitcast.472, ...), dimensions={5} | concatenate | bytes 28311552 | tf_op jit(solution)/shard_map/concatenate | solution.py:779
  914.8 68.1 %scatter_sum.1 = bf16[16,4608]{1,0:T(8,128)(2,1)} custom-call(bf16[4,2,2,2,48,4608]{5,4,3,2,1,0:T(8,128)(2,1)} %concatenate.23.grads, bf16[64,48]{1,0:T(8,128)(2,1)} %and_convert_fusion.split), custom_call_target="tpu_custom_call" | custom-call | bytes 29360128 | tf_op jit(solution)/shard_map/scatter_sum/pallas_call | solution.py:505
  (369 shorter events, 264.5 us)
Async XLA Ops:
  7.2 121.1 %all-gather.6.cloned.1.call-start = ((), (), s32[]{:S(2)}) async-start(), calls=%async_computation.9 | async-start | bytes 3342336 | tf_op jit(solution)/shard_map/all_gather | solution.py:593
  7.2 68.4 %copy-start.40 = (s32[48]{0:T(128)}, s32[48]{0:T(128)S(1)}, u32[]{:S(2)}) copy-start(s32[48]{0:T(128)S(1)} %get-tuple-element.749) | copy-start | bytes 580
  7.2 68.4 %copy-start.42 = (s32[48]{0:T(128)}, s32[48]{0:T(128)S(1)}, u32[]{:S(2)}) copy-start(s32[48]{0:T(128)S(1)} %get-tuple-element.750) | copy-start | bytes 580
  7.3 68.3 %copy-start.44 = (s32[64]{0:T(128)}, s32[64]{0:T(128)S(1)}, u32[]{:S(2)}) copy-start(s32[64]{0:T(128)S(1)} %get-tuple-element.747) | copy-start | bytes 772
  7.3 68.3 %copy-start.46 = (s32[64]{0:T(128)}, s32[64]{0:T(128)S(1)}, u32[]{:S(2)}) copy-start(s32[64]{0:T(128)S(1)} %get-tuple-element.748) | copy-start | bytes 772
  8.6 76.5 %copy-start.28 = (f32[192]{0:T(256)}, f32[192]{0:T(256)S(1)}, u32[]{:S(2)}) copy-start(f32[192]{0:T(256)S(1)} %add_rsqrt_fusion.1) | copy-start | bytes 2308
  12.4 64.9 %copy-start.2 = (bf16[192,1536]{1,0:T(8,128)(2,1)S(1)}, bf16[192,1536]{1,0:T(8,128)(2,1)}, u32[]{:S(2)}) copy-start(bf16[192,1536]{1,0:T(8,128)(2,1)} %param.22) | copy-start | bytes 1769476
  77.3 7.7 copy-start.15
  80.0 4.6 copy-start.25
  80.0 102.3 %all-gather.8.cloned.1.call-start = ((), (), s32[]{:S(2)}) async-start(), calls=%async_computation.10 | async-start | bytes 3342336 | tf_op jit(solution)/shard_map/all_gather | solution.py:592
  82.7 246.1 %all-gather.12.cloned.1.call-start = ((), (), s32[]{:S(2)}) async-start(), calls=%async_computation.12 | async-start | bytes 3538944 | tf_op jit(solution)/shard_map/all_gather | solution.py:574
  83.4 283.7 %all-gather.10.cloned.1.call-start = ((), (), s32[]{:S(2)}) async-start(), calls=%async_computation.11 | async-start | bytes 3538944 | tf_op jit(solution)/shard_map/all_gather | solution.py:573
  84.0 355.7 %all-gather.14.cloned.1.call-start = ((), (), s32[]{:S(2)}) async-start(), calls=%async_computation.13 | async-start | bytes 3538944 | tf_op jit(solution)/shard_map/all_gather | solution.py:575
  85.0 4.4 copy-start.36
  91.2 46.0 %copy-start.37 = (s32[192,2]{0,1:T(2,128)}, s32[192,2]{0,1:T(2,128)S(1)}, u32[]{:S(2)}) copy-start(s32[192,2]{0,1:T(2,128)S(1)} %multiply_add_fusion.2) | copy-start | bytes 4612
  272.3 4.5 copy-start.7
  272.3 4.7 copy-start.11
  276.9 11.2 %copy-start.4 = (bf16[192,1536]{1,0:T(8,128)(2,1)}, bf16[192,1536]{1,0:T(8,128)(2,1)S(1)}, u32[]{:S(2)}) copy-start(bf16[192,1536]{1,0:T(8,128)(2,1)S(1)} %multiply_convert_fusion.3) | copy-start | bytes 1769476
  282.3 4.6 copy-start.9
  282.3 41.7 %all-to-all-start = ((bf16[16,1,36,1536]{3,2,1,0:T(8,128)(2,1)}), bf16[16,1,36,1536]{3,2,1,0:T(8,128)(2,1)}, u32[]{:S(2)}, u32[]{:S(2)}) async-start(bf16[16,1,36,1536]{3,2,1,0:T(8,128)(2,1)} %bitcast.467), calls=%async_computation | async-start | bytes 3932160 | tf_op jit(solution)/shard_map/all_to_all | solution.py:635
  287.0 2.6 copy-start.38
  289.5 3.9 copy-start.30
  289.5 3.8 copy-start.32
  289.5 3.8 copy-start.39
  324.0 115.6 %all-to-all-start.2 = ((bf16[16,1,36,1536]{3,2,1,0:T(8,128)(2,1)}), bf16[16,1,36,1536]{3,2,1,0:T(8,128)(2,1)}, u32[]{:S(2)}, u32[]{:S(2)}) async-start(bf16[16,1,36,1536]{3,2,1,0:T(8,128)(2,1)} %bitcast.466), calls=%async_computation.2 | async-start | bytes 3932160 | tf_op jit(solution)/shard_map/all_to_all | solution.py:673
  328.7 436.2 %reduce-scatter.14.cloned.1.call-start = ((), (), s32[]{:S(2)}) async-start(), calls=%async_computation.16 | async-start | bytes 3538944 | tf_op jit(solution)/shard_map/reduce_scatter | solution.py:705
  448.0 6.8 copy-start.49
  454.7 312.2 %reduce-scatter.12.cloned.1.call-start = ((), (), s32[]{:S(2)}) async-start(), calls=%async_computation.15 | async-start | bytes 3538944 | tf_op jit(solution)/shard_map/reduce_scatter | solution.py:702
  467.3 43.3 %all-to-all-start.1 = ((bf16[16,1,36,1536]{3,2,1,0:T(8,128)(2,1)}), bf16[16,1,36,1536]{3,2,1,0:T(8,128)(2,1)}, u32[]{:S(2)}, u32[]{:S(2)}) async-start(bf16[16,1,36,1536]{3,2,1,0:T(8,128)(2,1)} %fusion.93), calls=%async_computation.1 | async-start | bytes 3932160 | tf_op jit(solution)/shard_map/all_to_all | solution.py:643
  475.1 4.8 copy-start.48
  475.1 4.8 copy-start.50
  510.6 43.2 %all-to-all-start.3 = ((bf16[16,1,36,1536]{3,2,1,0:T(8,128)(2,1)}), bf16[16,1,36,1536]{3,2,1,0:T(8,128)(2,1)}, u32[]{:S(2)}, u32[]{:S(2)}) async-start(bf16[16,1,36,1536]{3,2,1,0:T(8,128)(2,1)} %fusion.96), calls=%async_computation.3 | async-start | bytes 3932160 | tf_op jit(solution)/shard_map/all_to_all | solution.py:709
  515.4 253.5 %reduce-scatter.10.cloned.1.call-start = ((), (), s32[]{:S(2)}) async-start(), calls=%async_computation.14 | async-start | bytes 3538944 | tf_op jit(solution)/shard_map/reduce_scatter | solution.py:699
  521.6 283.7 %reduce-scatter.16.cloned.1.call-start = ((), (), s32[]{:S(2)}) async-start(), calls=%async_computation.17 | async-start | bytes 3342336
  525.5 4.2 copy-start.31
  525.5 4.2 copy-start.33
  525.5 4.3 copy-start.27
  563.7 5.7 copy-start.14
  563.7 5.7 copy-start.24
  730.9 152.4 %reduce-scatter.18.cloned.1.call-start = ((), (), s32[]{:S(2)}) async-start(), calls=%async_computation.18 | async-start | bytes 3342336
  748.9 3.5 copy-start.3
  748.9 3.5 copy-start.16
  748.9 3.5 copy-start.29
  752.4 3.7 copy-start.1
  752.5 3.7 copy-start.8
  883.3 4.8 copy-start.20
  886.6 3.4 copy-start.19
  914.8 71.6 %copy-start.6 = (f32[192,1536]{1,0:T(8,128)S(1)}, f32[192,1536]{1,0:T(8,128)}, u32[]{:S(2)}) copy-start(f32[192,1536]{1,0:T(8,128)} %get-tuple-element.746) | copy-start | bytes 3538948
  (19 other events, 27.3 us)
Sparse Core Ops, SparseCore 0:
  80.1 48.1 all-gather.5
  131.3 50.9 all-gather.7
  183.9 68.2 all-gather.11
  253.7 113.2 all-gather.9
  368.5 71.0 all-gather.13
  454.8 113.0 reduce-scatter.13
  570.4 71.5 reduce-scatter.11
  644.4 71.5 reduce-scatter.9
  731.0 74.2 reduce-scatter.15
  809.2 74.0 reduce-scatter.17

commit v2 on v1

v2 whole, which is shorter than its diff:
```python
import functools

import jax
import jax.numpy as jnp
from jax import lax
from jax.experimental import pallas as pl
from jax.experimental.pallas import tpu as pltpu
from jax.sharding import PartitionSpec as P

QUERY_HEAD_COUNT = 24
KEY_VALUE_HEADS = 8
HEAD_SIZE = 64
TOP = 2

EPSILON = 1e-06
NEGATIVE = -1e30
MESH = pl.DeviceIdType.MESH

PACK = 4608
HALF = PACK // 2
QUARTER = PACK // 4
RING_ORDERS = (("y", "z", "x"), ("y", "z", "x"), ("y", "x", "z"))


def place():
    dp = lax.axis_index("dp")
    ctx = lax.axis_index("ctx")
    return {"y": dp // 2, "z": (ctx // 8) * 2 + dp % 2, "x": (ctx // 2) % 4, "core": ctx % 2}


def device_of(spot):
    z = spot["z"]
    return (spot["y"] * 2 + z % 2, (z // 2) * 8 + spot["x"] * 2 + spot["core"])


def moved(spot, axis, step):
    other = dict(spot)
    if axis == "core":
        other["core"] = 1 - spot["core"]
    else:
        other[axis] = (spot[axis] + step) % 4
    return other


def member(spot, step):
    index = (spot["x"] % 2) * 2 + spot["core"]
    target = (index // 2 + step // 2) % 2 * 2 + (index % 2 + step % 2) % 2
    other = dict(spot)
    other["x"] = (spot["x"] // 2) * 2 + target // 2
    other["core"] = target % 2
    return other, target


def partner(spot):
    other = dict(spot)
    other["z"] = spot["z"] // 2 * 2 + (spot["z"] + 1) % 2
    other["core"] = (spot["core"] + 1) % 2
    return other


def meet(spot):
    barrier = pltpu.get_barrier_semaphore()
    others = [member(spot, step)[0] for step in (1, 2, 3)] + [partner(spot)]
    others += [moved(spot, axis, step) for axis in "xyz" for step in (1, 2, 3)]
    for other in others:
        pl.semaphore_signal(barrier, inc=1, device_id=device_of(other), device_id_type=MESH)
    pl.semaphore_wait(barrier, len(others))


def region(spot, known, part, base):
    def pick(axis, value, size):
        return pl.ds(0, size) if axis in known else pl.ds(value, 1)

    z = spot["z"]
    if "x" in known:
        columns = pl.ds(base, HALF)
    else:
        columns = pl.ds(pl.multiple_of(base + (spot["x"] % 2) * QUARTER, 128), QUARTER)
    return (
        pick("y", spot["y"], 4),
        pick("z", z % 2, 2),
        pick("z", z // 2, 2),
        pick("x", spot["x"] // 2, 2),
        pl.ds(part * 16, 16),
        columns,
    )


def expert_rows(ref, spot, core, half=None):
    rows = ref.shape[0] // 8
    first = (spot["y"] * 2 + core) * rows
    if half is not None:
        rows //= 2
        first += half * rows
    return ref.at[pl.ds(pl.multiple_of(first, 32), rows)]


def half_region(where, axis, half):
    if axis == "y":
        return where[:3] + (pl.ds(half, 1),) + where[4:]
    return (pl.ds(2 * half, 2),) + where[1:]


def relay(ring, numbers, send, recv, whole, half):
    spot, axis = ring

    def copy(ref, step, number):
        return pltpu.make_async_remote_copy(
            src_ref=ref,
            dst_ref=ref,
            send_sem=send.at[numbers + number],
            recv_sem=recv.at[numbers + number],
            device_id=device_of(moved(spot, axis, step)),
            device_id_type=MESH,
        )

    first = [copy(whole(spot), 1, 0), copy(whole(spot), 3, 1)]
    second = [copy(half(moved(spot, axis, 3), 0), 1, 2), copy(half(moved(spot, axis, 1), 1), 3, 3)]
    return first, second


def gather_kernel(
    shard, merge, own_gate, own_up, own_down, out, gate_out, up_out, down_out, pieces, joined,
    send0, recv0, send, recv, send_core, recv_core, local,
    swap_send, swap_recv, swap_local, line_send, line_recv, mate_send, mate_recv, ring_send, ring_recv,
):
    spot = place()
    meet(spot)
    mate = moved(spot, "core", 1)
    stays = spot["core"] == spot["z"] % 2
    experts = ((own_gate, gate_out), (own_up, up_out), (own_down, down_out))

    def swaps():
        return [
            pltpu.make_async_remote_copy(
                src_ref=own,
                dst_ref=expert_rows(whole, spot, spot["z"] % 2),
                send_sem=swap_send.at[n],
                recv_sem=swap_recv.at[n],
                device_id=device_of(partner(spot)),
                device_id_type=MESH,
            )
            for n, (own, whole) in enumerate(experts)
        ]

    def stays_here():
        return [
            pltpu.make_async_copy(own, expert_rows(whole, spot, spot["core"]), swap_local.at[n])
            for n, (own, whole) in enumerate(experts)
        ]

    def line(n):
        whole = experts[n][1]
        return relay(
            (spot, "y"),
            4 * n,
            line_send,
            line_recv,
            lambda at: expert_rows(whole, at, spot["core"]),
            lambda at, half: expert_rows(whole, at, spot["core"], half),
        )

    def to_mates(step):
        source = moved(spot, "y", 4 - step)
        return [
            pltpu.make_async_remote_copy(
                src_ref=expert_rows(whole, source, spot["core"]),
                dst_ref=expert_rows(whole, source, spot["core"]),
                send_sem=mate_send.at[3 * step + n],
                recv_sem=mate_recv.at[3 * step + n],
                device_id=device_of(mate),
                device_id_type=MESH,
            )
            for n, (own, whole) in enumerate(experts)
        ]

    def start_all(copies):
        for copy in copies:
            copy.start()

    @pl.when(stays)
    def _():
        start_all(stays_here())

    @pl.when(jnp.logical_not(stays))
    def _():
        start_all(swaps())

    index = (spot["x"] % 2) * 2 + spot["core"]
    quarter = spot["core"] * 2 + spot["x"] % 2
    copies = []
    for step in (1, 2, 3):
        other, target = member(spot, step)
        goal = other["core"] * 2 + other["x"] % 2
        copy = pltpu.make_async_remote_copy(
            src_ref=shard.at[:, pl.ds(pl.multiple_of(goal * QUARTER, 128), QUARTER)],
            dst_ref=pieces.at[index],
            send_sem=send0.at[step - 1],
            recv_sem=recv0.at[step - 1],
            device_id=device_of(other),
            device_id_type=MESH,
        )
        copy.start()
        copies.append(copy)
    pieces[index] = shard[:, pl.ds(pl.multiple_of(quarter * QUARTER, 128), QUARTER)]
    for copy in copies:
        copy.wait()
    joined[...] = jnp.dot(
        merge[...], pieces[...].reshape(64, QUARTER), preferred_element_type=jnp.float32
    ).astype(jnp.bfloat16)
    base = pl.multiple_of(spot["core"] * HALF, 128)
    mine = region(spot, "", 0, base)
    own = pltpu.make_async_copy(
        joined,
        out.at[spot["y"], spot["z"] % 2, spot["z"] // 2, spot["x"] // 2, :, mine[5]],
        local,
    )
    own.start()
    own.wait()
    core_copies = []

    def to_mate(number, where):
        copy = pltpu.make_async_remote_copy(
            src_ref=out.at[where],
            dst_ref=out.at[where],
            send_sem=send_core.at[number],
            recv_sem=recv_core.at[number],
            device_id=device_of(mate),
            device_id_type=MESH,
        )
        copy.start()
        core_copies.append(copy)

    flights, relays, finals = {}, [], []
    for stage in range(3):
        for part, order in enumerate(RING_ORDERS):
            axis, known = order[stage], order[:stage]
            if stage > 0:
                for copy in flights[part]:
                    copy.wait_recv()
            where = region(spot, known, part, base)
            if stage == 2:
                ring = relay(
                    (spot, axis),
                    4 * part,
                    ring_send,
                    ring_recv,
                    lambda at, known=known, part=part: out.at[region(at, known, part, base)],
                    lambda at, half, known=known, part=part, axis=axis: out.at[
                        half_region(region(at, known, part, base), axis, half)
                    ],
                )
                start_all(ring[0])
                relays.append(ring)
                finals.append((axis, known))
                to_mate(part * 4, where)
                continue
            started = []
            for step in (1, 3, 2):
                number = (stage * 3 + part) * 3 + step - 1
                copy = pltpu.make_async_remote_copy(
                    src_ref=out.at[where],
                    dst_ref=out.at[where],
                    send_sem=send.at[number],
                    recv_sem=recv.at[number],
                    device_id=device_of(moved(spot, axis, step)),
                    device_id_type=MESH,
                )
                copy.start()
                started.append(copy)
            flights[part] = started
            copies += started
        if stage == 1:

            @pl.when(stays)
            def _():
                for copy in stays_here():
                    copy.wait()

            @pl.when(jnp.logical_not(stays))
            def _():
                for copy in swaps():
                    copy.wait()

            lines = [line(n) for n in range(3)]
            for first, _ in lines:
                start_all(first)
            own_mates = to_mates(0)
            start_all(own_mates)

    mates = {step: to_mates(step) for step in (1, 3, 2)}
    for first, second in lines + relays:
        for number in range(2):
            first[number].wait_recv()
            second[number].start()
    for part, (axis, _) in enumerate(finals):
        for step in (1, 3):
            to_mate(part * 4 + step, region(moved(spot, axis, 4 - step), RING_ORDERS[part][:2], part, base))
    for n in range(3):
        mates[1][n].start()
        mates[3][n].start()
    for n, (_, second) in enumerate(lines):
        for copy in second:
            copy.wait_recv()
        mates[2][n].start()
    for part, (_, second) in enumerate(relays):
        for copy in second:
            copy.wait_recv()
        axis = RING_ORDERS[part][2]
        to_mate(part * 4 + 2, region(moved(spot, axis, 2), RING_ORDERS[part][:2], part, base))
    line_copies = [copy for first, second in lines + relays for copy in first + second]
    for copy in copies[3:] + line_copies:
        copy.wait_send()
    for copy in core_copies:
        copy.wait()
    for copy in own_mates + mates[1] + mates[2] + mates[3]:
        copy.wait()


def gather_weights(shard, gate, up, down):
    shard = jnp.pad(shard, ((0, 4), (0, 0)))
    target = jnp.arange(48, dtype=jnp.int32)[:, None]
    source = jnp.arange(64, dtype=jnp.int32)[None, :]
    merge = ((target // 12 == source // 16) & (target % 12 == source % 16)).astype(jnp.bfloat16)
    vmem = pl.BlockSpec(memory_space=pltpu.VMEM)
    anywhere = pl.BlockSpec(memory_space=pl.ANY)
    experts = [
        jax.ShapeDtypeStruct((8 * part.shape[0], part.shape[1]), jnp.bfloat16)
        for part in (gate, up, down)
    ]
    dma = pltpu.SemaphoreType.DMA
    packed, *experts = pl.pallas_call(
        gather_kernel,
        out_shape=[jax.ShapeDtypeStruct((4, 2, 2, 2, 48, PACK), jnp.bfloat16)] + experts,
        in_specs=[vmem] * 2 + [anywhere] * 3,
        out_specs=[anywhere] * 4,
        scratch_shapes=[
            pltpu.VMEM((4, 16, QUARTER), jnp.bfloat16),
            pltpu.VMEM((48, QUARTER), jnp.bfloat16),
            dma((3,)), dma((3,)), dma((18,)), dma((18,)), dma((12,)), dma((12,)), dma,
            dma((3,)), dma((3,)), dma((3,)), dma((12,)), dma((12,)), dma((12,)), dma((12,)),
            dma((12,)), dma((12,)),
        ],
        compiler_params=pltpu.CompilerParams(collective_id=1, has_side_effects=True),
        cost_estimate=pl.CostEstimate(flops=0, bytes_accessed=40 * 2**20, transcendentals=0),
        name="gather_weights",
    )(shard, merge, gate, up, down)
    return packed.reshape(1536, PACK), experts


def scatter_kernel(
    normed, grad_qkv, branch, attended, rest, split, grad_gate, grad_up, grad_down,
    out, gate_out, up_out, down_out,
    grads, total, from_mate, done, packed,
    send_core, recv_core, send, recv, send0, recv0,
    mate_send, mate_recv, own_sem, line_send, line_recv, swap_send, swap_recv,
    *buffers,
):
    spot = place()
    landing = (buffers[:3], buffers[3:6], buffers[6:9])
    held, mates, lines, results, arrived = (buffers[9 + 3 * n : 12 + 3 * n] for n in range(5))
    wholes, finals = (grad_gate, grad_up, grad_down), (gate_out, up_out, down_out)
    mate = moved(spot, "core", 1)
    own_copies, mate_copies = [], []
    for n, whole in enumerate(wholes):
        for y in range(4):
            rows = whole.shape[0] // 8

            def part(core, whole=whole, y=y, rows=rows):
                return whole.at[pl.ds(pl.multiple_of((2 * y + core) * rows, 64), rows)]

            own = pltpu.make_async_copy(part(spot["core"]), held[n].at[y], own_sem.at[4 * n + y])
            own.start()
            own_copies.append(own)
            mate_copies.append(
                pltpu.make_async_remote_copy(
                    src_ref=part(mate["core"]),
                    dst_ref=mates[n].at[y],
                    send_sem=mate_send.at[4 * n + y],
                    recv_sem=mate_recv.at[4 * n + y],
                    device_id=device_of(mate),
                    device_id_type=MESH,
                )
            )
    meet(spot)
    for copy in mate_copies:
        copy.start()

    base = pl.multiple_of(spot["core"] * HALF, 128)
    mate_base = pl.multiple_of(mate["core"] * HALF, 128)
    tile = 256
    grads_shape = (4, 2, 2, 2, 48, tile)

    def fill(turned, right, first):
        @pl.loop(0, right.shape[1] // tile)
        def _(n):
            at = pl.ds(pl.multiple_of(n * tile, tile), tile)
            to = pl.ds(pl.multiple_of(first + n * tile, tile), tile)
            grads[:, :, :, :, :, to] = (
                jnp.dot(turned, right[:, at], preferred_element_type=jnp.float32)
                .astype(jnp.bfloat16)
                .reshape(grads_shape)
            )

    fill(normed[...].T, grad_qkv, 0)
    fill(branch[...].T, attended, grad_qkv.shape[1])
    at = grad_qkv.shape[1] + attended.shape[1]
    grads[:, :, :, :, :, at:] = rest[...].reshape(4, 2, 2, 2, 48, PACK - at)
    core_copies = []
    for part in range(3):
        rows = pl.ds(part * 16, 16)
        copy = pltpu.make_async_remote_copy(
            src_ref=grads.at[:, :, :, :, rows, pl.ds(mate_base, HALF)],
            dst_ref=from_mate.at[:, :, :, :, rows, :],
            send_sem=send_core.at[part],
            recv_sem=recv_core.at[part],
            device_id=device_of(mate),
            device_id_type=MESH,
        )
        copy.start()
        core_copies.append(copy)
    all_copies = core_copies + mate_copies

    line_copies = []
    for n in range(3):
        for copy in mate_copies[4 * n : 4 * n + 4]:
            copy.wait_recv()
        for copy in own_copies[4 * n : 4 * n + 4]:
            copy.wait()

        @pl.loop(0, 4)
        def _(y, n=n):
            held[n][y] = (
                held[n][y].astype(jnp.float32) + mates[n][y].astype(jnp.float32)
            ).astype(jnp.bfloat16)

        for step in (1, 3, 2):
            other = moved(spot, "y", step)
            copy = pltpu.make_async_remote_copy(
                src_ref=held[n].at[other["y"]],
                dst_ref=lines[n].at[step - 1],
                send_sem=line_send.at[3 * n + step - 1],
                recv_sem=line_recv.at[3 * n + step - 1],
                device_id=device_of(other),
                device_id_type=MESH,
            )
            copy.start()
            line_copies.append(copy)
    all_copies += line_copies

    pending = []
    for part, order in enumerate(RING_ORDERS):
        rows = pl.ds(part * 16, 16)
        core_copies[part].wait_recv()

        @pl.loop(0, 32)
        def _(block):
            at = (block // 8, (block // 4) % 2, (block // 2) % 2, block % 2, rows)
            total[at] = (
                grads[at + (pl.ds(base, HALF),)].astype(jnp.float32)
                + from_mate[at].astype(jnp.float32)
            ).astype(jnp.bfloat16)

        pending.append(start_ring(spot, part, 0, total, landing, send, recv, all_copies))
    for stage in range(3):
        if stage == 2:
            sum_lines(spot, held, lines, line_copies, results)
            swap_results(spot, results, arrived, swap_send, swap_recv, True)
        for part, order in enumerate(RING_ORDERS):
            known = order[: 2 - stage]
            for copy in pending[part]:
                copy.wait_recv()
            where = region(spot, known, part, 0)
            add_ring(spot, known, part, total, landing[stage][part], where)
            if stage < 2:
                pending[part] = start_ring(spot, part, stage + 1, total, landing, send, recv, all_copies)
    index = (spot["x"] % 2) * 2 + spot["core"]
    quarter = spot["core"] * 2 + spot["x"] % 2
    mine = region(spot, "", 0, 0)
    done[...] = total[spot["y"], spot["z"] % 2, spot["z"] // 2, spot["x"] // 2, :, mine[5]]
    packed[...] = (
        jnp.dot(split[...], done[...], preferred_element_type=jnp.float32)
        .astype(jnp.bfloat16)
        .reshape(4, 16, QUARTER)
    )
    columns = pl.ds(pl.multiple_of(quarter * QUARTER, 128), QUARTER)
    copies = []
    for step in (1, 2, 3):
        other, target = member(spot, step)
        copy = pltpu.make_async_remote_copy(
            src_ref=packed.at[target],
            dst_ref=out.at[:, columns],
            send_sem=send0.at[step - 1],
            recv_sem=recv0.at[step - 1],
            device_id=device_of(other),
            device_id_type=MESH,
        )
        copy.start()
        copies.append(copy)
    out[:, columns] = packed[index]
    swap_results(spot, results, arrived, swap_send, swap_recv, False)
    stays = spot["core"] == spot["z"] % 2

    @pl.when(stays)
    def _():
        for result, final in zip(results, finals):
            final[...] = result[...].astype(jnp.float32)

    @pl.when(jnp.logical_not(stays))
    def _():
        for result, final in zip(arrived, finals):
            final[...] = result[...].astype(jnp.float32)

    for copy in copies:
        copy.wait()
    for copy in all_copies:
        copy.wait_send()


def sum_lines(spot, held, lines, line_copies, results):
    for copy in line_copies:
        copy.wait_recv()
    for mine, line, result in zip(held, lines, results):
        total = mine[spot["y"]].astype(jnp.float32)
        for step in range(3):
            total += line[step].astype(jnp.float32)
        result[...] = total.astype(jnp.bfloat16)


def swap_results(spot, results, arrived, send, recv, start):
    @pl.when(spot["core"] != spot["z"] % 2)
    def _():
        for n, (result, place_in) in enumerate(zip(results, arrived)):
            copy = pltpu.make_async_remote_copy(
                src_ref=result,
                dst_ref=place_in,
                send_sem=send.at[n],
                recv_sem=recv.at[n],
                device_id=device_of(partner(spot)),
                device_id_type=MESH,
            )
            if start:
                copy.start()
            else:
                copy.wait()


def start_ring(spot, part, stage, total, landing, send, recv, all_copies):
    order = RING_ORDERS[part]
    axis, known = order[2 - stage], order[: 2 - stage]
    started = []
    for step in (1, 3, 2):
        other = moved(spot, axis, step)
        number = (stage * 3 + part) * 3 + step - 1
        copy = pltpu.make_async_remote_copy(
            src_ref=total.at[region(other, known, part, 0)],
            dst_ref=landing[stage][part].at[step - 1],
            send_sem=send.at[number],
            recv_sem=recv.at[number],
            device_id=device_of(other),
            device_id_type=MESH,
        )
        copy.start()
        started.append(copy)
    all_copies += started
    return started


def landing_shape(known):
    return (
        4 if "y" in known else 1,
        2 if "z" in known else 1,
        2 if "z" in known else 1,
        2 if "x" in known else 1,
        16,
        HALF if "x" in known else QUARTER,
    )


def add_ring(spot, known, part, total, landing, where):
    shape = landing_shape(known)
    count = shape[0] * shape[1] * shape[2] * shape[3]

    def body(block):
        a, b, c, d = (
            block // (shape[1] * shape[2] * shape[3]),
            (block // (shape[2] * shape[3])) % shape[1],
            (block // shape[3]) % shape[2],
            block % shape[3],
        )
        at = (
            a + (0 if "y" in known else spot["y"]),
            b + (0 if "z" in known else spot["z"] % 2),
            c + (0 if "z" in known else spot["z"] // 2),
            d + (0 if "x" in known else spot["x"] // 2),
            pl.ds(part * 16, 16),
            where[5],
        )
        summed = total[at].astype(jnp.float32)
        for step in range(3):
            summed += landing[step, a, b, c, d].astype(jnp.float32)
        total[at] = summed.astype(jnp.bfloat16)

    if count == 1:
        body(0)
    else:
        pl.loop(0, count)(body)


def scatter_sum(normed, grad_qkv, branch, attended, rest, expert_grads):
    source = jnp.arange(48, dtype=jnp.int32)[None, :]
    target = jnp.arange(64, dtype=jnp.int32)[:, None]
    split = ((source // 12 == target // 16) & (source % 12 == target % 16)).astype(jnp.bfloat16)
    low = jnp.bfloat16
    landings = [
        pltpu.VMEM((3,) + landing_shape(order[: 2 - stage]), low)
        for stage in range(3)
        for order in RING_ORDERS
    ]
    blocks = [(part.shape[0] // 8, part.shape[1]) for part in expert_grads]
    landings += [pltpu.VMEM((4,) + block, low) for block in blocks] * 2
    landings += [pltpu.VMEM((3,) + block, low) for block in blocks]
    landings += [pltpu.VMEM(block, low) for block in blocks] * 2
    vmem = pl.BlockSpec(memory_space=pltpu.VMEM)
    anywhere = pl.BlockSpec(memory_space=pl.ANY)
    dma = pltpu.SemaphoreType.DMA
    out, *finals = pl.pallas_call(
        scatter_kernel,
        out_shape=[jax.ShapeDtypeStruct((16, PACK), low)]
        + [jax.ShapeDtypeStruct(block, jnp.float32) for block in blocks],
        in_specs=[vmem] * 6 + [anywhere] * 3,
        out_specs=[vmem] * 4,
        scratch_shapes=[
            pltpu.VMEM((4, 2, 2, 2, 48, PACK), low),
            pltpu.VMEM((4, 2, 2, 2, 48, HALF), low),
            pltpu.VMEM((4, 2, 2, 2, 48, HALF), low),
            pltpu.VMEM((48, QUARTER), low),
            pltpu.VMEM((4, 16, QUARTER), low),
            dma((3,)), dma((3,)), dma((27,)), dma((27,)), dma((3,)), dma((3,)),
            dma((12,)), dma((12,)), dma((12,)), dma((9,)), dma((9,)), dma((3,)), dma((3,)),
        ]
        + landings,
        compiler_params=pltpu.CompilerParams(
            collective_id=2, has_side_effects=True, vmem_limit_bytes=62 * 2**20
        ),
        cost_estimate=pl.CostEstimate(
            flops=2 * 192 * 1536 * 4096, bytes_accessed=28 * 2**20, transcendentals=0
        ),
        name="scatter_sum",
    )(normed, grad_qkv, branch, attended, rest, split, *expert_grads)
    return out[:12], finals


def inverse_rms(values):
    return lax.rsqrt(jnp.mean(values * values, axis=-1, keepdims=True) + EPSILON)


def norm_backward(grad_normed, values, inverse, gain):
    unit_rows = values * inverse
    grad_unit = grad_normed * gain
    grad_values = inverse * (
        grad_unit - unit_rows * jnp.mean(grad_unit * unit_rows, axis=-1, keepdims=True)
    )
    return (grad_values, jnp.sum(grad_normed * unit_rows, axis=0))


def contract_rows(left, right):
    return lax.dot_general(
        left, right, (((0,), (0,)), ((), ())), preferred_element_type=jnp.float32
    )


def contract_cols(left, right):
    return lax.dot_general(
        left, right, (((1,), (1,)), ((), ())), preferred_element_type=jnp.float32
    )


MAIN_ROWS = 32
REST_ROWS = 16
REST_WIDTH = 384
CAPACITY = 36
SOURCES = 16
TILE = 256


def across(left, right):
    return lax.dot_general(
        left, right, (((1,), (1,)), ((), ())), preferred_element_type=jnp.float32
    )


def dot32(left, right):
    return jnp.dot(left, right, preferred_element_type=jnp.float32)


def in_three(column, lanes):
    first = column.astype(jnp.bfloat16).astype(jnp.float32)
    second = (column - first).astype(jnp.bfloat16).astype(jnp.float32)
    third = column - first - second
    return jnp.where(lanes % 3 == 0, first, jnp.where(lanes % 3 == 1, second, third))


def dispatch_tables(routes):
    rows = routes.shape[0]
    low = jnp.bfloat16
    experts = jnp.arange(SOURCES, dtype=jnp.int32)
    picked = (routes.reshape(-1)[:, None] == experts[None, :]).astype(jnp.float32)
    earlier = jnp.cumsum(picked, axis=0) - 1.0
    slots = jnp.sum(picked * earlier, axis=-1).astype(jnp.int32).reshape(rows, TOP).T[:, :, None]
    chosen = routes.T[:, :, None]
    main = jnp.arange(SOURCES * MAIN_ROWS, dtype=jnp.int32)[None, None, :]
    place_main = ((chosen == main // MAIN_ROWS) & (slots == main % MAIN_ROWS)).astype(low)
    rest = jnp.arange(SOURCES * REST_ROWS, dtype=jnp.int32)[None, None, None, :]
    quarter = jnp.arange(4, dtype=jnp.int32)[None, :, None, None]
    place_rest = (
        (chosen[:, None] == rest // REST_ROWS)
        & ((rest // 4) % 4 == quarter)
        & (slots[:, None] == MAIN_ROWS + rest % 4)
    ).astype(low)
    place_gate = (
        (chosen == rest[0] // REST_ROWS) & (slots % REST_ROWS == rest[0] % REST_ROWS)
    ).astype(low)
    lanes = jnp.arange(128, dtype=jnp.int32)[None, None, :]
    gate_lanes = (lanes // 3 == slots // REST_ROWS).astype(jnp.float32)
    return place_main, place_rest, place_gate, gate_lanes


def unpack_tables():
    low = jnp.bfloat16
    row = jnp.arange(4 * CAPACITY, dtype=jnp.int32)[:, None]
    device, slot = row // CAPACITY, row % CAPACITY
    main = jnp.arange(4 * MAIN_ROWS, dtype=jnp.int32)[None, :]
    from_main = ((device == main // MAIN_ROWS) & (slot == main % MAIN_ROWS)).astype(low)
    rest = jnp.arange(4 * REST_ROWS, dtype=jnp.int32)[None, :]
    from_rest = jnp.stack(
        [
            (
                (device == rest // REST_ROWS)
                & ((rest // 4) % 4 == quarter)
                & (slot == MAIN_ROWS + rest % 4)
            ).astype(low)
            for quarter in range(4)
        ]
    )
    from_gate = ((device == rest // REST_ROWS) & (slot % REST_ROWS == rest % REST_ROWS)).astype(low)
    lanes = jnp.arange(128, dtype=jnp.int32)[None, :]
    lane_mask = (lanes // 3 == slot // REST_ROWS).astype(jnp.float32)
    return (
        from_main, from_main.T, from_rest, from_rest.transpose(0, 2, 1), from_gate, from_gate.T,
        lane_mask,
    )


def experts_kernel(
    normed, cotangent, gates, place_main, place_rest, place_gate, gate_lanes,
    place_main_t, place_rest_t, place_gate_t,
    from_main, to_main, from_rest, to_rest, from_gate, to_gate, lane_mask,
    *rest_refs,
):
    weight_parts, rest_refs = rest_refs[:WEIGHT_PARTS], rest_refs[WEIGHT_PARTS:]
    grad_outs, rest_refs = rest_refs[3:6], rest_refs[:3] + rest_refs[6:]
    (
        grad_normed, mixture, grad_gates, gate_w, up_w, down_w,
        x_main, x_rest, c_main, c_rest, x_main_in, x_rest_in, c_main_in, c_rest_in,
        d_main, d_rest, d_main_in, d_rest_in, y_main, y_rest, y_main_in, y_rest_in,
        rows_x, rows_c, gate_pre, up_pre, hidden, grad_gate_pre, grad_up_pre, rows_d, rows_y,
        turned,
        weight_sem, out_sem, send, recv,
    ) = rest_refs
    low, wide = jnp.bfloat16, jnp.float32
    dp, ctx = lax.axis_index("dp"), lax.axis_index("ctx")
    loads = [
        pltpu.make_async_copy(part, whole, weight_sem.at[n])
        for n, (part, whole) in enumerate(zip(weight_parts, (gate_w, up_w, down_w)))
    ]
    for load in loads:
        load.start()
    y, z_lo, core = dp // 2, dp % 2, ctx % 2
    expert = ctx // 2 * 2 + z_lo
    at_home = z_lo == core

    def holder(step):
        other = (ctx + step) % SOURCES
        return other, (2 * y + other % 2, other // 2 * 2 + z_lo)

    def sender(step):
        other = (expert + step) % SOURCES
        return other, (2 * y + core, other)

    barrier = pltpu.get_barrier_semaphore()
    for step in range(1, SOURCES):
        for pick in (holder, sender):
            pl.semaphore_signal(barrier, inc=1, device_id=pick(step)[1], device_id_type=MESH)

    @pl.when(jnp.logical_not(at_home))
    def _():
        for pick in (holder, sender):
            pl.semaphore_signal(barrier, inc=1, device_id=pick(0)[1], device_id_type=MESH)

    def wait_barrier():
        pl.semaphore_wait(barrier, 2 * (SOURCES - 1) + 2 * ((z_lo + core) % 2))

    def pack(source, main, rest):
        main[...] = dot32(place_main[...], source[...]).astype(low).reshape(main.shape)
        total = jnp.zeros((SOURCES * REST_ROWS, REST_WIDTH), wide)
        for quarter in range(4):
            total += dot32(
                place_rest[quarter], source[:, quarter * REST_WIDTH : (quarter + 1) * REST_WIDTH]
            )
        rest[:, :, :REST_WIDTH] = total.astype(low).reshape(SOURCES, REST_ROWS, REST_WIDTH)

    def start(number, pick, slot, main, rest, main_in, rest_in):
        copies = []
        pairs = ((main, main_in), (rest, rest_in))

        def remote(step, which):
            other, device = pick(step)
            src, dst = pairs[which]
            at = (number * 2 + which) * SOURCES + step
            return pltpu.make_async_remote_copy(
                src_ref=src.at[other],
                dst_ref=dst.at[slot],
                send_sem=send.at[at],
                recv_sem=recv.at[at],
                device_id=device,
                device_id_type=MESH,
            )

        def local(which):
            src, dst = pairs[which]
            at = (number * 2 + which) * SOURCES
            return pltpu.make_async_copy(src.at[slot], dst.at[slot], recv.at[at])

        for step in range(1, SOURCES):
            for which in range(2):
                copy = remote(step, which)
                copy.start()
                copies.append(copy)

        @pl.when(at_home)
        def _():
            for which in range(2):
                local(which).start()

        @pl.when(jnp.logical_not(at_home))
        def _():
            for which in range(2):
                remote(0, which).start()

        def wait_recv():
            @pl.when(at_home)
            def _():
                for which in range(2):
                    local(which).wait()

            @pl.when(jnp.logical_not(at_home))
            def _():
                for which in range(2):
                    remote(0, which).wait_recv()

            for copy in copies:
                copy.wait_recv()

        def wait_send():
            @pl.when(jnp.logical_not(at_home))
            def _():
                for which in range(2):
                    remote(0, which).wait_send()

            for copy in copies:
                copy.wait_send()

        return wait_recv, wait_send

    def unpack(main_in, rest_in, rows, group):
        at = pl.ds(4 * group, 4)
        main = main_in[at].reshape(4 * MAIN_ROWS, -1)
        rest = rest_in[at].reshape(4 * REST_ROWS, -1)
        for quarter in range(4):
            lanes = slice(quarter * REST_WIDTH, (quarter + 1) * REST_WIDTH)
            rows[pl.ds(group * 4 * CAPACITY, 4 * CAPACITY), lanes] = (
                dot32(from_main[...], main[:, lanes])
                + dot32(from_rest[quarter], rest[:, :REST_WIDTH])
            ).astype(low)

    def repack(rows, main, rest, group):
        at = pl.ds(4 * group, 4)
        block = rows[pl.ds(group * 4 * CAPACITY, 4 * CAPACITY), :]
        main[at] = dot32(to_main[...], block).astype(low).reshape(4, MAIN_ROWS, -1)
        total = jnp.zeros((4 * REST_ROWS, REST_WIDTH), wide)
        for quarter in range(4):
            total += dot32(
                to_rest[quarter], block[:, quarter * REST_WIDTH : (quarter + 1) * REST_WIDTH]
            )
        rest[at, :, :REST_WIDTH] = total.astype(low).reshape(4, REST_ROWS, REST_WIDTH)

    pack(normed, x_main, x_rest)
    lanes = lax.broadcasted_iota(jnp.int32, (normed.shape[0], 128), 1)
    gate_rows = jnp.zeros((SOURCES * REST_ROWS, 128), wide)
    for choice in range(TOP):
        held = in_three(gates[:, choice : choice + 1], lanes) * gate_lanes[choice]
        gate_rows += dot32(place_gate[choice], held.astype(low))
    x_rest[:, :, REST_WIDTH:] = gate_rows.astype(low).reshape(SOURCES, REST_ROWS, 128)
    wait_barrier()
    flights = start(0, holder, ctx, x_main, x_rest, x_main_in, x_rest_in)
    pack(cotangent, c_main, c_rest)
    cotangent_flights = start(1, holder, ctx, c_main, c_rest, c_main_in, c_rest_in)
    for load in loads:
        load.wait()
    flights[0]()
    for group in range(4):
        unpack(x_main_in, x_rest_in, rows_x, group)

    @pl.loop(0, gate_w.shape[1] // TILE)
    def _(tile):
        at = pl.ds(pl.multiple_of(tile * TILE, TILE), TILE)
        gate = dot32(rows_x[...], gate_w[:, at])
        up = dot32(rows_x[...], up_w[:, at])
        gate_pre[:, at] = gate
        up_pre[:, at] = up
        hidden[:, at] = (gate / (1.0 + jnp.exp(-gate)) * up).astype(low)

    @pl.loop(0, down_w.shape[1] // TILE)
    def _(tile):
        at = pl.ds(pl.multiple_of(tile * TILE, TILE), TILE)
        rows_y[:, at] = dot32(hidden[...], down_w[:, at]).astype(low)

    cotangent_flights[0]()
    lanes = lax.broadcasted_iota(jnp.int32, (4 * CAPACITY, 128), 1)
    for group in range(4):
        unpack(c_main_in, c_rest_in, rows_c, group)
        at = pl.ds(group * 4 * CAPACITY, 4 * CAPACITY)
        carried = x_rest_in[pl.ds(4 * group, 4), :, pl.ds(REST_WIDTH, 128)].reshape(4 * REST_ROWS, 128)
        gate = jnp.sum(dot32(from_gate[...], carried) * lane_mask[...], axis=1, keepdims=True)
        grad = rows_c[at, :].astype(wide)
        grad_gate = jnp.sum(grad * rows_y[at, :].astype(wide), axis=1, keepdims=True)
        rows_c[at, :] = (gate * grad).astype(low)
        held = (in_three(grad_gate, lanes) * lane_mask[...]).astype(low)
        d_rest[pl.ds(4 * group, 4), :, pl.ds(REST_WIDTH, 128)] = (
            dot32(to_gate[...], held).astype(low).reshape(4, REST_ROWS, 128)
        )

    @pl.loop(0, down_w.shape[0] // TILE)
    def _(tile):
        at = pl.ds(pl.multiple_of(tile * TILE, TILE), TILE)
        grad_hidden = across(rows_c[...], down_w[at, :])
        gate = gate_pre[:, at]
        sigmoid = 1.0 / (1.0 + jnp.exp(-gate))
        grad_gate_pre[:, at] = (
            grad_hidden * up_pre[:, at] * sigmoid * (1.0 + gate * (1.0 - sigmoid))
        ).astype(low)
        grad_up_pre[:, at] = (grad_hidden * gate * sigmoid).astype(low)

    @pl.loop(0, gate_w.shape[0] // TILE)
    def _(tile):
        at = pl.ds(pl.multiple_of(tile * TILE, TILE), TILE)
        rows_d[:, at] = (
            across(grad_gate_pre[...], gate_w[at, :]) + across(grad_up_pre[...], up_w[at, :])
        ).astype(low)

    for group in range(4):
        repack(rows_d, d_main, d_rest, group)
    flights_d = start(2, sender, expert, d_main, d_rest, d_main_in, d_rest_in)
    for group in range(4):
        repack(rows_y, y_main, y_rest, group)
    flights_y = start(3, sender, expert, y_main, y_rest, y_main_in, y_rest_in)

    turned[...] = rows_x[...].T

    @pl.loop(0, gate_w.shape[1] // TILE)
    def _(tile):
        at = pl.ds(pl.multiple_of(tile * TILE, TILE), TILE)
        gate_w[:, at] = dot32(turned[...], grad_gate_pre[:, at]).astype(low)
        up_w[:, at] = dot32(turned[...], grad_up_pre[:, at]).astype(low)

    turned[pl.ds(0, hidden.shape[1]), :] = hidden[...].T

    @pl.loop(0, down_w.shape[1] // TILE)
    def _(tile):
        at = pl.ds(pl.multiple_of(tile * TILE, TILE), TILE)
        down_w[:, at] = dot32(turned[pl.ds(0, hidden.shape[1]), :], rows_c[:, at]).astype(low)

    stores = [
        pltpu.make_async_copy(whole, grad, out_sem.at[n])
        for n, (whole, grad) in enumerate(zip((gate_w, up_w, down_w), grad_outs))
    ]
    for store in stores:
        store.start()
    flights_d[0]()
    main = d_main_in[...].reshape(SOURCES * MAIN_ROWS, -1)
    rest = d_rest_in[...].reshape(SOURCES * REST_ROWS, -1)
    for quarter in range(4):
        at = slice(quarter * REST_WIDTH, (quarter + 1) * REST_WIDTH)
        grad_normed[:, at] = dot32(place_main_t[0] + place_main_t[1], main[:, at]) + dot32(
            place_rest_t[0, quarter] + place_rest_t[1, quarter], rest[:, :REST_WIDTH]
        )
    for choice in range(TOP):
        grad_gates[:, choice : choice + 1] = jnp.sum(
            dot32(place_gate_t[choice], rest[:, REST_WIDTH:]) * gate_lanes[choice],
            axis=1,
            keepdims=True,
        )
    flights_y[0]()
    main = y_main_in[...].reshape(SOURCES * MAIN_ROWS, -1)
    rest = y_rest_in[...].reshape(SOURCES * REST_ROWS, -1)
    for quarter in range(4):
        at = slice(quarter * REST_WIDTH, (quarter + 1) * REST_WIDTH)
        total = jnp.zeros((normed.shape[0], REST_WIDTH), wide)
        for choice in range(TOP):
            total += gates[:, choice : choice + 1] * (
                dot32(place_main_t[choice], main[:, at])
                + dot32(place_rest_t[choice, quarter], rest[:, :REST_WIDTH])
            )
        mixture[:, at] = total
    for flight in (flights, cotangent_flights, flights_d, flights_y):
        flight[1]()
    for copy in stores:
        copy.wait()


WEIGHT_PARTS = 3


def run_experts(normed, cotangent, gates, routes, weights):
    rows, width = normed.shape
    hidden_width = weights[0].shape[-1]
    low, wide = jnp.bfloat16, jnp.float32
    count = SOURCES * CAPACITY
    place_main, place_rest, place_gate, gate_lanes = dispatch_tables(routes)
    send_main = (place_main[0] + place_main[1]).T
    send_rest = (place_rest[0] + place_rest[1]).transpose(0, 2, 1)
    send_gate = place_gate.transpose(0, 2, 1)
    vmem = pl.BlockSpec(memory_space=pltpu.VMEM)
    anywhere = pl.BlockSpec(memory_space=pl.ANY)
    main = pltpu.VMEM((SOURCES, MAIN_ROWS, width), low)
    long_rest = pltpu.VMEM((SOURCES, REST_ROWS, REST_WIDTH + 128), low)
    rest = pltpu.VMEM((SOURCES, REST_ROWS, REST_WIDTH), low)
    flights = 8 * SOURCES
    return pl.pallas_call(
        experts_kernel,
        out_shape=(
            jax.ShapeDtypeStruct((rows, width), wide),
            jax.ShapeDtypeStruct((rows, width), wide),
            jax.ShapeDtypeStruct((rows, TOP), wide),
            *[jax.ShapeDtypeStruct((width, hidden_width), low)] * 2,
            jax.ShapeDtypeStruct((hidden_width, width), low),
        ),
        in_specs=[vmem] * 17 + [anywhere] * WEIGHT_PARTS,
        out_specs=[vmem] * 3 + [anywhere] * 3,
        scratch_shapes=[
            pltpu.VMEM((width, hidden_width), low),
            pltpu.VMEM((width, hidden_width), low),
            pltpu.VMEM((hidden_width, width), low),
            main, long_rest, main, rest, main, long_rest, main, rest,
            main, long_rest, main, long_rest, main, rest, main, rest,
            pltpu.VMEM((count, width), low),
            pltpu.VMEM((count, width), low),
            pltpu.VMEM((count, hidden_width), wide),
            pltpu.VMEM((count, hidden_width), wide),
            pltpu.VMEM((count, hidden_width), low),
            pltpu.VMEM((count, hidden_width), low),
            pltpu.VMEM((count, hidden_width), low),
            pltpu.VMEM((count, width), low),
            pltpu.VMEM((count, width), low),
            pltpu.VMEM((width, count), low),
            pltpu.SemaphoreType.DMA((3,)),
            pltpu.SemaphoreType.DMA((3,)),
            pltpu.SemaphoreType.DMA((flights,)),
            pltpu.SemaphoreType.DMA((flights,)),
        ],
        compiler_params=pltpu.CompilerParams(
            collective_id=3, has_side_effects=True, vmem_limit_bytes=60 * 2**20
        ),
        cost_estimate=pl.CostEstimate(
            flops=18 * count * width * hidden_width, bytes_accessed=32 * 2**20, transcendentals=0
        ),
        name="run_experts",
    )(
        normed, cotangent, gates, send_main, send_rest, send_gate, gate_lanes,
        place_main, place_rest, place_gate, *unpack_tables(), *weights,
    )


def others_of(ctx):
    return [(step, (ctx + step) % SOURCES) for step in range(1, SOURCES)]


def greet(dp, ctx):
    barrier = pltpu.get_barrier_semaphore()
    for _, other in others_of(ctx):
        pl.semaphore_signal(barrier, inc=1, device_id=(dp, other), device_id_type=MESH)
    return barrier


def send_blocks(pairs, dp, ctx, send, recv):
    copies = []
    for step, other in others_of(ctx):
        for source, place_in, first in pairs:
            copy = pltpu.make_async_remote_copy(
                src_ref=source(other),
                dst_ref=place_in,
                send_sem=send.at[first + step - 1],
                recv_sem=recv.at[first + step - 1],
                device_id=(dp, other),
                device_id_type=MESH,
            )
            copy.start()
            copies.append(copy)
    return copies


def to_heads_kernel(with_kv, rows_ref, *refs):
    if with_kv:
        head_rows, head_kv, packed, send, recv, local = refs
    else:
        head_rows, packed, send, recv, local = refs
    dp, ctx = lax.axis_index("dp"), lax.axis_index("ctx")
    barrier = greet(dp, ctx)
    half = rows_ref.shape[0] // 2
    for head in range(KEY_VALUE_HEADS):
        for core in range(2):
            packed[2 * head + core] = rows_ref[
                core * half : (core + 1) * half, head * HEADS_WIDE : (head + 1) * HEADS_WIDE
            ]
    pl.semaphore_wait(barrier, SOURCES - 1)

    def kv_of(other):
        start = QUERY_HEAD_COUNT * HEAD_SIZE + (other // 2) * 2 * HEAD_SIZE
        return rows_ref.at[:, pl.ds(pl.multiple_of(start, 128), 2 * HEAD_SIZE)]

    pairs = [(lambda other: packed.at[other], head_rows.at[ctx], 0)]
    if with_kv:
        pairs = [(kv_of, head_kv.at[ctx], SOURCES - 1)] + pairs
    copies = send_blocks(pairs, dp, ctx, send, recv)
    own = [pltpu.make_async_copy(packed.at[ctx], head_rows.at[ctx], local.at[0])]
    if with_kv:
        own.append(pltpu.make_async_copy(kv_of(ctx), head_kv.at[ctx], local.at[1]))
    for copy in own:
        copy.start()
    for copy in own + copies:
        copy.wait()


def to_heads(rows, with_kv, number):
    half = rows.shape[0] // 2
    low = jnp.bfloat16
    vmem = pl.BlockSpec(memory_space=pltpu.VMEM)
    count = (2 if with_kv else 1) * (SOURCES - 1)
    shapes = [jax.ShapeDtypeStruct((SOURCES, half, HEADS_WIDE), low)]
    if with_kv:
        shapes.append(jax.ShapeDtypeStruct((SOURCES, 2 * half, 2 * HEAD_SIZE), low))
    out = pl.pallas_call(
        functools.partial(to_heads_kernel, with_kv),
        out_shape=shapes,
        in_specs=[vmem],
        out_specs=[vmem] * len(shapes),
        scratch_shapes=[
            pltpu.VMEM((SOURCES, half, HEADS_WIDE), low),
            pltpu.SemaphoreType.DMA((count,)),
            pltpu.SemaphoreType.DMA((count,)),
            pltpu.SemaphoreType.DMA((2,)),
        ],
        compiler_params=pltpu.CompilerParams(
            collective_id=number, has_side_effects=True, vmem_limit_bytes=16 * 2**20
        ),
        cost_estimate=pl.CostEstimate(flops=0, bytes_accessed=4 * 2**20, transcendentals=0),
        name="to_heads",
    )(rows)
    return [part.reshape(-1, part.shape[-1]) for part in out]


def to_tokens_kernel(with_kv, head_rows, *refs):
    if with_kv:
        head_kv, out, rows_in, kv_in, send, recv = refs
    else:
        out, rows_in, send, recv = refs
    dp, ctx = lax.axis_index("dp"), lax.axis_index("ctx")
    barrier = greet(dp, ctx)
    half = head_rows.shape[1]
    pl.semaphore_wait(barrier, SOURCES - 1)
    pairs = [(lambda other: head_rows.at[other], rows_in.at[ctx], 0)]
    if with_kv:
        pairs = [(lambda other: head_kv.at[other], kv_in.at[ctx], SOURCES - 1)] + pairs
    copies = send_blocks(pairs, dp, ctx, send, recv)
    rows_in[ctx] = head_rows[ctx]
    if with_kv:
        kv_in[ctx] = head_kv[ctx]
    for copy in copies:
        copy.wait()
    for head in range(KEY_VALUE_HEADS):
        for core in range(2):
            out[
                core * half : (core + 1) * half, head * HEADS_WIDE : (head + 1) * HEADS_WIDE
            ] = rows_in[2 * head + core]
        if with_kv:
            start = QUERY_HEAD_COUNT * HEAD_SIZE + head * 2 * HEAD_SIZE
            out[:, start : start + 2 * HEAD_SIZE] = (
                kv_in[2 * head].astype(jnp.float32) + kv_in[2 * head + 1].astype(jnp.float32)
            ).astype(jnp.bfloat16)


def to_tokens(head_rows, head_kv, number):
    half = head_rows.shape[0] // SOURCES
    low = jnp.bfloat16
    vmem = pl.BlockSpec(memory_space=pltpu.VMEM)
    with_kv = head_kv is not None
    width = QUERY_HEAD_COUNT * HEAD_SIZE
    arrays = [head_rows.reshape(SOURCES, half, HEADS_WIDE)]
    landing = [pltpu.VMEM((SOURCES, half, HEADS_WIDE), low)]
    if with_kv:
        arrays.append(head_kv.reshape(SOURCES, 2 * half, 2 * HEAD_SIZE))
        landing.append(pltpu.VMEM((SOURCES, 2 * half, 2 * HEAD_SIZE), low))
        width += KEY_VALUE_HEADS * 2 * HEAD_SIZE
    count = len(arrays) * (SOURCES - 1)
    return pl.pallas_call(
        functools.partial(to_tokens_kernel, with_kv),
        out_shape=jax.ShapeDtypeStruct((2 * half, width), low),
        in_specs=[vmem] * len(arrays),
        out_specs=vmem,
        scratch_shapes=landing
        + [pltpu.SemaphoreType.DMA((count,)), pltpu.SemaphoreType.DMA((count,))],
        compiler_params=pltpu.CompilerParams(
            collective_id=number, has_side_effects=True, vmem_limit_bytes=16 * 2**20
        ),
        cost_estimate=pl.CostEstimate(flops=0, bytes_accessed=4 * 2**20, transcendentals=0),
        name="to_tokens",
    )(*arrays)


KEY_STEP = 256
QUERY_STEP = 256
GROUP = QUERY_HEAD_COUNT // KEY_VALUE_HEADS
HEADS_WIDE = GROUP * HEAD_SIZE


def allowed_block(block, pos, start):
    keys = lax.broadcasted_iota(jnp.int32, (KEY_STEP, QUERY_STEP), 0) + block * KEY_STEP
    return (keys <= pos) & (keys >= start)


def attend_kernel(low, high, pos_ref, start_ref, query_ref, kv_ref, kvt_ref, out_ref, outt_ref, log_ref):
    zeros = jnp.zeros((QUERY_STEP, HEAD_SIZE), jnp.bfloat16)

    @pl.loop(0, query_ref.shape[0] // QUERY_STEP)
    def _(tile):
        rows = pl.ds(pl.multiple_of(tile * QUERY_STEP, QUERY_STEP), QUERY_STEP)
        pos, start = pos_ref[:, rows], start_ref[:, rows]
        queries = query_ref[rows, :]
        padded = [
            jnp.concatenate([queries[:, h * HEAD_SIZE : (h + 1) * HEAD_SIZE], zeros], axis=1)
            for h in range(GROUP)
        ]

        def step(block, carry):
            keys = pl.ds(pl.multiple_of(block * KEY_STEP, KEY_STEP), KEY_STEP)
            kv = kv_ref[keys, :]
            values_t = kvt_ref[HEAD_SIZE:, keys]
            allowed = allowed_block(block, pos, start)
            new = []
            for h in range(GROUP):
                highest, total, summed = carry[h]
                scores = jnp.where(allowed, across(kv, padded[h]), NEGATIVE)
                new_high = jnp.maximum(highest, jnp.max(scores, axis=0, keepdims=True))
                weights = jnp.exp(scores - new_high)
                shrink = jnp.exp(highest - new_high)
                total = total * shrink + jnp.sum(weights, axis=0, keepdims=True)
                summed = summed * shrink + dot32(values_t, weights.astype(jnp.bfloat16))
                new.append((new_high, total, summed))
            return tuple(new)

        first = tuple(
            (
                jnp.full((1, QUERY_STEP), NEGATIVE, jnp.float32),
                jnp.zeros((1, QUERY_STEP), jnp.float32),
                jnp.zeros((HEAD_SIZE, QUERY_STEP), jnp.float32),
            )
            for _ in range(GROUP)
        )
        last = lax.fori_loop(low[tile], high[tile], step, first)
        pieces = []
        for h in range(GROUP):
            highest, total, summed = last[h]
            log_ref[h : h + 1, rows] = highest + jnp.log(total)
            summed = summed / total
            outt_ref[h, :, rows] = summed
            pieces.append(summed)
        out_ref[rows, :] = jnp.concatenate(pieces, axis=0).T.astype(jnp.bfloat16)


def attend_back_kernel(
    low, high, pos_ref, start_ref, query_ref, kv_ref, kvt_ref, outt_ref, log_ref, grad_ref,
    grad_query_ref, grad_kv_ref, sums,
):
    zeros = jnp.zeros((QUERY_STEP, HEAD_SIZE), jnp.bfloat16)
    sums[...] = jnp.zeros_like(sums)

    @pl.loop(0, query_ref.shape[0] // QUERY_STEP)
    def _(tile):
        rows = pl.ds(pl.multiple_of(tile * QUERY_STEP, QUERY_STEP), QUERY_STEP)
        pos, start = pos_ref[:, rows], start_ref[:, rows]
        queries, grads = query_ref[rows, :], grad_ref[rows, :]
        grads_t = grads.astype(jnp.float32).T
        query_pads, grad_pads, deltas, logs = [], [], [], []
        for h in range(GROUP):
            part = slice(h * HEAD_SIZE, (h + 1) * HEAD_SIZE)
            query_pads.append(jnp.concatenate([queries[:, part], zeros], axis=1))
            grad_pads.append(jnp.concatenate([zeros, grads[:, part]], axis=1))
            deltas.append(jnp.sum(grads_t[part, :] * outt_ref[h, :, rows], axis=0, keepdims=True))
            logs.append(log_ref[h : h + 1, rows])

        def step(block, carry):
            keys = pl.ds(pl.multiple_of(block * KEY_STEP, KEY_STEP), KEY_STEP)
            kv = kv_ref[keys, :]
            keys_t = kvt_ref[:HEAD_SIZE, keys]
            allowed = allowed_block(block, pos, start)
            new = []
            total = sums[keys, :]
            for h in range(GROUP):
                scores = jnp.where(allowed, across(kv, query_pads[h]), NEGATIVE)
                probs = jnp.exp(scores - logs[h])
                grad_probs = across(kv, grad_pads[h])
                grad_scores = (probs * (grad_probs - deltas[h])).astype(jnp.bfloat16)
                total += dot32(probs.astype(jnp.bfloat16), grad_pads[h])
                total += dot32(grad_scores, query_pads[h])
                new.append(carry[h] + dot32(keys_t, grad_scores))
            sums[keys, :] = total
            return tuple(new)

        first = tuple(jnp.zeros((HEAD_SIZE, QUERY_STEP), jnp.float32) for _ in range(GROUP))
        last = lax.fori_loop(low[tile], high[tile], step, first)
        factor = HEAD_SIZE ** (-0.5)
        grad_query_ref[rows, :] = (jnp.concatenate(last, axis=0) * factor).T.astype(jnp.bfloat16)

    grad_kv_ref[...] = sums[...].astype(jnp.bfloat16)


def attend_call(kernel, name, bounds, arrays, out_shape, scratch, matmuls, area):
    vmem = pl.BlockSpec(memory_space=pltpu.VMEM)
    return pl.pallas_call(
        kernel,
        out_shape=out_shape,
        grid_spec=pltpu.PrefetchScalarGridSpec(
            num_scalar_prefetch=2,
            grid=(1,),
            in_specs=[vmem] * len(arrays),
            out_specs=[vmem] * len(out_shape),
            scratch_shapes=scratch,
        ),
        compiler_params=pltpu.CompilerParams(vmem_limit_bytes=32 * 2**20),
        cost_estimate=pl.CostEstimate(
            flops=matmuls * 2 * HEAD_SIZE * area, bytes_accessed=8 * 2**20, transcendentals=area
        ),
        name=name,
    )(*bounds, *arrays)


def shards(
    tokens,
    segments,
    routes,
    gain_attn,
    w_query,
    key_weight,
    value_weight,
    w_out,
    w_router,
    gain_ffn,
    w_gate,
    w_up,
    w_down,
    cotangent,
):
    low = jnp.bfloat16
    wide = jnp.float32
    device_rows, width = tokens.shape
    sequence = segments.shape[0]
    half = device_rows // 2
    core = lax.axis_index("ctx") % 2
    ctx_count = lax.axis_size("ctx")
    slice_rows = w_query.shape[0]
    kv_shards = jnp.stack(
        [
            key_weight.reshape(slice_rows, KEY_VALUE_HEADS, HEAD_SIZE),
            value_weight.reshape(slice_rows, KEY_VALUE_HEADS, HEAD_SIZE),
        ],
        axis=2,
    ).reshape(slice_rows, 2 * KEY_VALUE_HEADS * HEAD_SIZE)
    shard = jnp.concatenate(
        [w_query, kv_shards, w_out, w_router, gain_attn[:, None], gain_ffn[:, None]], axis=1
    )
    shard = jnp.pad(shard, ((0, 0), (0, PACK - shard.shape[1])))
    packed, expert_weights = gather_weights(shard, w_gate[0], w_up[0], w_down[0])
    qkv_proj = packed[:, :2560]
    out_proj = packed[:, 2560:4096]
    router_proj = packed[:, 4096:4112]
    scale_one = packed[:, 4112].astype(wide)
    scale_two = packed[:, 4113].astype(wide)
    order = jnp.arange(ctx_count * half, dtype=jnp.int32)
    query_pos = (order // half) * device_rows + core * half + order % half
    first_of = jnp.stack([jnp.sum((segments < n).astype(jnp.int32)) for n in range(5)])
    starts = jnp.sum(
        jnp.where(segments[:, None] == jnp.arange(5, dtype=jnp.int32)[None, :], first_of[None, :], 0),
        axis=1,
    )
    query_start = lax.dynamic_slice_in_dim(
        starts.reshape(ctx_count, device_rows), core * half, half, axis=1
    ).reshape(-1)
    tiles = query_pos.reshape(-1, QUERY_STEP)
    bounds = (
        query_start.reshape(-1, QUERY_STEP)[:, 0] // KEY_STEP,
        tiles[:, -1] // KEY_STEP + 1,
    )
    mask_rows = (query_pos[None, :], query_start[None, :])

    residual = tokens.astype(wide)
    inverse_one = inverse_rms(residual)
    normed = (residual * inverse_one * scale_one).astype(low)
    qkv = jnp.dot(normed, qkv_proj, preferred_element_type=wide).astype(low)

    factor = HEAD_SIZE ** (-0.5)
    qkv = jnp.concatenate([qkv[:, :width] * factor, qkv[:, width:]], axis=1)
    head_queries, head_kv = to_heads(qkv, True, 4)
    head_kvt = head_kv.T
    count = head_queries.shape[0]
    area = GROUP * count * sequence // 3
    head_out, head_outt, log_total = attend_call(
        attend_kernel,
        "attend",
        bounds,
        (*mask_rows, head_queries, head_kv, head_kvt),
        (
            jax.ShapeDtypeStruct((count, HEADS_WIDE), low),
            jax.ShapeDtypeStruct((GROUP, HEAD_SIZE, count), wide),
            jax.ShapeDtypeStruct((GROUP, count), wide),
        ),
        [],
        2,
        area,
    )
    attended = to_tokens(head_out, None, 5)

    hidden_one = residual + contract_cols(attended, out_proj)
    inverse_two = inverse_rms(hidden_one)
    normed_two = (hidden_one * inverse_two * scale_two).astype(low)
    logits = jnp.dot(normed_two, router_proj, preferred_element_type=wide)
    picked = (
        routes[:, :, None] == jnp.arange(SOURCES, dtype=jnp.int32)[None, None, :]
    ).astype(wide)
    chosen = jnp.sum(picked * logits[:, None, :], axis=-1)
    gate_weights = jax.nn.softmax(chosen, axis=-1)
    grad_normed_two, mixture, grad_gates, *expert_grads = run_experts(
        normed_two, cotangent, gate_weights, routes, expert_weights
    )
    mixed = (hidden_one + mixture).astype(low)
    grad_y = cotangent.astype(wide)
    grad_chosen = gate_weights * (
        grad_gates - jnp.sum(gate_weights * grad_gates, axis=-1, keepdims=True)
    )
    grad_logits = jnp.sum(picked * grad_chosen[:, :, None], axis=1).astype(low)
    grad_normed_two = grad_normed_two + contract_cols(grad_logits, router_proj)
    grad_router_full = contract_rows(normed_two, grad_logits)
    grad_hidden_one, grad_gain_two = norm_backward(
        grad_normed_two, hidden_one, inverse_two, scale_two
    )
    grad_hidden_one = grad_hidden_one + grad_y
    grad_branch = grad_hidden_one.astype(low)
    grad_attended = jnp.dot(grad_branch, out_proj, preferred_element_type=wide).astype(low)

    (head_grads,) = to_heads(grad_attended, False, 6)
    head_grad_queries, head_grad_kv = attend_call(
        attend_back_kernel,
        "attend_back",
        bounds,
        (*mask_rows, head_queries, head_kv, head_kvt, head_outt, log_total, head_grads),
        (
            jax.ShapeDtypeStruct((count, HEADS_WIDE), low),
            jax.ShapeDtypeStruct((sequence, 2 * HEAD_SIZE), low),
        ),
        [pltpu.VMEM((sequence, 2 * HEAD_SIZE), wide)],
        5,
        area,
    )
    grad_qkv = to_tokens(head_grad_queries, head_grad_kv, 7)
    grad_normed = contract_cols(grad_qkv, qkv_proj)
    grad_residual, grad_gain_one = norm_backward(grad_normed, residual, inverse_one, scale_one)
    grad_input = (grad_residual + grad_hidden_one).astype(low)
    rest = jnp.concatenate(
        [
            grad_router_full.astype(low),
            grad_gain_one.astype(low)[:, None],
            grad_gain_two.astype(low)[:, None],
            jnp.zeros((width, PACK - 4114), low),
        ],
        axis=1,
    )
    share, (grad_gate, grad_up, grad_down) = scatter_sum(
        normed, grad_qkv, grad_branch, attended, rest, expert_grads
    )
    share = share.astype(wide)
    kv_share = share[:, 1536:2560].reshape(slice_rows, KEY_VALUE_HEADS, 2, HEAD_SIZE)
    return (
        mixed,
        grad_input,
        share[:, 4112],
        share[:, :1536],
        kv_share[:, :, 0].reshape(slice_rows, -1),
        kv_share[:, :, 1].reshape(slice_rows, -1),
        share[:, 2560:4096],
        share[:, 4096:4112],
        share[:, 4113],
        grad_gate[None],
        grad_up[None],
        grad_down[None],
    )


def solution(mesh):
    in_specs = (
        P(("dp", "ctx"), None),
        P("dp"),
        P(("dp", "ctx"), None),
        P(("dp", "ctx")),
        P(("dp", "ctx"), None),
        P(("dp", "ctx"), None),
        P(("dp", "ctx"), None),
        P(("dp", "ctx"), None),
        P(("dp", "ctx"), None),
        P(("dp", "ctx")),
        P("ctx", "dp", None),
        P("ctx", "dp", None),
        P("ctx", "dp", None),
        P(("dp", "ctx"), None),
    )
    out_specs = (
        P(("dp", "ctx"), None),
        P(("dp", "ctx"), None),
        P(("dp", "ctx")),
        P(("dp", "ctx"), None),
        P(("dp", "ctx"), None),
        P(("dp", "ctx"), None),
        P(("dp", "ctx"), None),
        P(("dp", "ctx"), None),
        P(("dp", "ctx")),
        P("ctx", "dp", None),
        P("ctx", "dp", None),
        P("ctx", "dp", None),
    )
    return jax.shard_map(shards, mesh=mesh, in_specs=in_specs, out_specs=out_specs, check_vma=False)
```

time: 1000 us -> 546 us (0.55)
  waiting for transfers between devices: 360 us -> 0 us
  Pallas kernels: 131 us -> 459 us
  matrix products: 292 us -> 24.3 us
  local copies, waits for them, and re-layouts: 134 us -> 27.4 us
  starting transfers between devices: 22.3 us -> 0 us
  between operations: 15.4 us -> 1.72 us
  other arithmetic: 37.6 us -> 26.8 us
    pallas_call x2 -> x9, Pallas kernels: 131 us -> 459 us  [the longest x1 123 us: run_experts(): pl.pallas_call(experts_kernel, out_shape=(jax.ShapeDtypeStruct((rows, wid...]
    dot_general x71 -> x3, matrix products: 262 us -> 10 us  [the longest x1 5.14 us: shards(): qkv = jnp.dot(normed, qkv_proj, preferred_element_type=wide).astype(low)]
    all_gather x5 -> x0, waiting for transfers between devices: 171 us -> none  [the longest x1 66.5 us: shards(): lax.all_gather(w_down, 'dp', axis=1, tiled=True)]
    unnamed x12 -> x0, waiting for transfers between devices: 112 us -> none
    all_to_all x4 -> x0, waiting for transfers between devices: 77.9 us -> none  [the longest x1 27.2 us: shards(): lax.all_to_all(outgoing, 'ctx', split_axis=0, concat_axis=0, tiled=True)]
    unnamed x116 -> x48, local copies, waits for them, and re-layouts: 55.8 us -> 5.98 us
    reshape x7 -> x4, local copies, waits for them, and re-layouts: 32.1 us -> 0.58 us  [the longest x1 0.29 us: to_heads(): return [part.reshape(-1, part.shape[-1]) for part in out]]
    concatenate x2, local copies, waits for them, and re-layouts: 23.7 us -> 1 us  [the longest x1 0.93 us: shards(): jnp.concatenate([w_query, kv_shards, w_out, w_router, gain_attn[:, None],...]
  transfers between devices with their start and end apart: 14 -> 0, of which waited for: 9 -> 0; matrix products, arithmetic and copies ran while one was open for 40% -> 0% of each run, Pallas kernels for 0% -> 0%
where the time goes in v2:
time: 546 us; the launch traced here: 540 us
  Pallas kernels  459 us (84%)
  local copies, waits for them, and re-layouts  27.4 us (5%)
  other arithmetic  26.8 us (5%)
  matrix products  24.3 us (4%)
    pallas_call x1, Pallas kernels, run_experts(): pl.pallas_call(experts_kernel, out_shape=(jax.ShapeDtypeStruct((rows, wid...  123 us
    pallas_call x1, Pallas kernels, scatter_sum(): pl.pallas_call(scatter_kernel, out_shape=[jax.ShapeDtypeStruct((16, PACK)...  103 us
    pallas_call x1, Pallas kernels, gather_weights(): pl.pallas_call(gather_kernel, out_shape=[jax.ShapeDtypeStruct((4, 2, 2, 2...  82.5 us
    pallas_call x2, Pallas kernels, attend_call(): pl.pallas_call(kernel, out_shape=out_shape, grid_spec=pltpu.PrefetchScala...  66.2 us
    pallas_call x2, Pallas kernels, to_tokens(): pl.pallas_call(functools.partial(to_tokens_kernel, with_kv), out_shape=ja...  45.1 us
    pallas_call x2, Pallas kernels, to_heads(): pl.pallas_call(functools.partial(to_heads_kernel, with_kv), out_shape=sha...  40 us
    dot_general x3, matrix products, contract_cols(): lax.dot_general(left, right, (((1,), (1,)), ((), ())), preferred_element_...  14.1 us

profile of v2, /device:TPU:1, one launch (start us, length us, event | category | flops | bytes accessed | tf_op | source)
XLA Modules:
  0.0 539.6 jit_solution(7859356566079260003)
XLA Ops:
  0.6 1.3 fusion.28
  1.9 0.8 stack_reshape.9
  2.7 0.8 stack_reshape.8
  3.8 0.7 copy.111
  4.5 0.8 copy.112
  5.3 0.9 concatenate.9
  7.6 82.5 %gather_weights.1 = (bf16[4,2,2,2,48,4608]{5,4,3,2,1,0:T(8,128)(2,1)}, bf16[1536,1024]{1,0:T(8,128)(2,1)}, bf16[1536,1024]{1,0:T(8,128)(2,1)}, bf16[1024,1536]{1,0:T(8,128)(2,1)}) custom-call(bf16[16,4608]{1,0:T(8,128)(2,1)} %pad.22.shard, bf16[48,64]{1,0:T(8,128)(2,1)} %and_convert_fusion.9.merge, bf16[192,1024]{1,0:T(8,128)(2,1)} %bitcast.84, ...), custom_call_target="tpu_custom_call" | custom-call | bytes 41943040 | tf_op jit(solution)/shard_map/gather_weights/pallas_call | solution.py:332
  90.1 1.5 fusion.67
  92.5 3.3 stack.35
  96.7 5.1 fusion.8
  102.1 26.7 %to_heads.2 = (bf16[16,96,192]{2,1,0:T(8,128)(2,1)S(1)}, bf16[16,192,128]{2,1,0:T(8,128)(2,1)S(1)}) custom-call(bf16[192,2560]{1,0:T(8,128)(2,1)S(1)} %pad_maximum_fusion.rows_ref), custom_call_target="tpu_custom_call" | custom-call | bytes 4194304 | tf_op jit(solution)/shard_map/to_heads/pallas_call | solution.py:1153
  129.1 34.6 %attend.1 = (bf16[1536,192]{1,0:T(8,128)(2,1)S(1)}, f32[3,64,1536]{2,1,0:T(8,128)S(1)}, f32[3,1536]{1,0:T(4,128)S(1)}) custom-call(s32[6]{0:T(128)S(1)} %and_select_fusion.24.low, s32[6]{0:T(128)S(1)} %fusion.64.high, s32[1,1536]{1,0:T(1,128)S(1)} %fusion.41.pos_ref, s32[1,1536]{1,0:T(1,128)S(1)} %broadcast_in_dim_reshape.4.start_ref, ...), custom_call_target="tpu_custom_call" | custom-call | flops 1207959552 | bytes 8388608 | tf_op jit(solution)/shard_map/attend/pallas_call | solution.py:1340
  163.7 16.1 %to_tokens.2.attended = bf16[192,1536]{1,0:T(8,128)(2,1)S(1)} custom-call(bf16[16,96,192]{2,1,0:T(8,128)(2,1)S(1)} %bitcast.77), custom_call_target="tpu_custom_call" | custom-call | bytes 4194304 | tf_op jit(solution)/shard_map/to_tokens/pallas_call | solution.py:1216
  179.8 5.2 multiply_reduce_fusion.2
  185.3 1.4 multiply_convert_fusion.normed
  186.8 0.8 copy-done.6
  187.6 1.3 fusion.31
  189.2 0.7 exponential_divide_fusion.gates
  190.4 0.9 reduce-window.6
  192.5 0.8 fusion.33
  193.3 1.8 copy.126.place_main
  195.1 0.8 broadcast_compare_fusion
  195.9 1.7 add_select_fusion
  197.5 1.0 copy.122
  198.5 0.9 and_convert_fusion.3
  199.3 1.1 and_convert_fusion.place_rest_t
  200.5 0.9 copy-done.8
  201.3 0.8 fusion.29
  202.1 2.0 copy.127.place_rest
  204.2 0.8 and_convert_fusion.2.place_gate
  205.1 0.8 compare_convert_fusion.gate_lanes
  208.2 0.8 copy.128.from_rest
  211.1 123.0 %run_experts.1 = (f32[192,1536]{1,0:T(8,128)}, f32[192,1536]{1,0:T(8,128)}, f32[192,2]{1,0:T(8,128)}, bf16[1536,1024]{1,0:T(8,128)(2,1)}, bf16[1536,1024]{1,0:T(8,128)(2,1)}, /*index=5*/bf16[1024,1536]{1,0:T(8,128)(2,1)}) custom-call(bf16[192,1536]{1,0:T(8,128)(2,1)} %copy-done.6, bf16[192,1536]{1,0:T(8,128)(2,1)} %cotangent.1, ...), custom_call_target="tpu_custom_call" | custom-call | flops 16307453952 | bytes 33554432 | tf_op jit(solution)/shard_map/run_experts/pallas_call | solution.py:1040
  334.2 1.1 multiply_reduce_fusion.3
  335.2 1.0 subtract_multiply_fusion
  336.4 2.4 multiply_reduce_fusion
  339.2 3.6 fusion.14.rows_ref
  342.9 13.3 %to_heads.3 = bf16[16,96,192]{2,1,0:T(8,128)(2,1)S(1)} custom-call(bf16[192,1536]{1,0:T(8,128)(2,1)S(1)} %fusion.14.rows_ref), custom_call_target="tpu_custom_call" | custom-call | bytes 4194304 | tf_op jit(solution)/shard_map/to_heads/pallas_call | solution.py:1153
  356.2 31.6 %attend_back.1 = (bf16[1536,192]{1,0:T(8,128)(2,1)S(1)}, bf16[3072,128]{1,0:T(8,128)(2,1)S(1)}) custom-call(s32[6]{0:T(128)S(1)} %and_select_fusion.24.low, s32[6]{0:T(128)S(1)} %fusion.64.high, s32[1,1536]{1,0:T(1,128)S(1)} %fusion.41.pos_ref, s32[1,1536]{1,0:T(1,128)S(1)} %broadcast_in_dim_reshape.4.start_ref, bf16[1536,192]{1,0:T(8,128)(2,1)S(1)} %bitcast.79, ...), custom_call_target="tpu_custom_call" | custom-call | flops 3019898880 | bytes 8388608 | tf_op jit(solution)/shard_map/attend_back/pallas_call | solution.py:1340
  387.8 29.0 %to_tokens.3.grad_qkv = bf16[192,2560]{1,0:T(8,128)(2,1)S(1)} custom-call(bf16[16,96,192]{2,1,0:T(8,128)(2,1)S(1)} %bitcast.75, bf16[16,192,128]{2,1,0:T(8,128)(2,1)S(1)} %bitcast.76), custom_call_target="tpu_custom_call" | custom-call | bytes 4194304 | tf_op jit(solution)/shard_map/to_tokens/pallas_call | solution.py:1216
  416.8 6.4 %fusion.27 = (bf16[1536]{0:T(1024)(128)(2,1)S(1)}, f32[192]{0:T(256)S(1)}, f32[192,1536]{1,0:T(8,128)S(1)}) fusion(bf16[192,1536]{1,0:T(8,128)(2,1)S(1)} %copy-done.5, f32[192]{0:T(256)S(1)} %add_rsqrt_fusion.1, f32[1536]{0:T(1024)S(1)} %convert_reduce_fusion.6, bf16[192,2560]{1,0:T(8,128)(2,1)S(1)} %to_tokens.3.grad_qkv, bf16[1536,4608]{1,0:T(8,128)(2,1)} %bitcast.93), kind=kOutput, calls=%fused_computation.27 | convolution fusion | flops 1512012032 | bytes 10627584 | tf_op jit(solution)/shard_map/dot_general | solution.py:674
  423.3 1.7 fusion.26
  426.0 1.9 maximum_maximum_fusion.rest
  428.6 102.6 %scatter_sum.1 = (bf16[16,4608]{1,0:T(8,128)(2,1)}, f32[192,1024]{1,0:T(8,128)}, f32[192,1024]{1,0:T(8,128)}, f32[128,1536]{1,0:T(8,128)}) custom-call(bf16[192,1536]{1,0:T(8,128)(2,1)} %copy-done.10, bf16[192,2560]{1,0:T(8,128)(2,1)} %copy-done, bf16[192,1536]{1,0:T(8,128)(2,1)} %copy-done.11, bf16[192,1536]{1,0:T(8,128)(2,1)} %copy-done.1, ...), custom_call_target="tpu_custom_call" | custom-call | flops 2415919104 | bytes 29360128 | tf_op jit(solution)/shard_map/scatter_sum/pallas_call | solution.py:627
  531.2 1.0 slice_convert_fusion
  536.0 0.9 copy.140
  536.9 0.9 copy.141
  538.3 0.9 copy.142
  (126 shorter events, 17.2 us)
Async XLA Ops:
  90.1 1.7 copy-start.20
  90.1 6.4 %copy-start.5 = (bf16[192,1536]{1,0:T(8,128)(2,1)S(1)}, bf16[192,1536]{1,0:T(8,128)(2,1)}, u32[]{:S(2)}) copy-start(bf16[192,1536]{1,0:T(8,128)(2,1)} %param.14) | copy-start | bytes 1769476
  96.7 5.2 copy-start.10
  163.7 21.3 %copy-start.2 = (f32[3,64,1536]{2,1,0:T(8,128)}, f32[3,64,1536]{2,1,0:T(8,128)S(1)}, u32[]{:S(2)}) copy-start(f32[3,64,1536]{2,1,0:T(8,128)S(1)} %get-tuple-element.41.outt_ref) | copy-start | bytes 3538948
  179.8 5.3 copy-start.1
  185.3 3.5 copy-start.19
  186.8 0.8 copy-start.6
  191.7 0.6 copy-start.14
  192.5 7.9 %copy-start.12 = (bf16[2,192,512]{2,1,0:T(8,128)(2,1)}, bf16[2,192,512]{2,1,0:T(8,128)(2,1)S(1)}, u32[]{:S(2)}) copy-start(bf16[2,192,512]{2,1,0:T(8,128)(2,1)S(1)} %and_convert_fusion.1.place_main_t) | copy-start | bytes 1179652
  200.5 0.9 copy-start.8
  202.1 2.9 copy-start.18
  336.4 2.5 copy-start.4
  336.4 2.5 copy-start.9
  339.2 3.7 copy-start.11
  342.9 13.3 %copy-start.3 = (f32[3,64,1536]{2,1,0:T(8,128)S(1)}, f32[3,64,1536]{2,1,0:T(8,128)}, u32[]{:S(2)}) copy-start(f32[3,64,1536]{2,1,0:T(8,128)} %copy-done.2) | copy-start | bytes 3538948
  416.8 6.4 %copy-start = (bf16[192,2560]{1,0:T(8,128)(2,1)}, bf16[192,2560]{1,0:T(8,128)(2,1)S(1)}, u32[]{:S(2)}) copy-start(bf16[192,2560]{1,0:T(8,128)(2,1)S(1)} %to_tokens.3.grad_qkv) | copy-start | bytes 2949124
  416.8 6.4 %copy-start.13 = (f32[192,1536]{1,0:T(8,128)S(1)}, f32[192,1536]{1,0:T(8,128)}, u32[]{:S(2)}) copy-start(f32[192,1536]{1,0:T(8,128)} %get-tuple-element.40) | copy-start | bytes 3538948
  423.3 2.2 copy-start.7
  531.2 4.8 copy-start.17
  533.6 3.3 copy-start.16
  536.9 1.4 copy-start.15

commit v3 on v2

v3 whole, which is shorter than its diff:
```python
import functools

import jax
import jax.numpy as jnp
import numpy as np
from jax import lax
from jax.experimental import pallas as pl
from jax.experimental.pallas import tpu as pltpu
from jax.sharding import PartitionSpec as P

QUERY_HEAD_COUNT = 24
KEY_VALUE_HEADS = 8
HEAD_SIZE = 64
TOP = 2

EPSILON = 1e-06
NEGATIVE = -1e30
SOURCES = 16
GROUP = QUERY_HEAD_COUNT // KEY_VALUE_HEADS
HEADS_WIDE = GROUP * HEAD_SIZE
MESH = pl.DeviceIdType.MESH

PACK = 4608
HALF = PACK // 2
QUARTER = PACK // 4
RING_ORDERS = (("x", "y", "z"), ("y", "z", "x"), ("z", "x", "y"))


def place():
    dp = lax.axis_index("dp")
    ctx = lax.axis_index("ctx")
    return {"y": dp // 2, "z": (ctx // 8) * 2 + dp % 2, "x": (ctx // 2) % 4, "core": ctx % 2}


def device_of(spot):
    z = spot["z"]
    return (spot["y"] * 2 + z % 2, (z // 2) * 8 + spot["x"] * 2 + spot["core"])


def moved(spot, axis, step):
    other = dict(spot)
    if axis == "core":
        other["core"] = 1 - spot["core"]
    else:
        other[axis] = (spot[axis] + step) % 4
    return other


def member(spot, step):
    index = (spot["x"] % 2) * 2 + spot["core"]
    target = (index // 2 + step // 2) % 2 * 2 + (index % 2 + step % 2) % 2
    other = dict(spot)
    other["x"] = (spot["x"] // 2) * 2 + target // 2
    other["core"] = target % 2
    return other, target


def partner(spot):
    other = dict(spot)
    other["z"] = spot["z"] // 2 * 2 + (spot["z"] + 1) % 2
    other["core"] = (spot["core"] + 1) % 2
    return other


def others_of(ctx):
    return [(step, (ctx + step) % SOURCES) for step in range(1, SOURCES)]


def meet(spot, heads):
    barrier = pltpu.get_barrier_semaphore()
    others = [member(spot, step)[0] for step in (1, 2, 3)] + [partner(spot)]
    others += [moved(spot, axis, step) for axis in "xyz" for step in (1, 2, 3)]
    others = [device_of(other) for other in others]
    others += [(lax.axis_index("dp"), other) for _, other in heads]
    for other in others:
        pl.semaphore_signal(barrier, inc=1, device_id=other, device_id_type=MESH)
    pl.semaphore_wait(barrier, len(others))


def region(spot, known, part, base):
    def pick(axis, value, size):
        return pl.ds(0, size) if axis in known else pl.ds(value, 1)

    z = spot["z"]
    if "x" in known:
        columns = pl.ds(base, HALF)
    else:
        columns = pl.ds(pl.multiple_of(base + (spot["x"] % 2) * QUARTER, 128), QUARTER)
    return (
        pick("y", spot["y"], 4),
        pick("z", z % 2, 2),
        pick("z", z // 2, 2),
        pick("x", spot["x"] // 2, 2),
        pl.ds(part * 16, 16),
        columns,
    )


def expert_rows(ref, spot, core, half=None):
    rows = ref.shape[0] // 8
    first = (spot["y"] * 2 + core) * rows
    if half is not None:
        rows //= 2
        first += half * rows
    return ref.at[pl.ds(pl.multiple_of(first, 32), rows)]


def half_region(where, axis, half):
    if axis == "y":
        return where[:1] + (pl.ds(half, 1),) + where[2:]
    return (pl.ds(2 * half, 2),) + where[1:]


def relay(ring, numbers, send, recv, whole, half):
    spot, axis = ring

    def copy(ref, step, number):
        return pltpu.make_async_remote_copy(
            src_ref=ref,
            dst_ref=ref,
            send_sem=send.at[numbers + number],
            recv_sem=recv.at[numbers + number],
            device_id=device_of(moved(spot, axis, step)),
            device_id_type=MESH,
        )

    first = [copy(whole(spot), 1, 0), copy(whole(spot), 3, 1)]
    second = [copy(half(moved(spot, axis, 3), 0), 1, 2), copy(half(moved(spot, axis, 1), 1), 3, 3)]
    return first, second


def gather_kernel(
    shard, merge, tokens, own_gate, own_up, own_down,
    out, gate_out, up_out, down_out, head_rows, head_kv, scales,
    pieces, joined, qkv_w, rest_w, normed, qkv, packed,
    send0, recv0, send, recv, send_core, recv_core, local,
    swap_send, swap_recv, swap_local, line_send, line_recv, mate_send, mate_recv, ring_send, ring_recv,
    head_send, head_recv, head_local,
):
    spot = place()
    dp, ctx = lax.axis_index("dp"), lax.axis_index("ctx")
    meet(spot, others_of(ctx))
    mate = moved(spot, "core", 1)
    stays = spot["core"] == spot["z"] % 2
    experts = ((own_gate, gate_out), (own_up, up_out), (own_down, down_out))

    def swaps():
        return [
            pltpu.make_async_remote_copy(
                src_ref=own,
                dst_ref=expert_rows(whole, spot, spot["z"] % 2),
                send_sem=swap_send.at[n],
                recv_sem=swap_recv.at[n],
                device_id=device_of(partner(spot)),
                device_id_type=MESH,
            )
            for n, (own, whole) in enumerate(experts)
        ]

    def stays_here():
        return [
            pltpu.make_async_copy(own, expert_rows(whole, spot, spot["core"]), swap_local.at[n])
            for n, (own, whole) in enumerate(experts)
        ]

    def line(n):
        whole = experts[n][1]
        return relay(
            (spot, "y"),
            4 * n,
            line_send,
            line_recv,
            lambda at: expert_rows(whole, at, spot["core"]),
            lambda at, half: expert_rows(whole, at, spot["core"], half),
        )

    def to_mates(step):
        source = moved(spot, "y", 4 - step)
        return [
            pltpu.make_async_remote_copy(
                src_ref=expert_rows(whole, source, spot["core"]),
                dst_ref=expert_rows(whole, source, spot["core"]),
                send_sem=mate_send.at[3 * step + n],
                recv_sem=mate_recv.at[3 * step + n],
                device_id=device_of(mate),
                device_id_type=MESH,
            )
            for n, (own, whole) in enumerate(experts)
        ]

    def start_all(copies):
        for copy in copies:
            copy.start()

    @pl.when(stays)
    def _():
        start_all(stays_here())

    @pl.when(jnp.logical_not(stays))
    def _():
        start_all(swaps())

    index = (spot["x"] % 2) * 2 + spot["core"]
    quarter = spot["core"] * 2 + spot["x"] % 2
    copies = []
    for step in (1, 2, 3):
        other, target = member(spot, step)
        goal = other["core"] * 2 + other["x"] % 2
        copy = pltpu.make_async_remote_copy(
            src_ref=shard.at[:, pl.ds(pl.multiple_of(goal * QUARTER, 128), QUARTER)],
            dst_ref=pieces.at[index],
            send_sem=send0.at[step - 1],
            recv_sem=recv0.at[step - 1],
            device_id=device_of(other),
            device_id_type=MESH,
        )
        copy.start()
        copies.append(copy)
    pieces[index] = shard[:, pl.ds(pl.multiple_of(quarter * QUARTER, 128), QUARTER)]
    for copy in copies:
        copy.wait()
    joined[...] = jnp.dot(
        merge[...], pieces[...].reshape(64, QUARTER), preferred_element_type=jnp.float32
    ).astype(jnp.bfloat16)
    base = pl.multiple_of(spot["core"] * HALF, 128)
    mine = region(spot, "", 0, base)
    own = pltpu.make_async_copy(
        joined,
        out.at[spot["y"], spot["z"] % 2, spot["z"] // 2, spot["x"] // 2, :, mine[5]],
        local,
    )
    own.start()
    own.wait()
    core_copies = []

    def to_mate(number, where):
        copy = pltpu.make_async_remote_copy(
            src_ref=out.at[where],
            dst_ref=out.at[where],
            send_sem=send_core.at[number],
            recv_sem=recv_core.at[number],
            device_id=device_of(mate),
            device_id_type=MESH,
        )
        copy.start()
        core_copies.append(copy)

    flights, relays, finals = {}, [], []
    for stage in range(3):
        for part, order in enumerate(RING_ORDERS):
            axis, known = order[stage], order[:stage]
            if stage > 0:
                for copy in flights[part]:
                    copy.wait_recv()
            where = region(spot, known, part, base)
            if stage == 2:
                ring = relay(
                    (spot, axis),
                    4 * part,
                    ring_send,
                    ring_recv,
                    lambda at, known=known, part=part: out.at[region(at, known, part, base)],
                    lambda at, half, known=known, part=part, axis=axis: out.at[
                        half_region(region(at, known, part, base), axis, half)
                    ],
                )
                start_all(ring[0])
                relays.append(ring)
                finals.append((axis, known))
                to_mate(part * 4, where)
                continue
            started = []
            for step in (1, 3, 2):
                number = (stage * 3 + part) * 3 + step - 1
                copy = pltpu.make_async_remote_copy(
                    src_ref=out.at[where],
                    dst_ref=out.at[where],
                    send_sem=send.at[number],
                    recv_sem=recv.at[number],
                    device_id=device_of(moved(spot, axis, step)),
                    device_id_type=MESH,
                )
                copy.start()
                started.append(copy)
            flights[part] = started
            copies += started
        if stage == 1:

            @pl.when(stays)
            def _():
                for copy in stays_here():
                    copy.wait()

            @pl.when(jnp.logical_not(stays))
            def _():
                for copy in swaps():
                    copy.wait()


    mates = {step: to_mates(step) for step in (1, 3, 2)}

    def pass_on(ring):
        first, second = ring
        for number in range(2):
            first[number].wait_recv()
            second[number].start()

    residual = tokens[...].astype(jnp.float32)
    inverse = lax.rsqrt(jnp.mean(residual * residual, axis=1, keepdims=True) + EPSILON)
    for ring in relays:
        pass_on(ring)
    lines = [line(n) for n in range(3)]
    for first, _ in lines:
        start_all(first)
    own_mates = to_mates(0)
    for part, (axis, _) in enumerate(finals):
        for step in (1, 3):
            to_mate(part * 4 + step, region(moved(spot, axis, 4 - step), RING_ORDERS[part][:2], part, base))
    for part, (_, second) in enumerate(relays):
        for copy in second:
            copy.wait_recv()
        axis = RING_ORDERS[part][2]
        to_mate(part * 4 + 2, region(moved(spot, axis, 2), RING_ORDERS[part][:2], part, base))
    for copy in core_copies:
        copy.wait_recv()
    kv_at = QUERY_HEAD_COUNT * HEAD_SIZE
    qkv_width = qkv.shape[1]
    loads = [
        pltpu.make_async_copy(
            out.at[:, :, :, :, :, pl.ds(PACK - 512, 128)], rest_w, head_local.at[2]
        ),
        pltpu.make_async_copy(out.at[:, :, :, :, :, pl.ds(0, qkv_width)], qkv_w, head_local.at[3]),
    ]
    for load in loads:
        load.start()
    loads[0].wait()
    gains = rest_w[...].reshape(1536, 128).astype(jnp.float32).T
    scales[...] = gains[16:24, :]
    normed[...] = (residual * inverse * gains[16:17, :]).astype(jnp.bfloat16)
    loads[1].wait()
    factor = HEAD_SIZE ** (-0.5)

    @pl.loop(0, qkv_width // 256)
    def _(n):
        at = pl.ds(pl.multiple_of(n * 256, 256), 256)
        rows = jnp.dot(
            normed[...], qkv_w[:, :, :, :, :, at].reshape(1536, 256), preferred_element_type=jnp.float32
        )
        qkv[:, at] = (rows * jnp.where(n < kv_at // 256, factor, 1.0)).astype(jnp.bfloat16)

    half = tokens.shape[0] // 2
    for head in range(KEY_VALUE_HEADS):
        for core in range(2):
            packed[2 * head + core] = qkv[
                core * half : (core + 1) * half, head * HEADS_WIDE : (head + 1) * HEADS_WIDE
            ]

    def kv_of(other):
        start = kv_at + (other // 2) * 2 * HEAD_SIZE
        return qkv.at[:, pl.ds(pl.multiple_of(start, 128), 2 * HEAD_SIZE)]

    own_heads = [
        pltpu.make_async_copy(packed.at[ctx], head_rows.at[ctx], head_local.at[0]),
        pltpu.make_async_copy(kv_of(ctx), head_kv.at[ctx], head_local.at[1]),
    ]
    for copy in own_heads:
        copy.start()
    head_copies = []
    for step, other in others_of(ctx):
        for source, place_in, first in (
            (kv_of(other), head_kv.at[ctx], SOURCES),
            (packed.at[other], head_rows.at[ctx], 0),
        ):
            copy = pltpu.make_async_remote_copy(
                src_ref=source,
                dst_ref=place_in,
                send_sem=head_send.at[first + step],
                recv_sem=head_recv.at[first + step],
                device_id=(dp, other),
                device_id_type=MESH,
            )
            copy.start()
            head_copies.append(copy)
    start_all(own_mates)
    for n, ring in enumerate(lines):
        pass_on(ring)
        mates[1][n].start()
        mates[3][n].start()
    for n, (_, second) in enumerate(lines):
        for copy in second:
            copy.wait_recv()
        mates[2][n].start()
    line_copies = [copy for first, second in lines + relays for copy in first + second]
    for copy in own_heads + head_copies:
        copy.wait()
    for copy in copies[3:] + line_copies:
        copy.wait_send()
    for copy in core_copies:
        copy.wait_send()
    for copy in own_mates + mates[1] + mates[2] + mates[3]:
        copy.wait()


def gather_weights(shard, tokens, gate, up, down):
    shard = jnp.pad(shard, ((0, 4), (0, 0)))
    target, source = np.arange(48)[:, None], np.arange(64)[None, :]
    merge = jnp.asarray(
        (target // 12 == source // 16) & (target % 12 == source % 16), jnp.bfloat16
    )
    vmem = pl.BlockSpec(memory_space=pltpu.VMEM)
    anywhere = pl.BlockSpec(memory_space=pltpu.HBM)
    low = jnp.bfloat16
    rows, width = tokens.shape
    qkv_width = QUERY_HEAD_COUNT * HEAD_SIZE + 2 * KEY_VALUE_HEADS * HEAD_SIZE
    experts = [
        jax.ShapeDtypeStruct((8 * part.shape[0], part.shape[1]), low) for part in (gate, up, down)
    ]
    dma = pltpu.SemaphoreType.DMA
    packed, *rest = pl.pallas_call(
        gather_kernel,
        out_shape=[jax.ShapeDtypeStruct((4, 2, 2, 2, 48, PACK), low)]
        + experts
        + [
            jax.ShapeDtypeStruct((SOURCES, rows // 2, HEADS_WIDE), low),
            jax.ShapeDtypeStruct((SOURCES, rows, 2 * HEAD_SIZE), low),
            jax.ShapeDtypeStruct((8, width), jnp.float32),
        ],
        in_specs=[vmem] * 3 + [anywhere] * 3,
        out_specs=[anywhere] * 4 + [vmem] * 3,
        scratch_shapes=[
            pltpu.VMEM((4, 16, QUARTER), low),
            pltpu.VMEM((48, QUARTER), low),
            pltpu.VMEM((4, 2, 2, 2, 48, qkv_width), low),
            pltpu.VMEM((4, 2, 2, 2, 48, 128), low),
            pltpu.VMEM((rows, width), low),
            pltpu.VMEM((rows, qkv_width), low),
            pltpu.VMEM((SOURCES, rows // 2, HEADS_WIDE), low),
            dma((3,)), dma((3,)), dma((18,)), dma((18,)), dma((12,)), dma((12,)), dma,
            dma((3,)), dma((3,)), dma((3,)), dma((12,)), dma((12,)), dma((12,)), dma((12,)),
            dma((12,)), dma((12,)),
            dma((2 * SOURCES,)), dma((2 * SOURCES,)), dma((4,)),
        ],
        compiler_params=pltpu.CompilerParams(
            collective_id=1, has_side_effects=True, vmem_limit_bytes=62 * 2**20
        ),
        cost_estimate=pl.CostEstimate(
            flops=2 * rows * width * qkv_width, bytes_accessed=40 * 2**20, transcendentals=0
        ),
        name="gather_weights",
    )(shard, merge, tokens, gate, up, down)
    return packed.reshape(1536, PACK), rest[:3], *rest[3:]


EARLY = 1536
SCATTER_ORDERS = (("x", "y", "z"), ("y", "z", "x"), ("z", "x", "y"))


def cut(spot, known, part, half):
    z = spot["z"]

    def pick(axis, value, size):
        return pl.ds(0, size) if axis in known else pl.ds(value, 1)

    columns = pl.ds(0, half)
    if "x" not in known:
        columns = pl.ds(pl.multiple_of((spot["x"] % 2) * (half // 2), 128), half // 2)
    return (
        pick("y", spot["y"], 4),
        pick("z", z % 2, 2),
        pick("z", z // 2, 2),
        pick("x", spot["x"] // 2, 2),
        pl.ds(part * 16, 16),
        columns,
    )


def landing_shape(known, half):
    return (
        4 if "y" in known else 1,
        2 if "z" in known else 1,
        2 if "z" in known else 1,
        2 if "x" in known else 1,
        16,
        half if "x" in known else half // 2,
    )


class Scatter:
    def __init__(self, spot, split, grads, total, done, packed, out, sems, landing):
        self.spot, self.split, self.grads, self.total, self.out = spot, split, grads, total, out
        self.done, self.packed = done, packed
        self.send_core, self.recv_core, self.send, self.recv, self.send_last, self.recv_last = sems
        self.landing = (landing[:3], landing[3:6], landing[6:9])
        self.half = total.shape[-1]
        self.base = pl.multiple_of(spot["core"] * self.half, 128)
        self.pending, self.copies = [], []

    def start(self):
        mate = moved(self.spot, "core", 1)
        mate_base = pl.multiple_of(mate["core"] * self.half, 128)
        for part in range(3):
            rows = pl.ds(part * 16, 16)
            copy = pltpu.make_async_remote_copy(
                src_ref=self.grads.at[:, :, :, :, rows, pl.ds(mate_base, self.half)],
                dst_ref=self.total.at[:, :, :, :, rows, :],
                send_sem=self.send_core.at[part],
                recv_sem=self.recv_core.at[part],
                device_id=device_of(mate),
                device_id_type=MESH,
            )
            copy.start()
            self.copies.append(copy)

    def first(self):
        cores = list(self.copies)
        for part in range(3):
            rows = pl.ds(part * 16, 16)
            cores[part].wait_recv()

            @pl.loop(0, 32)
            def _(block):
                at = (block // 8, (block // 4) % 2, (block // 2) % 2, block % 2, rows)
                self.total[at] = (
                    self.grads[at + (pl.ds(self.base, self.half),)].astype(jnp.float32)
                    + self.total[at].astype(jnp.float32)
                ).astype(jnp.bfloat16)

            self.pending.append(self.ring(part, 0))

    def ring(self, part, stage):
        axis, known = SCATTER_ORDERS[part][2 - stage], SCATTER_ORDERS[part][: 2 - stage]
        started = []
        for step in (1, 3, 2):
            other = moved(self.spot, axis, step)
            number = (stage * 3 + part) * 3 + step - 1
            copy = pltpu.make_async_remote_copy(
                src_ref=self.total.at[cut(other, known, part, self.half)],
                dst_ref=self.landing[stage][part].at[step - 1],
                send_sem=self.send.at[number],
                recv_sem=self.recv.at[number],
                device_id=device_of(other),
                device_id_type=MESH,
            )
            copy.start()
            started.append(copy)
        self.copies += started
        return started

    def next(self, stage):
        for part in range(3):
            known = SCATTER_ORDERS[part][: 2 - stage]
            for copy in self.pending[part]:
                copy.wait_recv()
            self.add(known, part, self.landing[stage][part])
            if stage < 2:
                self.pending[part] = self.ring(part, stage + 1)

    def add(self, known, part, landing):
        spot = self.spot
        shape = landing_shape(known, self.half)
        columns = cut(spot, known, part, self.half)[5]

        def body(block):
            a, b, c, d = (
                block // (shape[1] * shape[2] * shape[3]),
                (block // (shape[2] * shape[3])) % shape[1],
                (block // shape[3]) % shape[2],
                block % shape[3],
            )
            at = (
                a + (0 if "y" in known else spot["y"]),
                b + (0 if "z" in known else spot["z"] % 2),
                c + (0 if "z" in known else spot["z"] // 2),
                d + (0 if "x" in known else spot["x"] // 2),
                pl.ds(part * 16, 16),
                columns,
            )
            summed = self.total[at].astype(jnp.float32)
            for step in range(3):
                summed += landing[step, a, b, c, d].astype(jnp.float32)
            self.total[at] = summed.astype(jnp.bfloat16)

        count = shape[0] * shape[1] * shape[2] * shape[3]
        if count == 1:
            body(0)
        else:
            pl.loop(0, count)(body)

    def finish(self):
        spot = self.spot
        quarter = self.half // 2
        index = (spot["x"] % 2) * 2 + spot["core"]
        place_in = spot["core"] * 2 + spot["x"] % 2
        mine = cut(spot, "", 0, self.half)
        self.done[...] = self.total[
            spot["y"], spot["z"] % 2, spot["z"] // 2, spot["x"] // 2, :, mine[5]
        ]
        self.packed[...] = (
            jnp.dot(self.split[...], self.done[...], preferred_element_type=jnp.float32)
            .astype(jnp.bfloat16)
            .reshape(4, 16, quarter)
        )
        columns = pl.ds(pl.multiple_of(place_in * quarter, 128), quarter)
        self.last = []
        for step in (1, 2, 3):
            other, target = member(spot, step)
            copy = pltpu.make_async_remote_copy(
                src_ref=self.packed.at[target],
                dst_ref=self.out.at[:, columns],
                send_sem=self.send_last.at[step - 1],
                recv_sem=self.recv_last.at[step - 1],
                device_id=device_of(other),
                device_id_type=MESH,
            )
            copy.start()
            self.last.append(copy)
        self.out[:, columns] = self.packed[index]

    def end(self):
        for copy in self.last:
            copy.wait()
        for copy in self.copies:
            copy.wait_send()


def scatter_kernel(
    head_rows, head_kv, tokens, scales, grad_hidden, branch, attended, router_grad, gain_grad, split,
    packed_w, grad_gate, grad_up, grad_down,
    grad_input, out, late_out, gate_out, up_out, down_out,
    rows_in, kv_in, grad_qkv, grad_normed, normed,
    mate_send, mate_recv, own_sem, line_send, line_recv, swap_send, swap_recv,
    head_send, head_recv, weight_sem,
    *buffers,
):
    spot = place()
    dp, ctx = lax.axis_index("dp"), lax.axis_index("ctx")
    held, mates, lines, results, arrived = (buffers[3 * n : 3 * n + 3] for n in range(5))
    early = Scatter(spot, split, *buffers[15:19], out, buffers[19:25], buffers[25:34])
    late = Scatter(spot, split, *buffers[34:38], late_out, buffers[38:44], buffers[44:])
    wholes, finals = (grad_gate, grad_up, grad_down), (gate_out, up_out, down_out)
    mate = moved(spot, "core", 1)
    qkv_width = grad_qkv.shape[1]
    load = pltpu.make_async_copy(
        packed_w.at[:, :, :, :, :, pl.ds(0, qkv_width)],
        late.grads.at[:, :, :, :, :, pl.ds(0, qkv_width)],
        weight_sem,
    )
    load.start()
    own_copies, mate_copies = [], []
    for n, whole in enumerate(wholes):
        for y in range(4):
            rows = whole.shape[0] // 8

            def part(core, whole=whole, y=y, rows=rows):
                return whole.at[pl.ds(pl.multiple_of((2 * y + core) * rows, 64), rows)]

            own = pltpu.make_async_copy(part(spot["core"]), held[n].at[y], own_sem.at[4 * n + y])
            own.start()
            own_copies.append(own)
            mate_copies.append(
                pltpu.make_async_remote_copy(
                    src_ref=part(mate["core"]),
                    dst_ref=mates[n].at[y],
                    send_sem=mate_send.at[4 * n + y],
                    recv_sem=mate_recv.at[4 * n + y],
                    device_id=device_of(mate),
                    device_id_type=MESH,
                )
            )
    meet(spot, others_of(ctx))
    for copy in mate_copies:
        copy.start()
    head_copies = []
    for step, other in others_of(ctx):
        for source, place_in, first in ((head_kv, kv_in, SOURCES), (head_rows, rows_in, 0)):
            copy = pltpu.make_async_remote_copy(
                src_ref=source.at[other],
                dst_ref=place_in.at[ctx],
                send_sem=head_send.at[first + step],
                recv_sem=head_recv.at[first + step],
                device_id=(dp, other),
                device_id_type=MESH,
            )
            copy.start()
            head_copies.append(copy)
    rows_in[ctx] = head_rows[ctx]
    kv_in[ctx] = head_kv[ctx]

    tile = 256
    grads_shape = (4, 2, 2, 2, 48, tile)

    def fill(turned, right, grads):
        @pl.loop(0, right.shape[1] // tile)
        def _(n):
            at = pl.ds(pl.multiple_of(n * tile, tile), tile)
            grads[:, :, :, :, :, at] = (
                jnp.dot(turned, right[:, at], preferred_element_type=jnp.float32)
                .astype(jnp.bfloat16)
                .reshape(grads_shape)
            )

    fill(branch[...].T, attended, early.grads)
    early.start()

    line_copies = []
    for n in range(3):
        for copy in mate_copies[4 * n : 4 * n + 4]:
            copy.wait_recv()
        for copy in own_copies[4 * n : 4 * n + 4]:
            copy.wait()

        @pl.loop(0, 4)
        def _(y, n=n):
            held[n][y] = (
                held[n][y].astype(jnp.float32) + mates[n][y].astype(jnp.float32)
            ).astype(jnp.bfloat16)

        for step in (1, 3, 2):
            other = moved(spot, "y", step)
            copy = pltpu.make_async_remote_copy(
                src_ref=held[n].at[other["y"]],
                dst_ref=lines[n].at[step - 1],
                send_sem=line_send.at[3 * n + step - 1],
                recv_sem=line_recv.at[3 * n + step - 1],
                device_id=device_of(other),
                device_id_type=MESH,
            )
            copy.start()
            line_copies.append(copy)

    early.first()

    half = tokens.shape[0] // 2
    residual = tokens[...].astype(jnp.float32)
    inverse = lax.rsqrt(jnp.mean(residual * residual, axis=1, keepdims=True) + EPSILON)
    unit = residual * inverse
    scale = scales[0:1, :]
    normed[...] = (unit * scale).astype(jnp.bfloat16)
    for copy in head_copies:
        copy.wait_recv()
    for head in range(KEY_VALUE_HEADS):
        for core in range(2):
            grad_qkv[
                core * half : (core + 1) * half, head * HEADS_WIDE : (head + 1) * HEADS_WIDE
            ] = rows_in[2 * head + core]
        start = QUERY_HEAD_COUNT * HEAD_SIZE + head * 2 * HEAD_SIZE
        grad_qkv[:, start : start + 2 * HEAD_SIZE] = (
            kv_in[2 * head].astype(jnp.float32) + kv_in[2 * head + 1].astype(jnp.float32)
        ).astype(jnp.bfloat16)
    load.wait()
    grad_normed[...] = jnp.zeros_like(grad_normed)

    @pl.loop(0, qkv_width // tile)
    def _(n):
        at = pl.ds(pl.multiple_of(n * tile, tile), tile)
        grad_normed[...] += contract_cols(
            grad_qkv[:, at], late.grads[:, :, :, :, :, at].reshape(1536, tile)
        )

    fill(normed[...].T, grad_qkv, late.grads)
    gain_column = jnp.sum(grad_normed[...] * unit, axis=0, keepdims=True)
    lanes = lax.broadcasted_iota(jnp.int32, (1536, 128), 1)
    first_column = jnp.broadcast_to(gain_column, (128, 1536)).T
    second_column = jnp.broadcast_to(gain_grad[...], (128, 1536)).T
    rest = jnp.where(
        lanes < 16,
        router_grad[...].astype(jnp.float32),
        jnp.where(lanes == 16, first_column, jnp.where(lanes == 17, second_column, 0.0)),
    )
    at = qkv_width
    late.grads[:, :, :, :, :, at : at + 128] = rest.astype(jnp.bfloat16).reshape(4, 2, 2, 2, 48, 128)
    late.grads[:, :, :, :, :, at + 128 :] = jnp.zeros(
        (4, 2, 2, 2, 48, late.grads.shape[-1] - at - 128), jnp.bfloat16
    )
    late.start()
    early.next(0)
    grads_here = grad_normed[...] * scale
    grads_here = inverse * (
        grads_here - unit * jnp.mean(grads_here * unit, axis=1, keepdims=True)
    )
    grad_input[...] = (grads_here + grad_hidden[...]).astype(jnp.bfloat16)
    late.first()
    early.next(1)
    sum_lines(spot, held, lines, line_copies, results)
    swap_results(spot, results, arrived, swap_send, swap_recv, True)
    late.next(0)
    early.next(2)
    early.finish()
    late.next(1)
    late.next(2)
    late.finish()
    swap_results(spot, results, arrived, swap_send, swap_recv, False)
    stays = spot["core"] == spot["z"] % 2

    @pl.when(stays)
    def _():
        for result, final in zip(results, finals):
            final[...] = result[...]

    @pl.when(jnp.logical_not(stays))
    def _():
        for result, final in zip(arrived, finals):
            final[...] = result[...]

    early.end()
    late.end()
    for copy in mate_copies + head_copies + line_copies:
        copy.wait_send()


def sum_lines(spot, held, lines, line_copies, results):
    for copy in line_copies:
        copy.wait_recv()
    for mine, line, result in zip(held, lines, results):
        total = mine[spot["y"]].astype(jnp.float32)
        for step in range(3):
            total += line[step].astype(jnp.float32)
        result[...] = total.astype(jnp.bfloat16)


def swap_results(spot, results, arrived, send, recv, start):
    @pl.when(spot["core"] != spot["z"] % 2)
    def _():
        for n, (result, place_in) in enumerate(zip(results, arrived)):
            copy = pltpu.make_async_remote_copy(
                src_ref=result,
                dst_ref=place_in,
                send_sem=send.at[n],
                recv_sem=recv.at[n],
                device_id=device_of(partner(spot)),
                device_id_type=MESH,
            )
            if start:
                copy.start()
            else:
                copy.wait()


def scatter_sum(
    head_rows, head_kv, tokens, scales, grad_hidden, branch, attended, router_grad, gain_grad, packed,
    expert_grads,
):
    source, target = np.arange(48)[None, :], np.arange(64)[:, None]
    split = jnp.asarray(
        (source // 12 == target // 16) & (source % 12 == target % 16), jnp.bfloat16
    )
    low = jnp.bfloat16
    dma = pltpu.SemaphoreType.DMA
    blocks = [(part.shape[0] // 8, part.shape[1]) for part in expert_grads]
    buffers = [pltpu.VMEM((4,) + block, low) for block in blocks] * 2
    buffers += [pltpu.VMEM((3,) + block, low) for block in blocks]
    buffers += [pltpu.VMEM(block, low) for block in blocks] * 2
    for columns in (EARLY, PACK - EARLY):
        buffers += [
            pltpu.VMEM((4, 2, 2, 2, 48, columns), low),
            pltpu.VMEM((4, 2, 2, 2, 48, columns // 2), low),
            pltpu.VMEM((48, columns // 4), low),
            pltpu.VMEM((4, 16, columns // 4), low),
            dma((3,)), dma((3,)), dma((27,)), dma((27,)), dma((3,)), dma((3,)),
        ]
        buffers += [
            pltpu.VMEM((3,) + landing_shape(order[: 2 - stage], columns // 2), low)
            for stage in range(3)
            for order in SCATTER_ORDERS
        ]
    vmem = pl.BlockSpec(memory_space=pltpu.VMEM)
    anywhere = pl.BlockSpec(memory_space=pltpu.HBM)
    rows, width = tokens.shape
    head_rows = head_rows.reshape(SOURCES, rows // 2, HEADS_WIDE)
    head_kv = head_kv.reshape(SOURCES, rows, 2 * HEAD_SIZE)
    qkv_width = QUERY_HEAD_COUNT * HEAD_SIZE + 2 * KEY_VALUE_HEADS * HEAD_SIZE
    grad_input, out, late_out, *finals = pl.pallas_call(
        scatter_kernel,
        out_shape=[jax.ShapeDtypeStruct((rows, width), low)]
        + [jax.ShapeDtypeStruct((16, columns), low) for columns in (EARLY, PACK - EARLY)]
        + [jax.ShapeDtypeStruct(block, low) for block in blocks],
        in_specs=[vmem] * 10 + [anywhere] * 4,
        out_specs=[vmem] * 6,
        scratch_shapes=[
            pltpu.VMEM(head_rows.shape, low),
            pltpu.VMEM(head_kv.shape, low),
            pltpu.VMEM((rows, qkv_width), low),
            pltpu.VMEM((rows, width), jnp.float32),
            pltpu.VMEM((rows, width), low),
            dma((12,)), dma((12,)), dma((12,)), dma((9,)), dma((9,)), dma((3,)), dma((3,)),
            dma((2 * SOURCES,)), dma((2 * SOURCES,)), dma,
        ]
        + buffers,
        compiler_params=pltpu.CompilerParams(
            collective_id=2, has_side_effects=True, vmem_limit_bytes=62 * 2**20
        ),
        cost_estimate=pl.CostEstimate(
            flops=2 * rows * width * 6656, bytes_accessed=28 * 2**20, transcendentals=0
        ),
        name="scatter_sum",
    )(
        head_rows, head_kv, tokens, scales, grad_hidden, branch, attended, router_grad, gain_grad, split,
        packed.reshape(4, 2, 2, 2, 48, PACK), *expert_grads,
    )
    return grad_input, out[:12], late_out[:12], [final.astype(jnp.float32) for final in finals]


def contract_cols(left, right):
    return lax.dot_general(
        left, right, (((1,), (1,)), ((), ())), preferred_element_type=jnp.float32
    )


MAIN_ROWS = 32
REST_ROWS = 16
REST_WIDTH = 384
CAPACITY = 36
TILE = 256


def across(left, right):
    return lax.dot_general(
        left, right, (((1,), (1,)), ((), ())), preferred_element_type=jnp.float32
    )


def dot32(left, right):
    return jnp.dot(left, right, preferred_element_type=jnp.float32)


def tiles(extent, body):
    pl.loop(0, extent // TILE)(lambda n: body(pl.ds(pl.multiple_of(n * TILE, TILE), TILE)))


def ones_at(condition):
    return jnp.where(condition, 1.0, 0.0).astype(jnp.bfloat16)


def in_three(column, lanes):
    first = column.astype(jnp.bfloat16).astype(jnp.float32)
    second = (column - first).astype(jnp.bfloat16).astype(jnp.float32)
    third = column - first - second
    return jnp.where(lanes % 3 == 0, first, jnp.where(lanes % 3 == 1, second, third))


def unpack_tables():
    row = np.arange(4 * CAPACITY)[:, None]
    device, slot = row // CAPACITY, row % CAPACITY
    main = np.arange(4 * MAIN_ROWS)[None, :]
    from_main = (device == main // MAIN_ROWS) & (slot == main % MAIN_ROWS)
    rest = np.arange(4 * REST_ROWS)[None, :]
    from_rest = np.stack(
        [
            (device == rest // REST_ROWS)
            & ((rest // 4) % 4 == quarter)
            & (slot == MAIN_ROWS + rest % 4)
            for quarter in range(4)
        ]
    )
    from_gate = (device == rest // REST_ROWS) & (slot % REST_ROWS == rest % REST_ROWS)
    lane_mask = np.arange(128)[None, :] // 3 == slot // REST_ROWS
    return [
        jnp.asarray(table, jnp.bfloat16)
        for table in (from_main, from_main.T, from_rest, from_rest.transpose(0, 2, 1), from_gate, from_gate.T)
    ] + [jnp.asarray(lane_mask, jnp.float32)]


def place_rows(routes, axis):
    rows = routes[0].shape[axis]
    experts = lax.broadcasted_iota(jnp.int32, (rows, 128) if axis == 0 else (128, rows), 1 - axis)
    picked = [jnp.where(route == experts, 1.0, 0.0) for route in routes]
    both = (picked[0] + picked[1]).astype(jnp.bfloat16)
    first = lax.broadcasted_iota(jnp.int32, (rows, rows), 0)
    second = lax.broadcasted_iota(jnp.int32, (rows, rows), 1)
    if axis == 0:
        earlier = dot32(ones_at(second < first), both)
    else:
        earlier = dot32(both, ones_at(first < second))
    places = []
    for route, pick in zip(routes, picked):
        slot = jnp.sum(pick * earlier, axis=1 - axis, keepdims=True).astype(jnp.int32)
        whole = slot < MAIN_ROWS
        main = jnp.where(whole, route * MAIN_ROWS + slot, -1)
        rest = jnp.where(whole, -64, route * REST_ROWS + slot - MAIN_ROWS)
        block = jnp.where(slot < REST_ROWS, 0, jnp.where(whole, 1, 2))
        places.append((main, rest, route * REST_ROWS + slot - REST_ROWS * block, block))
    return places


def middle_kernel(
    head_out, tokens, cotangent, routes, routes_t, scale,
    from_main, to_main, from_rest, to_rest, from_gate, to_gate, lane_mask,
    packed_w, gate_src, up_src, down_src,
    attended, mixed, grad_hidden, grad_branch, router_grad, gain_grad, head_grads,
    gate_grad, up_grad, down_grad,
    gate_w, up_w, down_w, out_w, router_w,
    rows_in, head_send, hidden_one, normed, grad_normed,
    send_main, send_rest, send_gate, place_main, place_rest, place_gate,
    x_main, x_rest, c_main, c_rest, x_main_in, x_rest_in, c_main_in, c_rest_in,
    d_main_in, d_rest_in, y_main_in, y_rest_in,
    rows_x, rows_c, gate_pre, up_pre, hidden, grad_gate_pre, grad_up_pre, rows_y, turned,
    weight_sem, out_sem, swap_send, swap_recv, send, recv,
):
    low, wide = jnp.bfloat16, jnp.float32
    dp, ctx = lax.axis_index("dp"), lax.axis_index("ctx")
    rows, width = tokens.shape
    half = rows // 2
    out_at = QUERY_HEAD_COUNT * HEAD_SIZE + 2 * KEY_VALUE_HEADS * HEAD_SIZE
    loads = [
        pltpu.make_async_copy(part, whole, weight_sem.at[n])
        for n, (part, whole) in enumerate(
            (
                (packed_w.at[:, pl.ds(out_at, width)], out_w),
                (packed_w.at[:, pl.ds(out_at + width, 128)], router_w),
                (gate_src, gate_w),
                (up_src, up_w),
                (down_src, down_w),
            )
        )
    ]
    for load in loads:
        load.start()
    y, z_lo, core = dp // 2, dp % 2, ctx % 2
    expert = ctx // 2 * 2 + z_lo
    at_home = z_lo == core

    def holder(step):
        other = (ctx + step) % SOURCES
        return other, (2 * y + other % 2, other // 2 * 2 + z_lo)

    def sender(step):
        other = (expert + step) % SOURCES
        return other, (2 * y + core, other)

    def neighbour(step):
        other = (ctx + step) % SOURCES
        return other, (dp, other)

    barrier = pltpu.get_barrier_semaphore()
    for step in range(1, SOURCES):
        for pick in (neighbour, holder, sender):
            pl.semaphore_signal(barrier, inc=1, device_id=pick(step)[1], device_id_type=MESH)

    @pl.when(jnp.logical_not(at_home))
    def _():
        for pick in (holder, sender):
            pl.semaphore_signal(barrier, inc=1, device_id=pick(0)[1], device_id_type=MESH)

    def start(number, pick, slot, main, rest, main_in, rest_in):
        copies = []
        pairs = ((main, main_in), (rest, rest_in))

        def remote(step, which):
            other, device = pick(step)
            src, dst = pairs[which]
            at = (number * 2 + which) * SOURCES + step
            return pltpu.make_async_remote_copy(
                src_ref=src.at[other],
                dst_ref=dst.at[slot],
                send_sem=send.at[at],
                recv_sem=recv.at[at],
                device_id=device,
                device_id_type=MESH,
            )

        def local(which):
            src, dst = pairs[which]
            at = (number * 2 + which) * SOURCES
            return pltpu.make_async_copy(src.at[slot], dst.at[slot], recv.at[at])

        for step in range(1, SOURCES):
            for which in range(2):
                copy = remote(step, which)
                copy.start()
                copies.append(copy)

        @pl.when(at_home)
        def _():
            for which in range(2):
                local(which).start()

        @pl.when(jnp.logical_not(at_home))
        def _():
            for which in range(2):
                remote(0, which).start()

        def wait_recv():
            @pl.when(at_home)
            def _():
                for which in range(2):
                    local(which).wait()

            @pl.when(jnp.logical_not(at_home))
            def _():
                for which in range(2):
                    remote(0, which).wait_recv()

            for copy in copies:
                copy.wait_recv()

        def wait_send():
            @pl.when(jnp.logical_not(at_home))
            def _():
                for which in range(2):
                    remote(0, which).wait_send()

            for copy in copies:
                copy.wait_send()

        return wait_recv, wait_send

    def swap(number, source, place_in):
        copies = []
        for step in range(1, SOURCES):
            other, device = neighbour(step)
            at = number * SOURCES + step
            copy = pltpu.make_async_remote_copy(
                src_ref=source.at[other],
                dst_ref=place_in.at[ctx],
                send_sem=swap_send.at[at],
                recv_sem=swap_recv.at[at],
                device_id=device,
                device_id_type=MESH,
            )
            copy.start()
            copies.append(copy)
        place_in[ctx] = source[ctx]
        return copies

    def pack(source, main, rest):
        main[...] = dot32(send_main[...], source[...]).astype(low).reshape(main.shape)
        total = jnp.zeros((SOURCES * REST_ROWS, REST_WIDTH), wide)
        for quarter in range(4):
            total += dot32(
                send_rest[quarter], source[:, quarter * REST_WIDTH : (quarter + 1) * REST_WIDTH]
            )
        rest[:, :, :REST_WIDTH] = total.astype(low).reshape(SOURCES, REST_ROWS, REST_WIDTH)

    def unpack(main_in, rest_in, out, group):
        at = pl.ds(4 * group, 4)
        main = main_in[at].reshape(4 * MAIN_ROWS, -1)
        rest = rest_in[at].reshape(4 * REST_ROWS, -1)
        for quarter in range(4):
            lanes = slice(quarter * REST_WIDTH, (quarter + 1) * REST_WIDTH)
            out[pl.ds(group * 4 * CAPACITY, 4 * CAPACITY), lanes] = (
                dot32(from_main[...], main[:, lanes])
                + dot32(from_rest[quarter], rest[:, :REST_WIDTH])
            ).astype(low)

    def repack(source, main, rest, group):
        at = pl.ds(4 * group, 4)
        block = source[pl.ds(group * 4 * CAPACITY, 4 * CAPACITY), :]
        main[at] = dot32(to_main[...], block).astype(low).reshape(4, MAIN_ROWS, -1)
        total = jnp.zeros((4 * REST_ROWS, REST_WIDTH), wide)
        for quarter in range(4):
            total += dot32(
                to_rest[quarter], block[:, quarter * REST_WIDTH : (quarter + 1) * REST_WIDTH]
            )
        rest[at, :, :REST_WIDTH] = total.astype(low).reshape(4, REST_ROWS, REST_WIDTH)

    pl.semaphore_wait(barrier, 3 * (SOURCES - 1) + 2 * ((z_lo + core) % 2))
    heads_in = swap(0, head_out, rows_in)

    main_rows = lax.broadcasted_iota(jnp.int32, (SOURCES * MAIN_ROWS, rows), 0)
    rest_rows = lax.broadcasted_iota(jnp.int32, (SOURCES * REST_ROWS, rows), 0)
    places = place_rows([routes_t[c : c + 1, :] for c in range(TOP)], 1)
    send_main[...] = ones_at((main_rows == places[0][0]) | (main_rows == places[1][0]))
    for quarter in range(4):
        send_rest[quarter] = ones_at(
            (rest_rows == places[0][1] + 4 * quarter) | (rest_rows == places[1][1] + 4 * quarter)
        )
    for choice in range(TOP):
        send_gate[choice] = ones_at(rest_rows == places[choice][2])
    main_lanes = lax.broadcasted_iota(jnp.int32, (rows, SOURCES * MAIN_ROWS), 1)
    rest_lanes = lax.broadcasted_iota(jnp.int32, (rows, SOURCES * REST_ROWS), 1)
    lanes = lax.broadcasted_iota(jnp.int32, (rows, 128), 1)
    places = place_rows([routes[:, c : c + 1] for c in range(TOP)], 0)
    gate_lanes = []
    for choice, (main, rest, gate, block) in enumerate(places):
        place_main[choice] = ones_at(main_lanes == main)
        for quarter in range(4):
            place_rest[choice, quarter] = ones_at(rest_lanes == rest + 4 * quarter)
        place_gate[choice] = ones_at(rest_lanes == gate)
        gate_lanes.append(jnp.where((lanes >= 3 * block) & (lanes < 3 * block + 3), 1.0, 0.0))
    pack(cotangent, c_main, c_rest)
    cotangent_flights = start(1, holder, ctx, c_main, c_rest, c_main_in, c_rest_in)

    for load in loads:
        load.wait()
    for copy in heads_in:
        copy.wait_recv()
    for head in range(KEY_VALUE_HEADS):
        for part in range(2):
            attended[
                part * half : (part + 1) * half, head * HEADS_WIDE : (head + 1) * HEADS_WIDE
            ] = rows_in[2 * head + part]

    @functools.partial(tiles, width)
    def _(at):
        hidden_one[:, at] = tokens[:, at].astype(wide) + across(attended[...], out_w[at, :])

    inverse = lax.rsqrt(jnp.mean(hidden_one[...] * hidden_one[...], axis=1, keepdims=True) + EPSILON)
    normed[...] = (hidden_one[...] * inverse * scale[...]).astype(low)
    logits = dot32(normed[...], router_w[...])
    on_route = [lanes == routes[:, choice : choice + 1] for choice in range(TOP)]
    chosen = [jnp.sum(jnp.where(on, logits, 0.0), axis=1, keepdims=True) for on in on_route]
    highest = jnp.maximum(chosen[0], chosen[1])
    powers = [jnp.exp(value - highest) for value in chosen]
    gates = [power / (powers[0] + powers[1]) for power in powers]

    pack(normed, x_main, x_rest)
    total = jnp.zeros((SOURCES * REST_ROWS, 128), wide)
    for choice in range(TOP):
        carried = in_three(gates[choice], lanes) * gate_lanes[choice]
        total += dot32(send_gate[choice], carried.astype(low))
    x_rest[:, :, REST_WIDTH:] = total.astype(low).reshape(SOURCES, REST_ROWS, 128)
    flights = start(0, holder, ctx, x_main, x_rest, x_main_in, x_rest_in)

    flights[0]()
    for group in range(4):
        unpack(x_main_in, x_rest_in, rows_x, group)

    @functools.partial(tiles, gate_w.shape[1])
    def _(at):
        gate = dot32(rows_x[...], gate_w[:, at])
        up = dot32(rows_x[...], up_w[:, at])
        gate_pre[:, at] = gate
        up_pre[:, at] = up
        hidden[:, at] = (gate / (1.0 + jnp.exp(-gate)) * up).astype(low)

    @functools.partial(tiles, width)
    def _(at):
        rows_y[:, at] = dot32(hidden[...], down_w[:, at]).astype(low)

    cotangent_flights[0]()
    cotangent_flights[1]()
    for group in range(4):
        repack(rows_y, c_main, c_rest, group)
    flights_y = start(3, sender, expert, c_main, c_rest, y_main_in, y_rest_in)

    flights[1]()
    expert_lanes = lax.broadcasted_iota(jnp.int32, (4 * CAPACITY, 128), 1)
    for group in range(4):
        unpack(c_main_in, c_rest_in, rows_c, group)
        at = pl.ds(group * 4 * CAPACITY, 4 * CAPACITY)
        carried = x_rest_in[pl.ds(4 * group, 4), :, pl.ds(REST_WIDTH, 128)].reshape(4 * REST_ROWS, 128)
        gate = jnp.sum(dot32(from_gate[...], carried) * lane_mask[...], axis=1, keepdims=True)
        grad = rows_c[at, :].astype(wide)
        grad_gate = jnp.sum(grad * rows_y[at, :].astype(wide), axis=1, keepdims=True)
        rows_c[at, :] = (gate * grad).astype(low)
        held = (in_three(grad_gate, expert_lanes) * lane_mask[...]).astype(low)
        x_rest[pl.ds(4 * group, 4), :, pl.ds(REST_WIDTH, 128)] = (
            dot32(to_gate[...], held).astype(low).reshape(4, REST_ROWS, 128)
        )

    @functools.partial(tiles, down_w.shape[0])
    def _(at):
        grad_hidden_rows = across(rows_c[...], down_w[at, :])
        gate = gate_pre[:, at]
        sigmoid = 1.0 / (1.0 + jnp.exp(-gate))
        grad_gate_pre[:, at] = (
            grad_hidden_rows * up_pre[:, at] * sigmoid * (1.0 + gate * (1.0 - sigmoid))
        ).astype(low)
        grad_up_pre[:, at] = (grad_hidden_rows * gate * sigmoid).astype(low)

    @functools.partial(tiles, width)
    def _(at):
        rows_y[:, at] = (
            across(grad_gate_pre[...], gate_w[at, :]) + across(grad_up_pre[...], up_w[at, :])
        ).astype(low)

    for group in range(4):
        repack(rows_y, x_main, x_rest, group)
    flights_d = start(2, sender, expert, x_main, x_rest, d_main_in, d_rest_in)

    turned[...] = rows_x[...].T

    @functools.partial(tiles, gate_w.shape[1])
    def _(at):
        gate_w[:, at] = dot32(turned[...], grad_gate_pre[:, at]).astype(low)
        up_w[:, at] = dot32(turned[...], grad_up_pre[:, at]).astype(low)

    turned[pl.ds(0, hidden.shape[1]), :] = hidden[...].T

    @functools.partial(tiles, width)
    def _(at):
        down_w[:, at] = dot32(turned[pl.ds(0, hidden.shape[1]), :], rows_c[:, at]).astype(low)

    stores = [
        pltpu.make_async_copy(whole, grad, out_sem.at[n])
        for n, (whole, grad) in enumerate(
            ((gate_w, gate_grad), (up_w, up_grad), (down_w, down_grad))
        )
    ]
    for store in stores:
        store.start()

    flights_d[0]()
    main = d_main_in[...].reshape(SOURCES * MAIN_ROWS, -1)
    rest = d_rest_in[...].reshape(SOURCES * REST_ROWS, -1)
    grad_gates = [
        jnp.sum(
            dot32(place_gate[choice], rest[:, REST_WIDTH:]) * gate_lanes[choice],
            axis=1,
            keepdims=True,
        )
        for choice in range(TOP)
    ]
    mean = gates[0] * grad_gates[0] + gates[1] * grad_gates[1]
    grad_logits = jnp.zeros((rows, 128), wide)
    for choice in range(TOP):
        grad_logits += jnp.where(
            on_route[choice], gates[choice] * (grad_gates[choice] - mean), 0.0
        )
    grad_logits = grad_logits.astype(low)
    for quarter in range(4):
        at = slice(quarter * REST_WIDTH, (quarter + 1) * REST_WIDTH)
        grad_normed[:, at] = (
            dot32(place_main[0] + place_main[1], main[:, at])
            + dot32(place_rest[0, quarter] + place_rest[1, quarter], rest[:, :REST_WIDTH])
            + across(grad_logits, router_w[at, :])
        )
    unit = hidden_one[...] * inverse
    grads = grad_normed[...]
    gain_grad[...] = jnp.sum(grads * unit, axis=0, keepdims=True)
    grads = grads * scale[...]
    grads = inverse * (grads - unit * jnp.mean(grads * unit, axis=1, keepdims=True))
    grad_hidden[...] = grads + cotangent[...].astype(wide)
    grad_branch[...] = grad_hidden[...].astype(low)

    @functools.partial(tiles, width)
    def _(at):
        grad_normed[:, at] = dot32(grad_branch[...], out_w[:, at])

    for head in range(KEY_VALUE_HEADS):
        for part in range(2):
            head_send[2 * head + part] = grad_normed[
                part * half : (part + 1) * half, head * HEADS_WIDE : (head + 1) * HEADS_WIDE
            ].astype(low)
    grads_in = swap(1, head_send, head_grads)
    router_grad[...] = dot32(normed[...].T, grad_logits).astype(low)

    flights_y[0]()
    main = y_main_in[...].reshape(SOURCES * MAIN_ROWS, -1)
    rest = y_rest_in[...].reshape(SOURCES * REST_ROWS, -1)
    for quarter in range(4):
        at = slice(quarter * REST_WIDTH, (quarter + 1) * REST_WIDTH)
        total = hidden_one[:, at]
        for choice in range(TOP):
            total += gates[choice] * (
                dot32(place_main[choice], main[:, at])
                + dot32(place_rest[choice, quarter], rest[:, :REST_WIDTH])
            )
        mixed[:, at] = total.astype(low)
    for copy in grads_in:
        copy.wait_recv()
    for copy in heads_in + grads_in:
        copy.wait_send()
    flights_d[1]()
    flights_y[1]()
    for copy in stores:
        copy.wait()


def run_middle(head_out, tokens, cotangent, routes, scale, packed, weights):
    rows, width = tokens.shape
    half = rows // 2
    hidden_width = weights[0].shape[-1]
    low, wide = jnp.bfloat16, jnp.float32
    count = SOURCES * CAPACITY
    vmem = pl.BlockSpec(memory_space=pltpu.VMEM)
    anywhere = pl.BlockSpec(memory_space=pltpu.HBM)
    main = pltpu.VMEM((SOURCES, MAIN_ROWS, width), low)
    long_rest = pltpu.VMEM((SOURCES, REST_ROWS, REST_WIDTH + 128), low)
    rest = pltpu.VMEM((SOURCES, REST_ROWS, REST_WIDTH), low)
    heads = pltpu.VMEM((SOURCES, half, HEADS_WIDE), low)
    dma = pltpu.SemaphoreType.DMA
    return pl.pallas_call(
        middle_kernel,
        out_shape=(
            jax.ShapeDtypeStruct((rows, width), low),
            jax.ShapeDtypeStruct((rows, width), low),
            jax.ShapeDtypeStruct((rows, width), wide),
            jax.ShapeDtypeStruct((rows, width), low),
            jax.ShapeDtypeStruct((width, 128), low),
            jax.ShapeDtypeStruct((1, width), wide),
            jax.ShapeDtypeStruct((SOURCES, half, HEADS_WIDE), low),
            jax.ShapeDtypeStruct((width, hidden_width), low),
            jax.ShapeDtypeStruct((width, hidden_width), low),
            jax.ShapeDtypeStruct((hidden_width, width), low),
        ),
        in_specs=[vmem] * 13 + [anywhere] * 4,
        out_specs=[vmem] * 7 + [anywhere] * 3,
        scratch_shapes=[
            pltpu.VMEM((width, hidden_width), low),
            pltpu.VMEM((width, hidden_width), low),
            pltpu.VMEM((hidden_width, width), low),
            pltpu.VMEM((width, width), low),
            pltpu.VMEM((width, 128), low),
            heads,
            heads,
            pltpu.VMEM((rows, width), wide),
            pltpu.VMEM((rows, width), low),
            pltpu.VMEM((rows, width), wide),

            pltpu.VMEM((SOURCES * MAIN_ROWS, rows), low),
            pltpu.VMEM((4, SOURCES * REST_ROWS, rows), low),
            pltpu.VMEM((TOP, SOURCES * REST_ROWS, rows), low),
            pltpu.VMEM((TOP, rows, SOURCES * MAIN_ROWS), low),
            pltpu.VMEM((TOP, 4, rows, SOURCES * REST_ROWS), low),
            pltpu.VMEM((TOP, rows, SOURCES * REST_ROWS), low),
            main, long_rest, main, rest, main, long_rest, main, rest,
            main, long_rest, main, rest,
            pltpu.VMEM((count, width), low),
            pltpu.VMEM((count, width), low),
            pltpu.VMEM((count, hidden_width), wide),
            pltpu.VMEM((count, hidden_width), wide),
            pltpu.VMEM((count, hidden_width), low),
            pltpu.VMEM((count, hidden_width), low),
            pltpu.VMEM((count, hidden_width), low),
            pltpu.VMEM((count, width), low),
            pltpu.VMEM((width, count), low),
            dma((5,)), dma((3,)), dma((2 * SOURCES,)), dma((2 * SOURCES,)),
            dma((8 * SOURCES,)), dma((8 * SOURCES,)),
        ],
        compiler_params=pltpu.CompilerParams(
            collective_id=3, has_side_effects=True, vmem_limit_bytes=62 * 2**20
        ),
        cost_estimate=pl.CostEstimate(
            flops=18 * count * width * hidden_width, bytes_accessed=40 * 2**20, transcendentals=0
        ),
        name="run_middle",
    )(
        head_out.reshape(SOURCES, half, HEADS_WIDE), tokens, cotangent, routes, routes.T, scale[None, :],
        *unpack_tables(), packed, *weights,
    )


KEY_STEP = 256
QUERY_STEP = 256


def allowed_block(block, pos, start):
    keys = lax.broadcasted_iota(jnp.int32, (KEY_STEP, QUERY_STEP), 0) + block * KEY_STEP
    return (keys <= pos) & (keys >= start)


def attend_kernel(low, high, pos_ref, start_ref, query_ref, kv_ref, kvt_ref, out_ref, outt_ref, log_ref):
    zeros = jnp.zeros((QUERY_STEP, HEAD_SIZE), jnp.bfloat16)

    @pl.loop(0, query_ref.shape[0] // QUERY_STEP)
    def _(tile):
        rows = pl.ds(pl.multiple_of(tile * QUERY_STEP, QUERY_STEP), QUERY_STEP)
        pos, start = pos_ref[:, rows], start_ref[:, rows]
        queries = query_ref[rows, :]
        padded = [
            jnp.concatenate([queries[:, h * HEAD_SIZE : (h + 1) * HEAD_SIZE], zeros], axis=1)
            for h in range(GROUP)
        ]

        def step(block, carry):
            keys = pl.ds(pl.multiple_of(block * KEY_STEP, KEY_STEP), KEY_STEP)
            kv = kv_ref[keys, :]
            values_t = kvt_ref[HEAD_SIZE:, keys]
            allowed = allowed_block(block, pos, start)
            new = []
            for h in range(GROUP):
                highest, total, summed = carry[h]
                scores = jnp.where(allowed, across(kv, padded[h]), NEGATIVE)
                new_high = jnp.maximum(highest, jnp.max(scores, axis=0, keepdims=True))
                weights = jnp.exp(scores - new_high)
                shrink = jnp.exp(highest - new_high)
                total = total * shrink + jnp.sum(weights, axis=0, keepdims=True)
                summed = summed * shrink + dot32(values_t, weights.astype(jnp.bfloat16))
                new.append((new_high, total, summed))
            return tuple(new)

        first = tuple(
            (
                jnp.full((1, QUERY_STEP), NEGATIVE, jnp.float32),
                jnp.zeros((1, QUERY_STEP), jnp.float32),
                jnp.zeros((HEAD_SIZE, QUERY_STEP), jnp.float32),
            )
            for _ in range(GROUP)
        )
        last = lax.fori_loop(low[tile], high[tile], step, first)
        pieces = []
        for h in range(GROUP):
            highest, total, summed = last[h]
            log_ref[h : h + 1, rows] = highest + jnp.log(total)
            summed = summed / total
            outt_ref[h, :, rows] = summed
            pieces.append(summed)
        out_ref[rows, :] = jnp.concatenate(pieces, axis=0).T.astype(jnp.bfloat16)


def attend_back_kernel(
    low, high, pos_ref, start_ref, query_ref, kv_ref, kvt_ref, outt_ref, log_ref, grad_ref,
    grad_query_ref, grad_kv_ref, sums,
):
    zeros = jnp.zeros((QUERY_STEP, HEAD_SIZE), jnp.bfloat16)
    sums[...] = jnp.zeros_like(sums)

    @pl.loop(0, query_ref.shape[0] // QUERY_STEP)
    def _(tile):
        rows = pl.ds(pl.multiple_of(tile * QUERY_STEP, QUERY_STEP), QUERY_STEP)
        pos, start = pos_ref[:, rows], start_ref[:, rows]
        queries, grads = query_ref[rows, :], grad_ref[rows, :]
        grads_t = grads.astype(jnp.float32).T
        query_pads, grad_pads, deltas, logs = [], [], [], []
        for h in range(GROUP):
            part = slice(h * HEAD_SIZE, (h + 1) * HEAD_SIZE)
            query_pads.append(jnp.concatenate([queries[:, part], zeros], axis=1))
            grad_pads.append(jnp.concatenate([zeros, grads[:, part]], axis=1))
            deltas.append(jnp.sum(grads_t[part, :] * outt_ref[h, :, rows], axis=0, keepdims=True))
            logs.append(log_ref[h : h + 1, rows])

        def step(block, carry):
            keys = pl.ds(pl.multiple_of(block * KEY_STEP, KEY_STEP), KEY_STEP)
            kv = kv_ref[keys, :]
            keys_t = kvt_ref[:HEAD_SIZE, keys]
            allowed = allowed_block(block, pos, start)
            new = []
            total = sums[keys, :]
            for h in range(GROUP):
                scores = jnp.where(allowed, across(kv, query_pads[h]), NEGATIVE)
                probs = jnp.exp(scores - logs[h])
                grad_probs = across(kv, grad_pads[h])
                grad_scores = (probs * (grad_probs - deltas[h])).astype(jnp.bfloat16)
                total += dot32(probs.astype(jnp.bfloat16), grad_pads[h])
                total += dot32(grad_scores, query_pads[h])
                new.append(carry[h] + dot32(keys_t, grad_scores))
            sums[keys, :] = total
            return tuple(new)

        first = tuple(jnp.zeros((HEAD_SIZE, QUERY_STEP), jnp.float32) for _ in range(GROUP))
        last = lax.fori_loop(low[tile], high[tile], step, first)
        factor = HEAD_SIZE ** (-0.5)
        grad_query_ref[rows, :] = (jnp.concatenate(last, axis=0) * factor).T.astype(jnp.bfloat16)

    grad_kv_ref[...] = sums[...].astype(jnp.bfloat16)


def attend_call(kernel, name, bounds, arrays, out_shape, scratch, matmuls, area):
    vmem = pl.BlockSpec(memory_space=pltpu.VMEM)
    return pl.pallas_call(
        kernel,
        out_shape=out_shape,
        grid_spec=pltpu.PrefetchScalarGridSpec(
            num_scalar_prefetch=2,
            grid=(1,),
            in_specs=[vmem] * len(arrays),
            out_specs=[vmem] * len(out_shape),
            scratch_shapes=scratch,
        ),
        compiler_params=pltpu.CompilerParams(vmem_limit_bytes=32 * 2**20),
        cost_estimate=pl.CostEstimate(
            flops=matmuls * 2 * HEAD_SIZE * area, bytes_accessed=8 * 2**20, transcendentals=area
        ),
        name=name,
    )(*bounds, *arrays)


def shards(
    tokens,
    segments,
    routes,
    gain_attn,
    w_query,
    key_weight,
    value_weight,
    w_out,
    w_router,
    gain_ffn,
    w_gate,
    w_up,
    w_down,
    cotangent,
):
    low = jnp.bfloat16
    wide = jnp.float32
    device_rows, width = tokens.shape
    sequence = segments.shape[0]
    half = device_rows // 2
    core = lax.axis_index("ctx") % 2
    ctx_count = lax.axis_size("ctx")
    slice_rows = w_query.shape[0]
    kv_shards = jnp.stack(
        [
            key_weight.reshape(slice_rows, KEY_VALUE_HEADS, HEAD_SIZE),
            value_weight.reshape(slice_rows, KEY_VALUE_HEADS, HEAD_SIZE),
        ],
        axis=2,
    ).reshape(slice_rows, 2 * KEY_VALUE_HEADS * HEAD_SIZE)
    shard = jnp.concatenate(
        [w_query, kv_shards, w_out, w_router, gain_attn[:, None], gain_ffn[:, None]], axis=1
    )
    shard = jnp.pad(shard, ((0, 0), (0, PACK - shard.shape[1])))
    packed, expert_weights, head_queries, head_kv, scales = gather_weights(
        shard, tokens, w_gate[0], w_up[0], w_down[0]
    )
    head_queries = head_queries.reshape(-1, HEADS_WIDE)
    head_kv = head_kv.reshape(sequence, 2 * HEAD_SIZE)
    order = jnp.arange(ctx_count * half, dtype=jnp.int32)
    query_pos = (order // half) * device_rows + core * half + order % half
    first_of = jnp.sum(
        (segments[:, None] < jnp.arange(5, dtype=jnp.int32)[None, :]).astype(jnp.int32), axis=0
    )
    starts = jnp.sum(
        jnp.where(segments[:, None] == jnp.arange(5, dtype=jnp.int32)[None, :], first_of[None, :], 0),
        axis=1,
    )
    query_start = lax.dynamic_slice_in_dim(
        starts.reshape(ctx_count, device_rows), core * half, half, axis=1
    ).reshape(-1)
    tiles = query_pos.reshape(-1, QUERY_STEP)
    bounds = (
        query_start.reshape(-1, QUERY_STEP)[:, 0] // KEY_STEP,
        tiles[:, -1] // KEY_STEP + 1,
    )
    mask_rows = (query_pos[None, :], query_start[None, :])

    head_kvt = head_kv.T
    count = head_queries.shape[0]
    area = GROUP * count * sequence // 3
    head_out, head_outt, log_total = attend_call(
        attend_kernel,
        "attend",
        bounds,
        (*mask_rows, head_queries, head_kv, head_kvt),
        (
            jax.ShapeDtypeStruct((count, HEADS_WIDE), low),
            jax.ShapeDtypeStruct((GROUP, HEAD_SIZE, count), wide),
            jax.ShapeDtypeStruct((GROUP, count), wide),
        ),
        [],
        2,
        area,
    )
    (
        attended, mixed, grad_hidden_one, grad_branch, grad_router_full, grad_gain_two, head_grads,
        *expert_grads,
    ) = run_middle(head_out, tokens, cotangent, routes, scales[1], packed, expert_weights)
    head_grads = head_grads.reshape(-1, HEADS_WIDE)

    head_grad_queries, head_grad_kv = attend_call(
        attend_back_kernel,
        "attend_back",
        bounds,
        (*mask_rows, head_queries, head_kv, head_kvt, head_outt, log_total, head_grads),
        (
            jax.ShapeDtypeStruct((count, HEADS_WIDE), low),
            jax.ShapeDtypeStruct((sequence, 2 * HEAD_SIZE), low),
        ),
        [pltpu.VMEM((sequence, 2 * HEAD_SIZE), wide)],
        5,
        area,
    )
    grad_input, out_share, share, (grad_gate, grad_up, grad_down) = scatter_sum(
        head_grad_queries, head_grad_kv, tokens, scales, grad_hidden_one, grad_branch, attended,
        grad_router_full, grad_gain_two, packed, expert_grads,
    )
    share, out_share = share.astype(wide), out_share.astype(wide)
    kv_share = share[:, 1536:2560].reshape(slice_rows, KEY_VALUE_HEADS, 2, HEAD_SIZE)
    return (
        mixed,
        grad_input,
        share[:, 2576],
        share[:, :1536],
        kv_share[:, :, 0].reshape(slice_rows, -1),
        kv_share[:, :, 1].reshape(slice_rows, -1),
        out_share,
        share[:, 2560:2576],
        share[:, 2577],
        grad_gate[None],
        grad_up[None],
        grad_down[None],
    )


def solution(mesh):
    in_specs = (
        P(("dp", "ctx"), None),
        P("dp"),
        P(("dp", "ctx"), None),
        P(("dp", "ctx")),
        P(("dp", "ctx"), None),
        P(("dp", "ctx"), None),
        P(("dp", "ctx"), None),
        P(("dp", "ctx"), None),
        P(("dp", "ctx"), None),
        P(("dp", "ctx")),
        P("ctx", "dp", None),
        P("ctx", "dp", None),
        P("ctx", "dp", None),
        P(("dp", "ctx"), None),
    )
    out_specs = (
        P(("dp", "ctx"), None),
        P(("dp", "ctx"), None),
        P(("dp", "ctx")),
        P(("dp", "ctx"), None),
        P(("dp", "ctx"), None),
        P(("dp", "ctx"), None),
        P(("dp", "ctx"), None),
        P(("dp", "ctx"), None),
        P(("dp", "ctx")),
        P("ctx", "dp", None),
        P("ctx", "dp", None),
        P("ctx", "dp", None),
    )
    return jax.shard_map(shards, mesh=mesh, in_specs=in_specs, out_specs=out_specs, check_vma=False)
```

time: 546 us -> 476 us (0.87)
  matrix products: 24.3 us -> 0 us
  Pallas kernels: 459 us -> 440 us
  other arithmetic: 26.8 us -> 9.3 us
    pallas_call x6 -> x2, Pallas kernels: 311 us -> 272 us  [the longest x1 140 us: run_middle(): pl.pallas_call(middle_kernel, out_shape=(jax.ShapeDtypeStruct((rows, widt...]
    pallas_call x1, Pallas kernels: 82.5 us -> 108 us  [gather_weights(): pl.pallas_call(gather_kernel, out_shape=[jax.ShapeDtypeStruct((4, 2, 2, 2...]
    dot_general x7 -> x0, matrix products: 24.3 us -> none  [the longest x3 14.1 us: contract_cols(): lax.dot_general(left, right, (((1,), (1,)), ((), ())), preferred_element_...]
    convert_element_type x21 -> x2, other arithmetic: 13.5 us -> 2.47 us  [shards(): share, out_share = (share.astype(wide), out_share.astype(wide))]
    unnamed x48 -> x29, local copies, waits for them, and re-layouts: 5.98 us -> 12.5 us
    pallas_call x2, Pallas kernels: 66.2 us -> 60.4 us  [attend_call(): pl.pallas_call(kernel, out_shape=out_shape, grid_spec=pltpu.PrefetchScala...]
where the time goes in v3:
time: 476 us; the launch traced here: 474 us
  Pallas kernels  440 us (92%)
  local copies, waits for them, and re-layouts  24.3 us (5%)
  other arithmetic  9.3 us (2%)
    pallas_call x1, Pallas kernels, run_middle(): pl.pallas_call(middle_kernel, out_shape=(jax.ShapeDtypeStruct((rows, widt...  140 us
    pallas_call x1, Pallas kernels, scatter_sum(): pl.pallas_call(scatter_kernel, out_shape=[jax.ShapeDtypeStruct((rows, wid...  132 us
    pallas_call x1, Pallas kernels, gather_weights(): pl.pallas_call(gather_kernel, out_shape=[jax.ShapeDtypeStruct((4, 2, 2, 2...  108 us
    pallas_call x2, Pallas kernels, attend_call(): pl.pallas_call(kernel, out_shape=out_shape, grid_spec=pltpu.PrefetchScala...  60.4 us
    unnamed x29, local copies, waits for them, and re-layouts  12.5 us

profile of v3, /device:TPU:1, one launch (start us, length us, event | category | flops | bytes accessed | tf_op | source)
XLA Modules:
  0.0 474.4 jit_solution(3137979849632665770)
XLA Ops:
  0.7 0.8 convert_reduce_fusion
  1.5 0.7 copy.57
  2.3 0.8 copy.58
  3.1 0.8 select_reduce_fusion
  3.9 0.1 reshape.116
  3.9 0.1 constant_dynamic-slice_fusion
  4.0 0.1 broadcast_in_dim_reshape.3.start_ref
  4.1 0.1 reshape_reshape.3
  4.2 0.1 slice_reduce_fusion.4
  4.3 0.8 stack_reshape.8
  5.1 0.8 stack_reshape.9
  5.9 0.1 pad_maximum_fusion
  6.1 0.1 reshape.117
  6.2 0.9 concatenate.3
  7.1 0.7 pad.12.shard
  7.8 1.4 copy.60.routes
  9.2 0.1 multiply_add_fusion
  9.3 107.8 %gather_weights.1 = (bf16[4,2,2,2,48,4608]{5,4,3,2,1,0:T(8,128)(2,1)}, bf16[1536,1024]{1,0:T(8,128)(2,1)}, bf16[1536,1024]{1,0:T(8,128)(2,1)}, bf16[1024,1536]{1...) custom-call(bf16[16,4608]{1,0:T(8,128)(2,1)} %pad.12.shard, ...), custom_call_target="tpu_custom_call" | custom-call | flops 1509949440 | bytes 41943040 | tf_op jit(solution)/shard_map/gather_weights/pallas_call | solution.py:419
  117.2 1.4 slice.38.scale
  118.6 1.4 copy.59
  120.0 1.1 copy-done
  121.1 1.1 copy-done.4
  122.2 31.6 %attend.1 = (bf16[1536,192]{1,0:T(8,128)(2,1)S(1)}, f32[3,64,1536]{2,1,0:T(8,128)S(1)}, f32[3,1536]{1,0:T(4,128)S(1)}) custom-call(s32[6]{0:T(128)S(1)} %and_select_fusion.5.low, s32[6]{0:T(128)S(1)} %fusion.6.high, s32[1,1536]{1,0:T(1,128)S(1)} %fusion.2.pos_ref, s32[1,1536]{1,0:T(1,128)S(1)} %broadcast_in_dim_reshape.3.start_ref, ...), custom_call_target="tpu_custom_call" | custom-call | flops 1207959552 | bytes 8388608 | tf_op jit(solution)/shard_map/attend/pallas_call | solution.py:1541
  153.8 0.0 copy-start.7
  153.9 0.9 copy-done.7
  154.7 1.0 copy-done.8
  155.7 140.2 %run_middle.1 = (bf16[192,1536]{1,0:T(8,128)(2,1)}, bf16[192,1536]{1,0:T(8,128)(2,1)}, f32[192,1536]{1,0:T(8,128)}, bf16[192,1536]{1,0:T(8,128)(2,1)}, bf16[1536...) custom-call(bf16[16,96,192]{2,1,0:T(8,128)(2,1)} %bitcast.43, ...), custom_call_target="tpu_custom_call" | custom-call | flops 16307453952 | bytes 41943040 | tf_op jit(solution)/shard_map/run_middle/pallas_call | solution.py:1373
  296.0 1.1 copy-done.5
  297.1 1.1 copy-done.6
  298.3 1.3 copy-done.9
  299.5 28.8 %attend_back.1 = (bf16[1536,192]{1,0:T(8,128)(2,1)S(1)}, bf16[3072,128]{1,0:T(8,128)(2,1)S(1)}) custom-call(s32[6]{0:T(128)S(1)} %and_select_fusion.5.low, s32[6]{0:T(128)S(1)} %fusion.6.high, s32[1,1536]{1,0:T(1,128)S(1)} %fusion.2.pos_ref, s32[1,1536]{1,0:T(1,128)S(1)} %broadcast_in_dim_reshape.3.start_ref, bf16[1536,192]{1,0:T(8,128)(2,1)S(1)} %bitcast.41, ...), custom_call_target="tpu_custom_call" | custom-call | flops 3019898880 | bytes 8388608 | tf_op jit(solution)/shard_map/attend_back/pallas_call | solution.py:1541
  328.3 0.9 copy-done.2
  329.2 0.9 copy-done.3
  330.1 131.6 %scatter_sum.1 = (bf16[192,1536]{1,0:T(8,128)(2,1)}, bf16[16,1536]{1,0:T(8,128)(2,1)}, bf16[16,3072]{1,0:T(8,128)(2,1)}, bf16[192,1024]{1,0:T(8,128)(2,1)}, bf16...) custom-call(bf16[16,96,192]{2,1,0:T(8,128)(2,1)} %bitcast.38, bf16[16,192,128]{2,1,0:T(8,128)(2,1)} %bitcast.39, ...), custom_call_target="tpu_custom_call" | custom-call | flops 3925868544 | bytes 29360128 | tf_op jit(solution)/shard_map/scatter_sum/pallas_call | solution.py:872
  461.7 1.6 slice_convert_fusion.1
  463.3 0.9 slice_convert_fusion
  464.2 0.7 slice_reduce_fusion.2
  464.9 0.6 slice.57
  465.5 0.6 slice.53
  466.1 0.1 reshape.125
  466.3 0.3 slice_reduce_fusion
  466.5 0.7 reshape_squeeze.7
  467.2 0.7 reshape_squeeze.6
  467.9 2.0 bitcast_convert_fusion.2
  469.9 2.0 bitcast_convert_fusion.1
  471.8 1.0 bitcast_convert_fusion
  472.8 0.8 copy.63
  473.6 0.8 copy.64
  (21 shorter events, 0.1 us)
Async XLA Ops:
  120.0 1.1 copy-start
  121.1 1.1 copy-start.4
  153.8 0.9 copy-start.7
  154.7 1.0 copy-start.8
  155.7 140.2 %copy-start.1 = (bf16[16,192,128]{2,1,0:T(8,128)(2,1)S(1)}, bf16[16,192,128]{2,1,0:T(8,128)(2,1)}, u32[]{:S(2)}) copy-start(bf16[16,192,128]{2,1,0:T(8,128)(2,1)} %get-tuple-element.41) | copy-start | bytes 2359300
  296.0 1.1 copy-start.5
  297.1 1.1 copy-start.6
  298.3 1.3 copy-start.9
  328.3 0.9 copy-start.2
  329.2 0.9 copy-start.3
  461.7 10.1 %copy-start.12 = (bf16[128,1536]{1,0:T(8,128)(2,1)S(1)}, bf16[128,1536]{1,0:T(8,128)(2,1)}, u32[]{:S(2)}) copy-start(bf16[128,1536]{1,0:T(8,128)(2,1)} %get-tuple-element.67) | copy-start | bytes 1179652
  461.7 11.1 %copy-start.10 = (bf16[192,1536]{1,0:T(8,128)(2,1)S(1)}, bf16[192,1536]{1,0:T(8,128)(2,1)}, u32[]{:S(2)}) copy-start(bf16[192,1536]{1,0:T(8,128)(2,1)} %get-tuple-element.86) | copy-start | bytes 1769476
  461.7 11.9 %copy-start.11 = (bf16[192,1536]{1,0:T(8,128)(2,1)S(1)}, bf16[192,1536]{1,0:T(8,128)(2,1)}, u32[]{:S(2)}) copy-start(bf16[192,1536]{1,0:T(8,128)(2,1)} %get-tuple-element.87) | copy-start | bytes 1769476

commit v4 on v3

--- a/solution.py
+++ b/solution.py
@@ -66,7 +66,7 @@
     return [(step, (ctx + step) % SOURCES) for step in range(1, SOURCES)]
 
 
-def meet(spot, heads):
+def meet(spot, heads, picks=()):
     barrier = pltpu.get_barrier_semaphore()
     others = [member(spot, step)[0] for step in (1, 2, 3)] + [partner(spot)]
     others += [moved(spot, axis, step) for axis in "xyz" for step in (1, 2, 3)]
@@ -74,7 +74,20 @@
     others += [(lax.axis_index("dp"), other) for _, other in heads]
     for other in others:
         pl.semaphore_signal(barrier, inc=1, device_id=other, device_id_type=MESH)
-    pl.semaphore_wait(barrier, len(others))
+    for pick in picks:
+        for step in range(1, SOURCES):
+            pl.semaphore_signal(barrier, inc=1, device_id=pick(step)[1], device_id_type=MESH)
+
+    if picks:
+
+        @pl.when(spot["z"] % 2 != spot["core"])
+        def _():
+            for pick in picks:
+                pl.semaphore_signal(barrier, inc=1, device_id=pick(0)[1], device_id_type=MESH)
+
+    away = (spot["z"] + spot["core"]) % 2
+    amount = len(others) + len(picks) * (SOURCES - 1)
+    pl.semaphore_wait(barrier, amount + len(picks) * away if picks else amount)
 
 
 def region(spot, known, part, base):
@@ -130,16 +143,18 @@
 
 
 def gather_kernel(
-    shard, merge, tokens, own_gate, own_up, own_down,
-    out, gate_out, up_out, down_out, head_rows, head_kv, scales,
+    shard, merge, tokens, cotangent, routes_t, own_gate, own_up, own_down,
+    out, gate_out, up_out, down_out, head_rows, head_kv, scales, c_main_in, c_rest_in,
     pieces, joined, qkv_w, rest_w, normed, qkv, packed,
     send0, recv0, send, recv, send_core, recv_core, local,
     swap_send, swap_recv, swap_local, line_send, line_recv, mate_send, mate_recv, ring_send, ring_recv,
     head_send, head_recv, head_local,
+    send_main, send_rest, c_main, c_rest, route_send, route_recv,
 ):
     spot = place()
     dp, ctx = lax.axis_index("dp"), lax.axis_index("ctx")
-    meet(spot, others_of(ctx))
+    holder, sender, start = expert_routes(dp, ctx, route_send, route_recv)
+    meet(spot, others_of(ctx), (holder, sender))
     mate = moved(spot, "core", 1)
     stays = spot["core"] == spot["z"] % 2
     experts = ((own_gate, gate_out), (own_up, up_out), (own_down, down_out))
@@ -217,6 +232,8 @@
         copy.start()
         copies.append(copy)
     pieces[index] = shard[:, pl.ds(pl.multiple_of(quarter * QUARTER, 128), QUARTER)]
+    fill_tables(routes_t, send_main, send_rest)
+    pack((send_main, send_rest), cotangent, c_main, c_rest)
     for copy in copies:
         copy.wait()
     joined[...] = jnp.dot(
@@ -313,6 +330,7 @@
     for first, _ in lines:
         start_all(first)
     own_mates = to_mates(0)
+    flights = start(0, holder, ctx, c_main, c_rest, c_main_in, c_rest_in)
     for part, (axis, _) in enumerate(finals):
         for step in (1, 3):
             to_mate(part * 4 + step, region(moved(spot, axis, 4 - step), RING_ORDERS[part][:2], part, base))
@@ -393,6 +411,8 @@
     line_copies = [copy for first, second in lines + relays for copy in first + second]
     for copy in own_heads + head_copies:
         copy.wait()
+    flights[0]()
+    flights[1]()
     for copy in copies[3:] + line_copies:
         copy.wait_send()
     for copy in core_copies:
@@ -401,7 +421,7 @@
         copy.wait()
 
 
-def gather_weights(shard, tokens, gate, up, down):
+def gather_weights(shard, tokens, cotangent, routes, gate, up, down):
     shard = jnp.pad(shard, ((0, 4), (0, 0)))
     target, source = np.arange(48)[:, None], np.arange(64)[None, :]
     merge = jnp.asarray(
@@ -424,9 +444,11 @@
             jax.ShapeDtypeStruct((SOURCES, rows // 2, HEADS_WIDE), low),
             jax.ShapeDtypeStruct((SOURCES, rows, 2 * HEAD_SIZE), low),
             jax.ShapeDtypeStruct((8, width), jnp.float32),
+            jax.ShapeDtypeStruct((SOURCES, MAIN_ROWS, width), low),
+            jax.ShapeDtypeStruct((SOURCES, REST_ROWS, REST_WIDTH), low),
         ],
-        in_specs=[vmem] * 3 + [anywhere] * 3,
-        out_specs=[anywhere] * 4 + [vmem] * 3,
+        in_specs=[vmem] * 5 + [anywhere] * 3,
+        out_specs=[anywhere] * 4 + [vmem] * 5,
         scratch_shapes=[
             pltpu.VMEM((4, 16, QUARTER), low),
             pltpu.VMEM((48, QUARTER), low),
@@ -439,6 +461,11 @@
             dma((3,)), dma((3,)), dma((3,)), dma((12,)), dma((12,)), dma((12,)), dma((12,)),
             dma((12,)), dma((12,)),
             dma((2 * SOURCES,)), dma((2 * SOURCES,)), dma((4,)),
+            pltpu.VMEM((SOURCES * MAIN_ROWS, rows), low),
+            pltpu.VMEM((4, SOURCES * REST_ROWS, rows), low),
+            pltpu.VMEM((SOURCES, MAIN_ROWS, width), low),
+            pltpu.VMEM((SOURCES, REST_ROWS, REST_WIDTH), low),
+            dma((2 * SOURCES,)), dma((2 * SOURCES,)),
         ],
         compiler_params=pltpu.CompilerParams(
             collective_id=1, has_side_effects=True, vmem_limit_bytes=62 * 2**20
@@ -447,12 +474,13 @@
             flops=2 * rows * width * qkv_width, bytes_accessed=40 * 2**20, transcendentals=0
         ),
         name="gather_weights",
-    )(shard, merge, tokens, gate, up, down)
+    )(shard, merge, tokens, cotangent, routes.T, gate, up, down)
     return packed.reshape(1536, PACK), rest[:3], *rest[3:]
 
 
 EARLY = 1536
-SCATTER_ORDERS = (("x", "y", "z"), ("y", "z", "x"), ("z", "x", "y"))
+EARLY_ORDERS = (("y", "z", "x"), ("y", "x", "z"), ("y", "z", "x"))
+LATE_ORDERS = (("y", "z", "x"), ("y", "x", "z"), ("y", "x", "z"))
 
 
 def cut(spot, known, part, half):
@@ -486,9 +514,10 @@
 
 
 class Scatter:
-    def __init__(self, spot, split, grads, total, done, packed, out, sems, landing):
+    def __init__(self, orders, spot, split, grads, total, done, packed, out, sems, landing):
         self.spot, self.split, self.grads, self.total, self.out = spot, split, grads, total, out
         self.done, self.packed = done, packed
+        self.orders = orders
         self.send_core, self.recv_core, self.send, self.recv, self.send_last, self.recv_last = sems
         self.landing = (landing[:3], landing[3:6], landing[6:9])
         self.half = total.shape[-1]
@@ -528,7 +557,7 @@
             self.pending.append(self.ring(part, 0))
 
     def ring(self, part, stage):
-        axis, known = SCATTER_ORDERS[part][2 - stage], SCATTER_ORDERS[part][: 2 - stage]
+        axis, known = self.orders[part][2 - stage], self.orders[part][: 2 - stage]
         started = []
         for step in (1, 3, 2):
             other = moved(self.spot, axis, step)
@@ -548,7 +577,7 @@
 
     def next(self, stage):
         for part in range(3):
-            known = SCATTER_ORDERS[part][: 2 - stage]
+            known = self.orders[part][: 2 - stage]
             for copy in self.pending[part]:
                 copy.wait_recv()
             self.add(known, part, self.landing[stage][part])
@@ -635,8 +664,8 @@
     spot = place()
     dp, ctx = lax.axis_index("dp"), lax.axis_index("ctx")
     held, mates, lines, results, arrived = (buffers[3 * n : 3 * n + 3] for n in range(5))
-    early = Scatter(spot, split, *buffers[15:19], out, buffers[19:25], buffers[25:34])
-    late = Scatter(spot, split, *buffers[34:38], late_out, buffers[38:44], buffers[44:])
+    early = Scatter(EARLY_ORDERS, spot, split, *buffers[15:19], out, buffers[19:25], buffers[25:34])
+    late = Scatter(LATE_ORDERS, spot, split, *buffers[34:38], late_out, buffers[38:44], buffers[44:])
     wholes, finals = (grad_gate, grad_up, grad_down), (gate_out, up_out, down_out)
     mate = moved(spot, "core", 1)
     qkv_width = grad_qkv.shape[1]
@@ -773,19 +802,19 @@
         (4, 2, 2, 2, 48, late.grads.shape[-1] - at - 128), jnp.bfloat16
     )
     late.start()
-    early.next(0)
     grads_here = grad_normed[...] * scale
     grads_here = inverse * (
         grads_here - unit * jnp.mean(grads_here * unit, axis=1, keepdims=True)
     )
     grad_input[...] = (grads_here + grad_hidden[...]).astype(jnp.bfloat16)
     late.first()
+    early.next(0)
     early.next(1)
+    early.next(2)
+    early.finish()
+    late.next(0)
     sum_lines(spot, held, lines, line_copies, results)
     swap_results(spot, results, arrived, swap_send, swap_recv, True)
-    late.next(0)
-    early.next(2)
-    early.finish()
     late.next(1)
     late.next(2)
     late.finish()
@@ -850,7 +879,7 @@
     buffers = [pltpu.VMEM((4,) + block, low) for block in blocks] * 2
     buffers += [pltpu.VMEM((3,) + block, low) for block in blocks]
     buffers += [pltpu.VMEM(block, low) for block in blocks] * 2
-    for columns in (EARLY, PACK - EARLY):
+    for columns, orders in ((EARLY, EARLY_ORDERS), (PACK - EARLY, LATE_ORDERS)):
         buffers += [
             pltpu.VMEM((4, 2, 2, 2, 48, columns), low),
             pltpu.VMEM((4, 2, 2, 2, 48, columns // 2), low),
@@ -861,7 +890,7 @@
         buffers += [
             pltpu.VMEM((3,) + landing_shape(order[: 2 - stage], columns // 2), low)
             for stage in range(3)
-            for order in SCATTER_ORDERS
+            for order in orders
         ]
     vmem = pl.BlockSpec(memory_space=pltpu.VMEM)
     anywhere = pl.BlockSpec(memory_space=pltpu.HBM)
@@ -982,8 +1011,113 @@
     return places
 
 
+def expert_routes(dp, ctx, send, recv):
+    y, z_lo, core = dp // 2, dp % 2, ctx % 2
+    expert = ctx // 2 * 2 + z_lo
+    at_home = z_lo == core
+
+    def holder(step):
+        other = (ctx + step) % SOURCES
+        return other, (2 * y + other % 2, other // 2 * 2 + z_lo)
+
+    def sender(step):
+        other = (expert + step) % SOURCES
+        return other, (2 * y + core, other)
+
+    def start(number, pick, slot, main, rest, main_in, rest_in):
+        copies = []
+        pairs = ((main, main_in), (rest, rest_in))
+
+        def remote(step, which):
+            other, device = pick(step)
+            src, dst = pairs[which]
+            at = (number * 2 + which) * SOURCES + step
+            return pltpu.make_async_remote_copy(
+                src_ref=src.at[other],
+                dst_ref=dst.at[slot],
+                send_sem=send.at[at],
+                recv_sem=recv.at[at],
+                device_id=device,
+                device_id_type=MESH,
+            )
+
+        def local(which):
+            src, dst = pairs[which]
+            at = (number * 2 + which) * SOURCES
+            return pltpu.make_async_copy(src.at[slot], dst.at[slot], recv.at[at])
+
+        for step in range(1, SOURCES):
+            for which in range(2):
+                copy = remote(step, which)
+                copy.start()
+                copies.append(copy)
+
+        @pl.when(at_home)
+        def _():
+            for which in range(2):
+                local(which).start()
+
+        @pl.when(jnp.logical_not(at_home))
+        def _():
+            for which in range(2):
+                remote(0, which).start()
+
+        def wait_recv():
+            @pl.when(at_home)
+            def _():
+                for which in range(2):
+                    local(which).wait()
+
+            @pl.when(jnp.logical_not(at_home))
+            def _():
+                for which in range(2):
+                    remote(0, which).wait_recv()
+
+            for copy in copies:
+                copy.wait_recv()
+
+        def wait_send():
+            @pl.when(jnp.logical_not(at_home))
+            def _():
+                for which in range(2):
+                    remote(0, which).wait_send()
+
+            for copy in copies:
+                copy.wait_send()
+
+        return wait_recv, wait_send
+
+    return holder, sender, start
+
+
+def pack(tables, source, main, rest):
+    send_main, send_rest = tables
+    main[...] = dot32(send_main[...], source[...]).astype(jnp.bfloat16).reshape(main.shape)
+    total = jnp.zeros((SOURCES * REST_ROWS, REST_WIDTH), jnp.float32)
+    for quarter in range(4):
+        total += dot32(
+            send_rest[quarter], source[:, quarter * REST_WIDTH : (quarter + 1) * REST_WIDTH]
+        )
+    rest[:, :, :REST_WIDTH] = (
+        total.astype(jnp.bfloat16).reshape(SOURCES, REST_ROWS, REST_WIDTH)
+    )
+
+
+def fill_tables(routes_t, send_main, send_rest):
+    rows = routes_t.shape[1]
+    main_rows = lax.broadcasted_iota(jnp.int32, (SOURCES * MAIN_ROWS, rows), 0)
+    rest_rows = lax.broadcasted_iota(jnp.int32, (SOURCES * REST_ROWS, rows), 0)
+    places = place_rows([routes_t[c : c + 1, :] for c in range(TOP)], 1)
+    send_main[...] = ones_at((main_rows == places[0][0]) | (main_rows == places[1][0]))
+    for quarter in range(4):
+        send_rest[quarter] = ones_at(
+            (rest_rows == places[0][1] + 4 * quarter) | (rest_rows == places[1][1] + 4 * quarter)
+        )
+    return rest_rows, places
+
+
 def middle_kernel(
-    head_out, tokens, cotangent, routes, routes_t, scale,
+    head_out, tokens, cotangent, c_main_in, c_rest_in, routes, routes_t, scale,
     from_main, to_main, from_rest, to_rest, from_gate, to_gate, lane_mask,
     packed_w, gate_src, up_src, down_src,
     attended, mixed, grad_hidden, grad_branch, router_grad, gain_grad, head_grads,
@@ -991,7 +1125,7 @@
     gate_w, up_w, down_w, out_w, router_w,
     rows_in, head_send, hidden_one, normed, grad_normed,
     send_main, send_rest, send_gate, place_main, place_rest, place_gate,
-    x_main, x_rest, c_main, c_rest, x_main_in, x_rest_in, c_main_in, c_rest_in,
+    x_main, x_rest, c_main, c_rest, x_main_in, x_rest_in,
     d_main_in, d_rest_in, y_main_in, y_rest_in,
     rows_x, rows_c, gate_pre, up_pre, hidden, grad_gate_pre, grad_up_pre, rows_y, turned,
     weight_sem, out_sem, swap_send, swap_recv, send, recv,
@@ -1015,17 +1149,9 @@
     ]
     for load in loads:
         load.start()
-    y, z_lo, core = dp // 2, dp % 2, ctx % 2
+    z_lo, core = dp % 2, ctx % 2
     expert = ctx // 2 * 2 + z_lo
-    at_home = z_lo == core
-
-    def holder(step):
-        other = (ctx + step) % SOURCES
-        return other, (2 * y + other % 2, other // 2 * 2 + z_lo)
-
-    def sender(step):
-        other = (expert + step) % SOURCES
-        return other, (2 * y + core, other)
+    holder, sender, start = expert_routes(dp, ctx, send, recv)
 
     def neighbour(step):
         other = (ctx + step) % SOURCES
@@ -1036,73 +1162,10 @@
         for pick in (neighbour, holder, sender):
             pl.semaphore_signal(barrier, inc=1, device_id=pick(step)[1], device_id_type=MESH)
 
-    @pl.when(jnp.logical_not(at_home))
+    @pl.when(z_lo != core)
     def _():
         for pick in (holder, sender):
             pl.semaphore_signal(barrier, inc=1, device_id=pick(0)[1], device_id_type=MESH)
-
-    def start(number, pick, slot, main, rest, main_in, rest_in):
-        copies = []
-        pairs = ((main, main_in), (rest, rest_in))
-
-        def remote(step, which):
-            other, device = pick(step)
-            src, dst = pairs[which]
-            at = (number * 2 + which) * SOURCES + step
-            return pltpu.make_async_remote_copy(
-                src_ref=src.at[other],
-                dst_ref=dst.at[slot],
-                send_sem=send.at[at],
-                recv_sem=recv.at[at],
-                device_id=device,
-                device_id_type=MESH,
-            )
-
-        def local(which):
-            src, dst = pairs[which]
-            at = (number * 2 + which) * SOURCES
-            return pltpu.make_async_copy(src.at[slot], dst.at[slot], recv.at[at])
-
-        for step in range(1, SOURCES):
-            for which in range(2):
-                copy = remote(step, which)
-                copy.start()
-                copies.append(copy)
-
-        @pl.when(at_home)
-        def _():
-            for which in range(2):
-                local(which).start()
-
-        @pl.when(jnp.logical_not(at_home))
-        def _():
-            for which in range(2):
-                remote(0, which).start()
-
-        def wait_recv():
-            @pl.when(at_home)
-            def _():
-                for which in range(2):
-                    local(which).wait()
-
-            @pl.when(jnp.logical_not(at_home))
-            def _():
-                for which in range(2):
-                    remote(0, which).wait_recv()
-
-            for copy in copies:
-                copy.wait_recv()
-
-        def wait_send():
-            @pl.when(jnp.logical_not(at_home))
-            def _():
-                for which in range(2):
-                    remote(0, which).wait_send()
-
-            for copy in copies:
-                copy.wait_send()
-
-        return wait_recv, wait_send
 
     def swap(number, source, place_in):
         copies = []
@@ -1122,15 +1185,6 @@
         place_in[ctx] = source[ctx]
         return copies
 
-    def pack(source, main, rest):
-        main[...] = dot32(send_main[...], source[...]).astype(low).reshape(main.shape)
-        total = jnp.zeros((SOURCES * REST_ROWS, REST_WIDTH), wide)
-        for quarter in range(4):
-            total += dot32(
-                send_rest[quarter], source[:, quarter * REST_WIDTH : (quarter + 1) * REST_WIDTH]
-            )
-        rest[:, :, :REST_WIDTH] = total.astype(low).reshape(SOURCES, REST_ROWS, REST_WIDTH)
-
     def unpack(main_in, rest_in, out, group):
         at = pl.ds(4 * group, 4)
         main = main_in[at].reshape(4 * MAIN_ROWS, -1)
@@ -1156,14 +1210,7 @@
     pl.semaphore_wait(barrier, 3 * (SOURCES - 1) + 2 * ((z_lo + core) % 2))
     heads_in = swap(0, head_out, rows_in)
 
-    main_rows = lax.broadcasted_iota(jnp.int32, (SOURCES * MAIN_ROWS, rows), 0)
-    rest_rows = lax.broadcasted_iota(jnp.int32, (SOURCES * REST_ROWS, rows), 0)
-    places = place_rows([routes_t[c : c + 1, :] for c in range(TOP)], 1)
-    send_main[...] = ones_at((main_rows == places[0][0]) | (main_rows == places[1][0]))
-    for quarter in range(4):
-        send_rest[quarter] = ones_at(
-            (rest_rows == places[0][1] + 4 * quarter) | (rest_rows == places[1][1] + 4 * quarter)
-        )
+    rest_rows, places = fill_tables(routes_t, send_main, send_rest)
     for choice in range(TOP):
         send_gate[choice] = ones_at(rest_rows == places[choice][2])
     main_lanes = lax.broadcasted_iota(jnp.int32, (rows, SOURCES * MAIN_ROWS), 1)
@@ -1177,8 +1224,6 @@
             place_rest[choice, quarter] = ones_at(rest_lanes == rest + 4 * quarter)
         place_gate[choice] = ones_at(rest_lanes == gate)
         gate_lanes.append(jnp.where((lanes >= 3 * block) & (lanes < 3 * block + 3), 1.0, 0.0))
-    pack(cotangent, c_main, c_rest)
-    cotangent_flights = start(1, holder, ctx, c_main, c_rest, c_main_in, c_rest_in)
 
     for load in loads:
         load.wait()
@@ -1203,7 +1248,7 @@
     powers = [jnp.exp(value - highest) for value in chosen]
     gates = [power / (powers[0] + powers[1]) for power in powers]
 
-    pack(normed, x_main, x_rest)
+    pack((send_main, send_rest), normed, x_main, x_rest)
     total = jnp.zeros((SOURCES * REST_ROWS, 128), wide)
     for choice in range(TOP):
         carried = in_three(gates[choice], lanes) * gate_lanes[choice]
@@ -1227,8 +1272,6 @@
     def _(at):
         rows_y[:, at] = dot32(hidden[...], down_w[:, at]).astype(low)
 
-    cotangent_flights[0]()
-    cotangent_flights[1]()
     for group in range(4):
         repack(rows_y, c_main, c_rest, group)
     flights_y = start(3, sender, expert, c_main, c_rest, y_main_in, y_rest_in)
@@ -1357,7 +1400,7 @@
         copy.wait()
 
 
-def run_middle(head_out, tokens, cotangent, routes, scale, packed, weights):
+def run_middle(head_out, tokens, cotangent, cotangent_rows, routes, scale, packed, weights):
     rows, width = tokens.shape
     half = rows // 2
     hidden_width = weights[0].shape[-1]
@@ -1384,7 +1427,7 @@
             jax.ShapeDtypeStruct((width, hidden_width), low),
             jax.ShapeDtypeStruct((hidden_width, width), low),
         ),
-        in_specs=[vmem] * 13 + [anywhere] * 4,
+        in_specs=[vmem] * 15 + [anywhere] * 4,
         out_specs=[vmem] * 7 + [anywhere] * 3,
         scratch_shapes=[
             pltpu.VMEM((width, hidden_width), low),
@@ -1404,8 +1447,7 @@
             pltpu.VMEM((TOP, rows, SOURCES * MAIN_ROWS), low),
             pltpu.VMEM((TOP, 4, rows, SOURCES * REST_ROWS), low),
             pltpu.VMEM((TOP, rows, SOURCES * REST_ROWS), low),
-            main, long_rest, main, rest, main, long_rest, main, rest,
-            main, long_rest, main, rest,
+            main, long_rest, main, rest, main, long_rest, main, long_rest, main, rest,
             pltpu.VMEM((count, width), low),
             pltpu.VMEM((count, width), low),
             pltpu.VMEM((count, hidden_width), wide),
@@ -1426,17 +1468,18 @@
         ),
         name="run_middle",
     )(
-        head_out.reshape(SOURCES, half, HEADS_WIDE), tokens, cotangent, routes, routes.T, scale[None, :],
+        head_out.reshape(SOURCES, half, HEADS_WIDE), tokens, cotangent, *cotangent_rows, routes, routes.T,
+        scale[None, :],
         *unpack_tables(), packed, *weights,
     )
 
 
-KEY_STEP = 256
-QUERY_STEP = 256
-
-
-def allowed_block(block, pos, start):
-    keys = lax.broadcasted_iota(jnp.int32, (KEY_STEP, QUERY_STEP), 0) + block * KEY_STEP
+KEY_STEP, QUERY_STEP = 512, 128
+BACK_KEY_STEP, BACK_QUERY_STEP = 256, 256
+
+
+def allowed_block(block, pos, start, key_step):
+    keys = lax.broadcasted_iota(jnp.int32, (key_step, pos.shape[1]), 0) + block * key_step
     return (keys <= pos) & (keys >= start)
 
 
@@ -1457,7 +1500,7 @@
             keys = pl.ds(pl.multiple_of(block * KEY_STEP, KEY_STEP), KEY_STEP)
             kv = kv_ref[keys, :]
             values_t = kvt_ref[HEAD_SIZE:, keys]
-            allowed = allowed_block(block, pos, start)
+            allowed = allowed_block(block, pos, start, KEY_STEP)
             new = []
             for h in range(GROUP):
                 highest, total, summed = carry[h]
@@ -1493,12 +1536,12 @@
     low, high, pos_ref, start_ref, query_ref, kv_ref, kvt_ref, outt_ref, log_ref, grad_ref,
     grad_query_ref, grad_kv_ref, sums,
 ):
-    zeros = jnp.zeros((QUERY_STEP, HEAD_SIZE), jnp.bfloat16)
+    zeros = jnp.zeros((BACK_QUERY_STEP, HEAD_SIZE), jnp.bfloat16)
     sums[...] = jnp.zeros_like(sums)
 
-    @pl.loop(0, query_ref.shape[0] // QUERY_STEP)
+    @pl.loop(0, query_ref.shape[0] // BACK_QUERY_STEP)
     def _(tile):
-        rows = pl.ds(pl.multiple_of(tile * QUERY_STEP, QUERY_STEP), QUERY_STEP)
+        rows = pl.ds(pl.multiple_of(tile * BACK_QUERY_STEP, BACK_QUERY_STEP), BACK_QUERY_STEP)
         pos, start = pos_ref[:, rows], start_ref[:, rows]
         queries, grads = query_ref[rows, :], grad_ref[rows, :]
         grads_t = grads.astype(jnp.float32).T
@@ -1511,10 +1554,10 @@
             logs.append(log_ref[h : h + 1, rows])
 
         def step(block, carry):
-            keys = pl.ds(pl.multiple_of(block * KEY_STEP, KEY_STEP), KEY_STEP)
+            keys = pl.ds(pl.multiple_of(block * BACK_KEY_STEP, BACK_KEY_STEP), BACK_KEY_STEP)
             kv = kv_ref[keys, :]
             keys_t = kvt_ref[:HEAD_SIZE, keys]
-            allowed = allowed_block(block, pos, start)
+            allowed = allowed_block(block, pos, start, BACK_KEY_STEP)
             new = []
             total = sums[keys, :]
             for h in range(GROUP):
@@ -1528,7 +1571,7 @@
             sums[keys, :] = total
             return tuple(new)
 
-        first = tuple(jnp.zeros((HEAD_SIZE, QUERY_STEP), jnp.float32) for _ in range(GROUP))
+        first = tuple(jnp.zeros((HEAD_SIZE, BACK_QUERY_STEP), jnp.float32) for _ in range(GROUP))
         last = lax.fori_loop(low[tile], high[tile], step, first)
         factor = HEAD_SIZE ** (-0.5)
         grad_query_ref[rows, :] = (jnp.concatenate(last, axis=0) * factor).T.astype(jnp.bfloat16)
@@ -1591,8 +1634,8 @@
         [w_query, kv_shards, w_out, w_router, gain_attn[:, None], gain_ffn[:, None]], axis=1
     )
     shard = jnp.pad(shard, ((0, 0), (0, PACK - shard.shape[1])))
-    packed, expert_weights, head_queries, head_kv, scales = gather_weights(
-        shard, tokens, w_gate[0], w_up[0], w_down[0]
+    packed, expert_weights, head_queries, head_kv, scales, *cotangent_rows = gather_weights(
+        shard, tokens, cotangent, routes, w_gate[0], w_up[0], w_down[0]
     )
     head_queries = head_queries.reshape(-1, HEADS_WIDE)
     head_kv = head_kv.reshape(sequence, 2 * HEAD_SIZE)
@@ -1608,11 +1651,13 @@
     query_start = lax.dynamic_slice_in_dim(
         starts.reshape(ctx_count, device_rows), core * half, half, axis=1
     ).reshape(-1)
-    tiles = query_pos.reshape(-1, QUERY_STEP)
-    bounds = (
-        query_start.reshape(-1, QUERY_STEP)[:, 0] // KEY_STEP,
-        tiles[:, -1] // KEY_STEP + 1,
-    )
+
+    def bounds_of(query_step, key_step):
+        return (
+            query_start.reshape(-1, query_step)[:, 0] // key_step,
+            query_pos.reshape(-1, query_step)[:, -1] // key_step + 1,
+        )
+
     mask_rows = (query_pos[None, :], query_start[None, :])
 
     head_kvt = head_kv.T
@@ -1621,7 +1666,7 @@
     head_out, head_outt, log_total = attend_call(
         attend_kernel,
         "attend",
-        bounds,
+        bounds_of(QUERY_STEP, KEY_STEP),
         (*mask_rows, head_queries, head_kv, head_kvt),
         (
             jax.ShapeDtypeStruct((count, HEADS_WIDE), low),
@@ -1635,13 +1680,15 @@
     (
         attended, mixed, grad_hidden_one, grad_branch, grad_router_full, grad_gain_two, head_grads,
         *expert_grads,
-    ) = run_middle(head_out, tokens, cotangent, routes, scales[1], packed, expert_weights)
+    ) = run_middle(
+        head_out, tokens, cotangent, cotangent_rows, routes, scales[1], packed, expert_weights
+    )
     head_grads = head_grads.reshape(-1, HEADS_WIDE)
 
     head_grad_queries, head_grad_kv = attend_call(
         attend_back_kernel,
         "attend_back",
-        bounds,
+        bounds_of(BACK_QUERY_STEP, BACK_KEY_STEP),
         (*mask_rows, head_queries, head_kv, head_kvt, head_outt, log_total, head_grads),
         (
             jax.ShapeDtypeStruct((count, HEADS_WIDE), low),

time: 476 us -> 443 us (0.931)
  Pallas kernels: 440 us -> 406 us
    pallas_call x1, Pallas kernels: 132 us -> 110 us  [scatter_sum(): pl.pallas_call(scatter_kernel, out_shape=[jax.ShapeDtypeStruct((rows, wid...]
    pallas_call x1, Pallas kernels: 140 us -> 126 us  [run_middle(): pl.pallas_call(middle_kernel, out_shape=(jax.ShapeDtypeStruct((rows, widt...]
where the time goes in v4:
time: 443 us; the launch traced here: 441 us
  Pallas kernels  406 us (92%)
  local copies, waits for them, and re-layouts  24.4 us (6%)
  other arithmetic  9.38 us (2%)
    pallas_call x1, Pallas kernels, run_middle(): pl.pallas_call(middle_kernel, out_shape=(jax.ShapeDtypeStruct((rows, widt...  126 us
    pallas_call x1, Pallas kernels, gather_weights(): pl.pallas_call(gather_kernel, out_shape=[jax.ShapeDtypeStruct((4, 2, 2, 2...  110 us
    pallas_call x1, Pallas kernels, scatter_sum(): pl.pallas_call(scatter_kernel, out_shape=[jax.ShapeDtypeStruct((rows, wid...  110 us
    pallas_call x2, Pallas kernels, attend_call(): pl.pallas_call(kernel, out_shape=out_shape, grid_spec=pltpu.PrefetchScala...  60.7 us
    unnamed x29, local copies, waits for them, and re-layouts  12.5 us

profile of v4, /device:TPU:1, one launch (start us, length us, event | category | flops | bytes accessed | tf_op | source)
XLA Modules:
  0.0 441.1 jit_solution(12112672623853732045)
XLA Ops:
  0.7 0.8 convert_reduce_fusion
  1.5 0.7 copy.57
  2.3 0.8 copy.58
  3.1 0.8 select_reduce_fusion
  3.9 0.1 reshape.121
  3.9 0.1 constant_dynamic-slice_fusion
  4.0 0.1 broadcast_in_dim_reshape.3.start_ref
  4.1 0.1 reshape_reshape.7
  4.2 0.1 slice_reduce_fusion.5
  4.3 0.1 reshape_reshape.6
  4.4 0.1 slice_reduce_fusion.4
  4.5 0.8 stack_reshape.8
  5.3 0.8 stack_reshape.9
  6.1 0.1 pad_maximum_fusion
  6.3 0.1 reshape.122
  6.4 0.9 concatenate.3
  7.3 0.7 pad.12.shard
  8.0 1.4 copy.60.routes
  9.6 109.7 %gather_weights.1 = (bf16[4,2,2,2,48,4608]{5,4,3,2,1,0:T(8,128)(2,1)}, bf16[1536,1024]{1,0:T(8,128)(2,1)}, bf16[1536,1024]{1,0:T(8,128)(2,1)}, bf16[1024,1536]{1...) custom-call(bf16[16,4608]{1,0:T(8,128)(2,1)} %pad.12.shard, ...), custom_call_target="tpu_custom_call" | custom-call | flops 1509949440 | bytes 41943040 | tf_op jit(solution)/shard_map/gather_weights/pallas_call | solution.py:439
  119.4 1.4 slice.44.scale
  120.8 1.4 copy.59
  122.2 1.1 copy-done
  123.3 1.1 copy-done.4
  124.4 28.4 %attend.1 = (bf16[1536,192]{1,0:T(8,128)(2,1)S(1)}, f32[3,64,1536]{2,1,0:T(8,128)S(1)}, f32[3,1536]{1,0:T(4,128)S(1)}) custom-call(s32[12]{0:T(128)S(1)} %and_select_fusion.9.low, s32[12]{0:T(128)S(1)} %fusion.10.high, s32[1,1536]{1,0:T(1,128)S(1)} %fusion.4.pos_ref, s32[1,1536]{1,0:T(1,128)S(1)} %broadcast_in_dim_reshape.3.start_ref, ...), custom_call_target="tpu_custom_call" | custom-call | flops 1207959552 | bytes 8388608 | tf_op jit(solution)/shard_map/attend/pallas_call | solution.py:1584
  152.8 0.9 copy-done.7
  153.7 1.0 copy-done.8
  154.7 126.5 %run_middle.1 = (bf16[192,1536]{1,0:T(8,128)(2,1)}, bf16[192,1536]{1,0:T(8,128)(2,1)}, f32[192,1536]{1,0:T(8,128)}, bf16[192,1536]{1,0:T(8,128)(2,1)}, bf16[1536...) custom-call(bf16[16,96,192]{2,1,0:T(8,128)(2,1)} %bitcast.53, ...), custom_call_target="tpu_custom_call" | custom-call | flops 16307453952 | bytes 41943040 | tf_op jit(solution)/shard_map/run_middle/pallas_call | solution.py:1416
  281.2 1.1 copy-done.5
  282.3 1.1 copy-done.6
  283.5 1.3 copy-done.9
  284.7 32.3 %attend_back.1 = (bf16[1536,192]{1,0:T(8,128)(2,1)S(1)}, bf16[3072,128]{1,0:T(8,128)(2,1)S(1)}) custom-call(s32[6]{0:T(128)S(1)} %and_select_fusion.5.low, s32[6]{0:T(128)S(1)} %fusion.9.high, s32[1,1536]{1,0:T(1,128)S(1)} %fusion.4.pos_ref, s32[1,1536]{1,0:T(1,128)S(1)} %broadcast_in_dim_reshape.3.start_ref, bf16[1536,192]{1,0:T(8,128)(2,1)S(1)} %bitcast.51, ...), custom_call_target="tpu_custom_call" | custom-call | flops 3019898880 | bytes 8388608 | tf_op jit(solution)/shard_map/attend_back/pallas_call | solution.py:1584
  317.1 0.9 copy-done.2
  317.9 0.9 copy-done.3
  318.8 109.6 %scatter_sum.1 = (bf16[192,1536]{1,0:T(8,128)(2,1)}, bf16[16,1536]{1,0:T(8,128)(2,1)}, bf16[16,3072]{1,0:T(8,128)(2,1)}, bf16[192,1024]{1,0:T(8,128)(2,1)}, bf16...) custom-call(bf16[16,96,192]{2,1,0:T(8,128)(2,1)} %bitcast.48, bf16[16,192,128]{2,1,0:T(8,128)(2,1)} %bitcast.49, ...), custom_call_target="tpu_custom_call" | custom-call | flops 3925868544 | bytes 29360128 | tf_op jit(solution)/shard_map/scatter_sum/pallas_call | solution.py:901
  428.4 1.6 slice_convert_fusion.1
  430.0 0.9 slice_convert_fusion
  430.9 0.7 slice_reduce_fusion.2
  431.6 0.6 slice.69
  432.2 0.6 slice.65
  432.8 0.1 reshape.130
  433.0 0.3 slice_reduce_fusion
  433.2 0.7 reshape_squeeze.7
  433.9 0.7 reshape_squeeze.6
  434.6 2.0 bitcast_convert_fusion.2
  436.6 2.0 bitcast_convert_fusion.1
  438.5 1.0 bitcast_convert_fusion
  439.5 0.8 copy.63
  440.3 0.8 copy.64
  (27 shorter events, 0.3 us)
Async XLA Ops:
  122.2 1.1 copy-start
  123.3 1.1 copy-start.4
  152.8 0.9 copy-start.7
  153.7 1.0 copy-start.8
  154.7 126.5 %copy-start.1 = (bf16[16,192,128]{2,1,0:T(8,128)(2,1)S(1)}, bf16[16,192,128]{2,1,0:T(8,128)(2,1)}, u32[]{:S(2)}) copy-start(bf16[16,192,128]{2,1,0:T(8,128)(2,1)} %get-tuple-element.43) | copy-start | bytes 2359300
  281.2 1.1 copy-start.5
  282.3 1.1 copy-start.6
  283.5 1.3 copy-start.9
  317.0 0.9 copy-start.2
  317.9 0.9 copy-start.3
  428.4 10.1 %copy-start.12 = (bf16[128,1536]{1,0:T(8,128)(2,1)S(1)}, bf16[128,1536]{1,0:T(8,128)(2,1)}, u32[]{:S(2)}) copy-start(bf16[128,1536]{1,0:T(8,128)(2,1)} %get-tuple-element.71) | copy-start | bytes 1179652
  428.4 11.1 %copy-start.10 = (bf16[192,1536]{1,0:T(8,128)(2,1)S(1)}, bf16[192,1536]{1,0:T(8,128)(2,1)}, u32[]{:S(2)}) copy-start(bf16[192,1536]{1,0:T(8,128)(2,1)} %get-tuple-element.92) | copy-start | bytes 1769476
  428.4 11.9 %copy-start.11 = (bf16[192,1536]{1,0:T(8,128)(2,1)S(1)}, bf16[192,1536]{1,0:T(8,128)(2,1)}, u32[]{:S(2)}) copy-start(bf16[192,1536]{1,0:T(8,128)(2,1)} %get-tuple-element.93) | copy-start | bytes 1769476

commit v5 on v4

--- a/solution.py
+++ b/solution.py
@@ -68,8 +68,8 @@
 
 def meet(spot, heads, picks=()):
     barrier = pltpu.get_barrier_semaphore()
-    others = [member(spot, step)[0] for step in (1, 2, 3)] + [partner(spot)]
-    others += [moved(spot, axis, step) for axis in "xyz" for step in (1, 2, 3)]
+    others = [partner(spot)] + [moved(spot, "y", step) for step in (1, 2, 3)]
+    others += [moved(spot, "z", step) for step in (1, 3)]
     others = [device_of(other) for other in others]
     others += [(lax.axis_index("dp"), other) for _, other in heads]
     for other in others:
@@ -145,7 +145,7 @@
 def gather_kernel(
     shard, merge, tokens, cotangent, routes_t, own_gate, own_up, own_down,
     out, gate_out, up_out, down_out, head_rows, head_kv, scales, c_main_in, c_rest_in,
-    pieces, joined, qkv_w, rest_w, normed, qkv, packed,
+    pieces, joined, qkv_w, rest_w, normed, qkv, packed, packed_kv,
     send0, recv0, send, recv, send_core, recv_core, local,
     swap_send, swap_recv, swap_local, line_send, line_recv, mate_send, mate_recv, ring_send, ring_recv,
     head_send, head_recv, head_local,
@@ -373,9 +373,15 @@
                 core * half : (core + 1) * half, head * HEADS_WIDE : (head + 1) * HEADS_WIDE
             ]
 
+    for head in range(KEY_VALUE_HEADS):
+        for which in range(2):
+            start = kv_at + (which * KEY_VALUE_HEADS + head) * HEAD_SIZE
+            packed_kv[head, :, which * HEAD_SIZE : (which + 1) * HEAD_SIZE] = qkv[
+                :, start : start + HEAD_SIZE
+            ]
+
     def kv_of(other):
-        start = kv_at + (other // 2) * 2 * HEAD_SIZE
-        return qkv.at[:, pl.ds(pl.multiple_of(start, 128), 2 * HEAD_SIZE)]
+        return packed_kv.at[other // 2]
 
     own_heads = [
         pltpu.make_async_copy(packed.at[ctx], head_rows.at[ctx], head_local.at[0]),
@@ -457,6 +463,7 @@
             pltpu.VMEM((rows, width), low),
             pltpu.VMEM((rows, qkv_width), low),
             pltpu.VMEM((SOURCES, rows // 2, HEADS_WIDE), low),
+            pltpu.VMEM((KEY_VALUE_HEADS, rows, 2 * HEAD_SIZE), low),
             dma((3,)), dma((3,)), dma((18,)), dma((18,)), dma((12,)), dma((12,)), dma,
             dma((3,)), dma((3,)), dma((3,)), dma((12,)), dma((12,)), dma((12,)), dma((12,)),
             dma((12,)), dma((12,)),
@@ -715,7 +722,7 @@
     rows_in[ctx] = head_rows[ctx]
     kv_in[ctx] = head_kv[ctx]
 
-    tile = 256
+    tile = 512
     grads_shape = (4, 2, 2, 2, 48, tile)
 
     def fill(turned, right, grads):
@@ -772,10 +779,14 @@
             grad_qkv[
                 core * half : (core + 1) * half, head * HEADS_WIDE : (head + 1) * HEADS_WIDE
             ] = rows_in[2 * head + core]
-        start = QUERY_HEAD_COUNT * HEAD_SIZE + head * 2 * HEAD_SIZE
-        grad_qkv[:, start : start + 2 * HEAD_SIZE] = (
+        kv_grad = (
             kv_in[2 * head].astype(jnp.float32) + kv_in[2 * head + 1].astype(jnp.float32)
         ).astype(jnp.bfloat16)
+        for which in range(2):
+            start = QUERY_HEAD_COUNT * HEAD_SIZE + (which * KEY_VALUE_HEADS + head) * HEAD_SIZE
+            grad_qkv[:, start : start + HEAD_SIZE] = kv_grad[
+                :, which * HEAD_SIZE : (which + 1) * HEAD_SIZE
+            ]
     load.wait()
     grad_normed[...] = jnp.zeros_like(grad_normed)
 
@@ -939,7 +950,7 @@
 REST_ROWS = 16
 REST_WIDTH = 384
 CAPACITY = 36
-TILE = 256
+TILE = 512
 
 
 def across(left, right):
@@ -1622,16 +1633,8 @@
     half = device_rows // 2
     core = lax.axis_index("ctx") % 2
     ctx_count = lax.axis_size("ctx")
-    slice_rows = w_query.shape[0]
-    kv_shards = jnp.stack(
-        [
-            key_weight.reshape(slice_rows, KEY_VALUE_HEADS, HEAD_SIZE),
-            value_weight.reshape(slice_rows, KEY_VALUE_HEADS, HEAD_SIZE),
-        ],
-        axis=2,
-    ).reshape(slice_rows, 2 * KEY_VALUE_HEADS * HEAD_SIZE)
     shard = jnp.concatenate(
-        [w_query, kv_shards, w_out, w_router, gain_attn[:, None], gain_ffn[:, None]], axis=1
+        [w_query, key_weight, value_weight, w_out, w_router, gain_attn[:, None], gain_ffn[:, None]], axis=1
     )
     shard = jnp.pad(shard, ((0, 0), (0, PACK - shard.shape[1])))
     packed, expert_weights, head_queries, head_kv, scales, *cotangent_rows = gather_weights(
@@ -1703,14 +1706,13 @@
         grad_router_full, grad_gain_two, packed, expert_grads,
     )
     share, out_share = share.astype(wide), out_share.astype(wide)
-    kv_share = share[:, 1536:2560].reshape(slice_rows, KEY_VALUE_HEADS, 2, HEAD_SIZE)
     return (
         mixed,
         grad_input,
         share[:, 2576],
         share[:, :1536],
-        kv_share[:, :, 0].reshape(slice_rows, -1),
-        kv_share[:, :, 1].reshape(slice_rows, -1),
+        share[:, 1536:2048],
+        share[:, 2048:2560],
         out_share,
         share[:, 2560:2576],
         share[:, 2577],

time: 443 us -> 438 us (0.989)
    pallas_call x2, Pallas kernels: 60.7 us -> 52.5 us  [attend_call(): pl.pallas_call(kernel, out_shape=out_shape, grid_spec=pltpu.PrefetchScala...]
    pallas_call x1, Pallas kernels: 110 us -> 117 us  [scatter_sum(): pl.pallas_call(scatter_kernel, out_shape=[jax.ShapeDtypeStruct((rows, wid...]
where the time goes in v5:
time: 438 us; the launch traced here: 436 us
  Pallas kernels  404 us (92%)
  local copies, waits for them, and re-layouts  21.6 us (5%)
  other arithmetic  9.25 us (2%)
    pallas_call x1, Pallas kernels, run_middle(): pl.pallas_call(middle_kernel, out_shape=(jax.ShapeDtypeStruct((rows, widt...  124 us
    pallas_call x1, Pallas kernels, scatter_sum(): pl.pallas_call(scatter_kernel, out_shape=[jax.ShapeDtypeStruct((rows, wid...  117 us
    pallas_call x1, Pallas kernels, gather_weights(): pl.pallas_call(gather_kernel, out_shape=[jax.ShapeDtypeStruct((4, 2, 2, 2...  110 us
    pallas_call x2, Pallas kernels, attend_call(): pl.pallas_call(kernel, out_shape=out_shape, grid_spec=pltpu.PrefetchScala...  52.5 us
    unnamed x29, local copies, waits for them, and re-layouts  12.5 us

profile of v5, /device:TPU:1, one launch (start us, length us, event | category | flops | bytes accessed | tf_op | source)
XLA Modules:
  0.0 435.6 jit_solution(21292634187871012)
XLA Ops:
  0.7 0.8 convert_reduce_fusion
  1.5 0.7 copy.49
  2.3 0.8 copy.50
  3.1 0.8 select_reduce_fusion
  3.9 0.1 reshape.115
  3.9 0.1 constant_dynamic-slice_fusion
  4.0 0.1 broadcast_in_dim_reshape.3.start_ref
  4.1 0.1 reshape_reshape.7
  4.2 0.1 slice_reduce_fusion.3
  4.3 0.1 reshape_reshape.6
  4.4 0.1 slice_reduce_fusion.2
  4.5 1.4 copy.52.routes
  6.0 0.9 concatenate.3
  6.9 0.7 pad.10.shard
  7.7 0.1 multiply_add_fusion
  7.8 110.2 %gather_weights.1 = (bf16[4,2,2,2,48,4608]{5,4,3,2,1,0:T(8,128)(2,1)}, bf16[1536,1024]{1,0:T(8,128)(2,1)}, bf16[1536,1024]{1,0:T(8,128)(2,1)}, bf16[1024,1536]{1...) custom-call(bf16[16,4608]{1,0:T(8,128)(2,1)} %pad.10.shard, ...), custom_call_target="tpu_custom_call" | custom-call | flops 1509949440 | bytes 41943040 | tf_op jit(solution)/shard_map/gather_weights/pallas_call | solution.py:445
  118.0 1.4 slice.41.scale
  119.4 1.4 copy.51
  120.8 0.0 copy-start
  120.8 1.1 copy-done
  121.9 1.1 copy-done.4
  123.0 23.7 %attend.1 = (bf16[1536,192]{1,0:T(8,128)(2,1)S(1)}, f32[3,64,1536]{2,1,0:T(8,128)S(1)}, f32[3,1536]{1,0:T(4,128)S(1)}) custom-call(s32[12]{0:T(128)S(1)} %and_select_fusion.9.low, s32[12]{0:T(128)S(1)} %fusion.10.high, s32[1,1536]{1,0:T(1,128)S(1)} %fusion.4.pos_ref, s32[1,1536]{1,0:T(1,128)S(1)} %broadcast_in_dim_reshape.3.start_ref, ...), custom_call_target="tpu_custom_call" | custom-call | flops 1207959552 | bytes 8388608 | tf_op jit(solution)/shard_map/attend/pallas_call | solution.py:1595
  146.8 0.0 copy-start.7
  146.8 0.9 copy-done.7
  147.6 1.0 copy-done.8
  148.7 124.0 %run_middle.1 = (bf16[192,1536]{1,0:T(8,128)(2,1)}, bf16[192,1536]{1,0:T(8,128)(2,1)}, f32[192,1536]{1,0:T(8,128)}, bf16[192,1536]{1,0:T(8,128)(2,1)}, bf16[1536...) custom-call(bf16[16,96,192]{2,1,0:T(8,128)(2,1)} %bitcast.53, ...), custom_call_target="tpu_custom_call" | custom-call | flops 16307453952 | bytes 41943040 | tf_op jit(solution)/shard_map/run_middle/pallas_call | solution.py:1427
  272.7 0.0 copy-done.1
  272.7 0.0 copy-start.5
  272.7 1.1 copy-done.5
  273.8 1.1 copy-done.6
  275.0 1.3 copy-done.9
  276.2 28.8 %attend_back.1 = (bf16[1536,192]{1,0:T(8,128)(2,1)S(1)}, bf16[3072,128]{1,0:T(8,128)(2,1)S(1)}) custom-call(s32[6]{0:T(128)S(1)} %and_select_fusion.5.low, s32[6]{0:T(128)S(1)} %fusion.9.high, s32[1,1536]{1,0:T(1,128)S(1)} %fusion.4.pos_ref, s32[1,1536]{1,0:T(1,128)S(1)} %broadcast_in_dim_reshape.3.start_ref, bf16[1536,192]{1,0:T(8,128)(2,1)S(1)} %bitcast.51, ...), custom_call_target="tpu_custom_call" | custom-call | flops 3019898880 | bytes 8388608 | tf_op jit(solution)/shard_map/attend_back/pallas_call | solution.py:1595
  305.0 0.0 copy-start.2
  305.0 0.9 copy-done.2
  305.9 0.9 copy-done.3
  306.8 117.2 %scatter_sum.1 = (bf16[192,1536]{1,0:T(8,128)(2,1)}, bf16[16,1536]{1,0:T(8,128)(2,1)}, bf16[16,3072]{1,0:T(8,128)(2,1)}, bf16[192,1024]{1,0:T(8,128)(2,1)}, bf16...) custom-call(bf16[16,96,192]{2,1,0:T(8,128)(2,1)} %bitcast.48, bf16[16,192,128]{2,1,0:T(8,128)(2,1)} %bitcast.49, ...), custom_call_target="tpu_custom_call" | custom-call | flops 3925868544 | bytes 29360128 | tf_op jit(solution)/shard_map/scatter_sum/pallas_call | solution.py:912
  424.0 0.0 copy-start.12
  424.0 1.6 slice_convert_fusion.1
  425.6 0.9 slice_convert_fusion
  426.5 0.7 slice_reduce_fusion
  427.2 0.6 slice.64
  427.8 0.6 fusion.11
  428.4 0.6 slice.61
  429.0 2.0 bitcast_convert_fusion.2
  431.0 2.0 bitcast_convert_fusion.1
  433.0 1.0 bitcast_convert_fusion
  433.9 0.8 copy.55
  434.7 0.8 copy.56
  (19 shorter events, 0.2 us)
Async XLA Ops:
  120.8 1.1 copy-start
  121.9 1.1 copy-start.4
  146.8 0.9 copy-start.7
  147.6 1.0 copy-start.8
  148.7 124.0 %copy-start.1 = (bf16[16,192,128]{2,1,0:T(8,128)(2,1)S(1)}, bf16[16,192,128]{2,1,0:T(8,128)(2,1)}, u32[]{:S(2)}) copy-start(bf16[16,192,128]{2,1,0:T(8,128)(2,1)} %get-tuple-element.43) | copy-start | bytes 2359300
  272.7 1.1 copy-start.5
  273.8 1.1 copy-start.6
  275.0 1.3 copy-start.9
  305.0 0.9 copy-start.2
  305.9 0.9 copy-start.3
  424.0 9.0 %copy-start.12 = (bf16[128,1536]{1,0:T(8,128)(2,1)S(1)}, bf16[128,1536]{1,0:T(8,128)(2,1)}, u32[]{:S(2)}) copy-start(bf16[128,1536]{1,0:T(8,128)(2,1)} %get-tuple-element.71) | copy-start | bytes 1179652
  424.0 9.9 %copy-start.10 = (bf16[192,1536]{1,0:T(8,128)(2,1)S(1)}, bf16[192,1536]{1,0:T(8,128)(2,1)}, u32[]{:S(2)}) copy-start(bf16[192,1536]{1,0:T(8,128)(2,1)} %get-tuple-element.92) | copy-start | bytes 1769476
  424.0 10.8 %copy-start.11 = (bf16[192,1536]{1,0:T(8,128)(2,1)S(1)}, bf16[192,1536]{1,0:T(8,128)(2,1)}, u32[]{:S(2)}) copy-start(bf16[192,1536]{1,0:T(8,128)(2,1)} %get-tuple-element.93) | copy-start | bytes 1769476
